TPU v7x, 32 devices: a whole 2x2x4 slice. The times are simulated.
32 devices in a mesh: grid: 8 (over y, x, core), band: 4 (over z).
Axes of the slice: x: 2, y: 2, z: 4, core: 2. Of those that a mesh axis runs over, the one named last changes fastest.
Arguments:
- coefficients: float32 [2, 4, 131072], P(None, 'band', 'grid'), may hold values from -60 to 60
- index_map: int32 [131072], P('grid'), may hold values from 0 to 884735, as said below
- potential: float32 [192, 36864], P('grid'), may hold values from 0.5 to 2.5
Outputs:
- subspace: float32 [2, 4, 4], P(None, None, 'band')
- residual: float32 [2, 4, 131072], P(None, 'band', 'grid')
Inputs may be any that keep to these rules, and one draw needn't show every extreme that they name: `index_map`: entries 16384 * g to 16384 * (g + 1) - 1 name distinct cells m = ga * 24 * 192 + (gb % 24) * 192 + gc of grid device g's slab of frequency planes, all with fa * fa + fc * fc < 2304, where fa and fc are ga and gc folded into -96 to 95.
All inputs are finite; a program needn't handle non-finite values.
Results may differ from a plain program's by a relative error of at most 0.000062.
Values sent between devices are 32-bit elements; how exact they have to be, the bound alone decides.
No kernel may reach another device: no remote copies, remote signals or barrier semaphores. Data moves between devices by JAX's collectives and lax.ppermute only.
A program may use at most 128 MiB of HBM per device.

v0:
```python
import math

import jax
import jax.numpy as jnp
from jax import lax
from jax.sharding import PartitionSpec as P

N = 192


def make_tables(row_freq, width):
    column_pos = jnp.arange(width, dtype=jnp.int32)
    product = row_freq[:, None] * column_pos[None, :] % width
    angle = product.astype(jnp.float32) * (2.0 * math.pi / width)
    return (jnp.cos(angle), jnp.sin(angle))


def transform(spectrum, pattern, cos_table, sine_table, direction):
    highest = lax.Precision.HIGHEST
    real_part, imag_part = spectrum
    real_cos = jnp.einsum(pattern, real_part, cos_table, precision=highest)
    real_sin = jnp.einsum(pattern, real_part, sine_table, precision=highest)
    imag_cos = jnp.einsum(pattern, imag_part, cos_table, precision=highest)
    imag_sin = jnp.einsum(pattern, imag_part, sine_table, precision=highest)
    if direction > 0:
        return (real_cos - imag_sin, real_sin + imag_cos)
    return (real_cos + imag_sin, imag_cos - real_sin)


def local(coefficients, index_map, potential):
    width = N
    parts = lax.axis_size("grid")
    planes = potential.shape[0]
    band_count = coefficients.shape[1]
    coef_count = coefficients.shape[2]
    total_coef = coef_count * parts
    norm_factor = 1.0 / float(width) ** 3
    cos_full, sine_full = make_tables(jnp.arange(width, dtype=jnp.int32), width)
    weighted_pot = potential.reshape(planes, width, width) * norm_factor
    cell_total = width * planes * width
    real_part = (
        jnp.zeros((band_count, cell_total), jnp.float32).at[:, index_map].set(coefficients[0])
    )
    imag_part = (
        jnp.zeros((band_count, cell_total), jnp.float32).at[:, index_map].set(coefficients[1])
    )
    spectrum = (
        real_part.reshape(band_count, width, planes, width),
        imag_part.reshape(band_count, width, planes, width),
    )
    spectrum = transform(spectrum, "bpqc,cd->bpqd", cos_full, sine_full, 1)
    spectrum = transform(spectrum, "bapc,ad->bdpc", cos_full, sine_full, 1)
    moved = transform(
        (
            lax.all_to_all(spectrum[0], "grid", split_axis=1, concat_axis=2, tiled=True),
            lax.all_to_all(spectrum[1], "grid", split_axis=1, concat_axis=2, tiled=True),
        ),
        "bxgc,gd->bxdc",
        cos_full,
        sine_full,
        1,
    )
    moved = (moved[0] * weighted_pot[None], moved[1] * weighted_pot[None])
    moved = transform(moved, "bxgc,gd->bxdc", cos_full, sine_full, -1)
    spectrum = (
        lax.all_to_all(moved[0], "grid", split_axis=2, concat_axis=1, tiled=True),
        lax.all_to_all(moved[1], "grid", split_axis=2, concat_axis=1, tiled=True),
    )
    spectrum = transform(spectrum, "bapc,ad->bdpc", cos_full, sine_full, -1)
    spectrum = transform(spectrum, "bpqc,cd->bpqd", cos_full, sine_full, -1)
    applied_re = jnp.take(spectrum[0].reshape(band_count, cell_total), index_map, axis=1)
    applied_im = jnp.take(spectrum[1].reshape(band_count, cell_total), index_map, axis=1)
    all_coefs = lax.all_gather(coefficients, "band", axis=1, tiled=True)
    highest = lax.Precision.HIGHEST
    coef_re = all_coefs[0]
    coef_im = all_coefs[1]
    part_re = (
        jnp.dot(coef_re, applied_re.T, precision=highest)
        + jnp.dot(coef_im, applied_im.T, precision=highest)
    ) / total_coef
    part_im = (
        jnp.dot(coef_re, applied_im.T, precision=highest)
        - jnp.dot(coef_im, applied_re.T, precision=highest)
    ) / total_coef
    sub_re, sub_im = lax.psum((part_re, part_im), "grid")
    resid_re = applied_re - (
        jnp.dot(sub_re.T, coef_re, precision=highest)
        - jnp.dot(sub_im.T, coef_im, precision=highest)
    )
    resid_im = applied_im - (
        jnp.dot(sub_im.T, coef_re, precision=highest)
        + jnp.dot(sub_re.T, coef_im, precision=highest)
    )
    return (jnp.stack([sub_re, sub_im]), jnp.stack([resid_re, resid_im]))


def solution(mesh):
    return jax.shard_map(
        local,
        mesh=mesh,
        in_specs=(P(None, "band", "grid"), P("grid"), P("grid", None)),
        out_specs=(P(None, None, "band"), P(None, "band", "grid")),
        check_vma=False,
    )
```

profile of v0, /device:TPU:0, one launch (start us, length us, event | category | flops | bytes accessed | tf_op | source)
XLA Modules:
  0.0 978.6 jit_solution(2750144714676379978)
XLA Ops:
  3.7 61.3 %scatter_custom_fusion = f32[884736]{0:T(1024)S(1)} fusion(s32[16384]{0:T(1024)} %get-tuple-element.12, f32[16384]{0:T(1024)} %bitcast.233, f32[]{:T(128)} %constant.18.clone.1), kind=kCustom, calls=%fused_computation.36 | custom fusion | bytes 3539456 | tf_op jit(solution)/shard_map/scatter | solution.py:42
  68.2 9.2 fusion.63
  77.4 7.0 fusion.75
  84.4 62.4 %scatter_custom_fusion.1 = f32[884736]{0:T(1024)} fusion(s32[16384]{0:T(1024)} %get-tuple-element.12, f32[16384]{0:T(1024)} %bitcast.232, f32[]{:T(128)} %constant.18.clone.1), kind=kCustom, calls=%fused_computation.34 | custom fusion | bytes 3539456 | tf_op jit(solution)/shard_map/scatter | solution.py:45
  152.1 8.8 convolution_add_fusion.1
  165.8 6.8 fusion.12
  172.6 6.4 subtract_bitcast_fusion.1
  189.4 8.7 fusion.10
  209.6 34.7 %all-to-all-done = f32[1,192,24,192]{3,2,0,1:T(8,128)} async-done(((f32[1,192,24,192]{3,2,0,1:T(8,128)}), f32[1,192,24,192]{3,2,0,1:T(8,128)}, u32[]{:S(2)}, u32[]{:S(2)}) %all-to-all-start) | async-done | bytes 3538976 | tf_op jit(solution)/shard_map/all_to_all | solution.py:55
  258.2 7.3 fusion.55
  265.4 7.2 fusion.78
  272.6 31.2 %all-to-all-done.1 = f32[1,192,24,192]{3,2,0,1:T(8,128)} async-done(((f32[1,192,24,192]{3,2,0,1:T(8,128)}), f32[1,192,24,192]{3,2,0,1:T(8,128)}, u32[]{:S(2)}, u32[]{:S(2)}) %all-to-all-start.1) | async-done | bytes 3538976 | tf_op jit(solution)/shard_map/all_to_all | solution.py:56
  307.5 9.0 fusion
  343.7 17.3 %all_gather.3 = f32[2,4,16384]{2,0,1:T(2,128)S(1)} all-gather(f32[2,1,16384]{2,0,1:T(2,128)S(1)} %copy.91), channel_id=1, replica_groups=mesh['grid'=8,'band'=4] {'band'}, dimensions={1}, use_global_device_ids=true | all-gather | bytes 655360 | tf_op jit(solution)/shard_map/all_gather | solution.py:73
  361.0 7.7 fusion.68
  379.3 19.1 %all-to-all-done.2 = f32[1,24,192,192]{3,1,0,2:T(8,128)} async-done(((f32[1,24,192,192]{3,1,0,2:T(8,128)}), f32[1,24,192,192]{3,1,0,2:T(8,128)}, u32[]{:S(2)}, u32[]{:S(2)}) %all-to-all-start.2) | async-done | bytes 3538976 | tf_op jit(solution)/shard_map/all_to_all | solution.py:66
  409.7 48.0 %all-to-all-done.3 = f32[1,24,192,192]{3,1,0,2:T(8,128)} async-done(((f32[1,24,192,192]{3,1,0,2:T(8,128)}), f32[1,24,192,192]{3,1,0,2:T(8,128)}, u32[]{:S(2)}, u32[]{:S(2)}) %all-to-all-start.3) | async-done | bytes 3538976 | tf_op jit(solution)/shard_map/all_to_all | solution.py:67
  477.6 7.6 fusion.2
  485.2 7.4 fusion.4
  498.6 8.7 fusion.22
  507.4 8.8 fusion.25
  526.5 261.0 %gather_fusion.1 = f32[16384]{0:T(1024)} fusion(f32[884736]{0:T(1024)} %reshape.248, s32[16384]{0:T(1024)} %get-tuple-element.11), kind=kCustom, calls=%fused_computation.1.clone | custom fusion | bytes 196608 | tf_op jit(solution)/shard_map/jit(_take)/gather | solution.py:72
  787.4 160.6 %gather_fusion = f32[16384]{0:T(1024)} fusion(f32[884736]{0:T(1024)S(1)} %reshape.245, s32[16384]{0:T(1024)} %get-tuple-element.11), kind=kCustom, calls=%fused_computation.clone | custom fusion | bytes 196608 | tf_op jit(solution)/shard_map/jit(_take)/gather | solution.py:71
  958.5 11.8 %all-reduce = (f32[4,1]{0,1:T(1,128)S(1)}, f32[4,1]{0,1:T(1,128)S(1)}) all-reduce(f32[4,1]{0,1:T(1,128)S(1)} %fusion.37, f32[4,1]{0,1:T(1,128)S(1)} %fusion.34), channel_id=1, replica_groups=mesh['grid'=8,'band'=4] {'grid'}, use_global_device_ids=true, to_apply=%region_3.5 | all-reduce | flops 8 | bytes 64 | tf_op jit(solution)/shard_map/psum | solution.py:85
  (91 shorter events, 159.2 us)
Async XLA Ops:
  68.2 9.2 copy-start.5
  146.8 14.1 %slice-start.8 = ((s8[4718592]{0:T(1024)(128)(4,1)}), s8[524288]{0:T(1024)(128)(4,1)S(1)}, s32[]{:S(2)}) async-start(s8[4718592]{0:T(1024)(128)(4,1)} %bitcast.216), calls=%async_computation.12 | async-start | bytes 1048576
  152.1 8.9 copy-start.2
  152.1 8.9 slice-start.9
  160.9 4.8 copy-start.1
  165.8 6.8 copy-start
  184.1 14.1 %slice-start = ((s8[4718592]{0:T(1024)(128)(4,1)}), s8[524288]{0:T(1024)(128)(4,1)S(1)}, s32[]{:S(2)}) async-start(s8[4718592]{0:T(1024)(128)(4,1)} %bitcast.200), calls=%async_computation.4 | async-start | bytes 1048576
  184.1 60.1 %all-to-all-start = ((f32[1,192,24,192]{3,2,0,1:T(8,128)}), f32[1,192,24,192]{3,2,0,1:T(8,128)}, u32[]{:S(2)}, u32[]{:S(2)}) async-start(f32[1,192,24,192]{3,2,0,1:T(8,128)} %copy.65), calls=%async_computation | async-start | bytes 9437184 | tf_op jit(solution)/shard_map/all_to_all | solution.py:55
  189.4 8.8 slice-start.1
  244.3 59.6 %all-to-all-start.1 = ((f32[1,192,24,192]{3,2,0,1:T(8,128)}), f32[1,192,24,192]{3,2,0,1:T(8,128)}, u32[]{:S(2)}, u32[]{:S(2)}) async-start(f32[1,192,24,192]{3,2,0,1:T(8,128)} %copy.72), calls=%async_computation.1 | async-start | bytes 9437184 | tf_op jit(solution)/shard_map/all_to_all | solution.py:56
  265.4 41.5 %slice-start.6 = ((s8[4718592]{0:T(1024)(128)(4,1)}), s8[524288]{0:T(1024)(128)(4,1)S(1)}, s32[]{:S(2)}) async-start(s8[4718592]{0:T(1024)(128)(4,1)} %bitcast.214), calls=%async_computation.10 | async-start | bytes 1048576
  303.9 3.6 slice-start.7
  303.9 12.6 %slice-start.10 = ((s8[4718592]{0:T(1024)(128)(4,1)}), s8[4194304]{0:T(1024)(128)(4,1)S(1)}, s32[]{:S(2)}) async-start(s8[4718592]{0:T(1024)(128)(4,1)} %bitcast.218), calls=%async_computation.14 | async-start | bytes 8388608
  307.5 9.0 slice-start.11
  316.5 11.7 %copy-start.3 = (f32[24,192,192]{2,1,0:T(8,128)}, f32[24,192,192]{2,1,0:T(8,128)S(1)}, u32[]{:S(2)}) copy-start(f32[24,192,192]{2,1,0:T(8,128)S(1)} %fusion) | copy-start | bytes 10616836
  322.6 5.5 copy-start.4
  338.9 4.7 copy-start.6
  338.9 59.5 %all-to-all-start.2 = ((f32[1,24,192,192]{3,1,0,2:T(8,128)}), f32[1,24,192,192]{3,1,0,2:T(8,128)}, u32[]{:S(2)}, u32[]{:S(2)}) async-start(f32[1,24,192,192]{3,1,0,2:T(8,128)} %copy.79), calls=%async_computation.2 | async-start | bytes 9437184 | tf_op jit(solution)/shard_map/all_to_all | solution.py:66
  343.7 25.0 %slice-start.4 = ((s8[4718592]{0:T(1024)(128)(4,1)}), s8[4194304]{0:T(1024)(128)(4,1)S(1)}, s32[]{:S(2)}) async-start(s8[4718592]{0:T(1024)(128)(4,1)} %bitcast.208), calls=%async_computation.8 | async-start | bytes 8388608
  361.0 7.7 slice-start.5
  398.4 59.3 %all-to-all-start.3 = ((f32[1,24,192,192]{3,1,0,2:T(8,128)}), f32[1,24,192,192]{3,1,0,2:T(8,128)}, u32[]{:S(2)}, u32[]{:S(2)}) async-start(f32[1,24,192,192]{3,1,0,2:T(8,128)} %copy.84), calls=%async_computation.3 | async-start | bytes 9437184 | tf_op jit(solution)/shard_map/all_to_all | solution.py:67
  457.7 8.6 slice-start.2
  460.7 5.6 slice-start.3
where the time goes:
time: 995 us; the launch traced here: 979 us
  local copies, waits for them, and re-layouts  605 us (61%)
  matrix products  183 us (18%)
  waiting for transfers between devices  133 us (13%)
  blocking collectives  29.1 us (3%)
  starting transfers between devices  19.8 us (2%)
    gather x1, local copies, waits for them, and re-layouts, local(): jnp.take(spectrum[1].reshape(band_count, cell_total), index_map, axis=1)  261 us
    gather x1, local copies, waits for them, and re-layouts, local(): jnp.take(spectrum[0].reshape(band_count, cell_total), index_map, axis=1)  161 us
    scatter x2, local copies, waits for them, and re-layouts, local(): jnp.zeros((band_count, cell_total), jnp.float32).at[:, index_map]  124 us
    all_to_all x1, waiting for transfers between devices, local(): lax.all_to_all(moved[1], 'grid', split_axis=2, concat_axis=1, tiled=True)  48 us
    dot_general x6, matrix products, transform(): imag_cos = jnp.einsum(pattern, imag_part, cos_table, precision=highest)  47.3 us
    dot_general x6, matrix products, transform(): real_sin = jnp.einsum(pattern, real_part, sine_table, precision=highest)  43.1 us
    dot_general x6, matrix products, transform(): real_cos = jnp.einsum(pattern, real_part, cos_table, precision=highest)  40.4 us
    dot_general x6, matrix products, transform(): imag_sin = jnp.einsum(pattern, imag_part, sine_table, precision=highest)  36.9 us
  transfers between devices with their start and end apart: 4, of which 4 were waited for; matrix products, arithmetic and copies ran while one was open for 7% of the time, Pallas kernels for 0%

commit v1 on v0

v1 whole, which is shorter than its diff:
```python
import functools
import math

import jax
import jax.numpy as jnp
import numpy as np
from jax import lax
from jax.experimental import pallas as pl
from jax.experimental.pallas import tpu as pltpu
from jax.sharding import PartitionSpec as P

N = 192
CHUNK = 256
LANES = 128
BF = jnp.bfloat16
F32 = jnp.float32
VMEM_BYTES = 56 * 1024 * 1024
NT = (((1,), (1,)), ((), ()))


def split(x):
    high = x.astype(BF)
    low = (x - high.astype(F32)).astype(BF)
    return high, low


def mm(a, b):
    return jnp.dot(a, b, preferred_element_type=F32)


def split_table(table):
    table = table.astype(np.float32)
    high = table.astype(BF)
    low = (table - high.astype(np.float32)).astype(BF)
    return high, low


@functools.cache
def tables():
    pos = np.arange(N)
    angle = 2.0 * math.pi * ((pos[:, None] * pos[None, :]) % N) / N
    cb, sb = np.cos(angle), np.sin(angle)
    b_fwd = np.block([[cb, -sb], [sb, cb]])
    b_inv = np.block([[cb, sb], [-sb, cb]])
    freq = np.arange(LANES)
    freq = np.where(freq < 64, freq, freq - LANES)
    keep = (np.abs(freq) < 48)[:, None]
    angle = 2.0 * math.pi * ((freq[:, None] * pos[None, :]) % N) / N
    cc, sc = np.cos(angle) * keep, np.sin(angle) * keep
    c_fwd = np.block([[cc, sc], [-sc, cc]])
    c_inv = np.block([[cc.T, -sc.T], [sc.T, cc.T]]) / float(N) ** 3
    bf_h, bf_l = split_table(b_fwd)
    bi_h, bi_l = split_table(b_inv)
    cf_h, cf_l = split_table(c_fwd)
    ci_h, ci_l = split_table(c_inv)
    return (
        np.concatenate([bf_h, bf_l, bf_h], axis=1),
        np.concatenate([cf_h, cf_l, cf_h], axis=0),
        np.concatenate([ci_h, ci_l, ci_h], axis=0),
        np.concatenate([bi_h, bi_l, bi_h], axis=1),
    )


def floor_div(x, divisor):
    return jnp.floor((x + 0.5) * (1.0 / divisor))


def sort_kernel(planes, m_ref, c_ref, out_ref, d_ref, acc_ref, val_ref, sum_ref, above_ref, gb_ref):
    rows = m_ref.shape[0]
    m = m_ref[...].astype(F32)
    line = floor_div(m, N)
    gc = m - N * line
    ga = floor_div(line, planes)
    gb = line - planes * ga
    ga = jnp.where(ga < 96, ga, ga - 96)
    gc = jnp.where(gc < 96, gc, gc - 64)
    lane_r = lax.broadcasted_iota(jnp.int32, (CHUNK, 2 * CHUNK), 0)
    lane_c = lax.broadcasted_iota(jnp.int32, (CHUNK, 2 * CHUNK), 1)
    tri = jnp.where((lane_r < lane_c) | (lane_c >= CHUNK), 1.0, 0.0).astype(BF)
    row_r = lax.broadcasted_iota(jnp.int32, (rows, rows), 0)
    row_c = lax.broadcasted_iota(jnp.int32, (rows, rows), 1)
    below = jnp.where(row_c < row_r, 1.0, 0.0).astype(BF)
    step_id = lax.broadcasted_iota(jnp.int32, (8, CHUNK), 1).astype(F32)
    base = jnp.zeros((1, CHUNK), F32)
    place = jnp.zeros((rows, CHUNK), F32)
    plane_of = jnp.zeros((8, CHUNK), F32)
    gb_ref[...] = gb

    def count(g, carry):
        inside = gb_ref[...] == g.astype(F32)
        sum_ref[g] = mm(jnp.where(inside, 1.0, 0.0).astype(BF), tri)
        return carry

    def climb(g, carry):
        above_ref[g] = mm(below, sum_ref[g, :, CHUNK:].astype(BF))
        return carry

    lax.fori_loop(0, planes, count, 0)
    lax.fori_loop(0, planes, climb, 0)
    for g in range(planes):
        above = above_ref[g]
        place = jnp.where(gb == float(g), sum_ref[g, :, :CHUNK] + above + base, place)
        base = base + above[rows - 1 : rows] + sum_ref[g, rows - 1 : rows, CHUNK:]
        if g < planes - 1:
            rank = g + jnp.floor((jnp.maximum(base, 1.0) - 1.0) * (1.0 / CHUNK))
            plane_of = plane_of + jnp.where(rank < step_id, 1.0, 0.0)
    d_ref[...] = place
    re_h, re_l = split(c_ref[0])
    im_h, im_l = split(c_ref[1])
    for q, value in enumerate((re_h, re_l, im_h, im_l, ga, gb, gc)):
        val_ref[q] = value.astype(F32)
    acc_ref[...] = jnp.zeros_like(acc_ref)
    hi_id = lax.broadcasted_iota(jnp.int32, (rows, CHUNK), 0).astype(F32).astype(BF)
    lo_id = lax.broadcasted_iota(jnp.int32, (CHUNK, CHUNK), 0).astype(F32).astype(BF)
    zero = jnp.zeros((rows, CHUNK), BF)

    def body(i, carry):
        part = pl.ds(pl.multiple_of(i * 8, 8), 8)
        d = d_ref[part, :]
        hi = jnp.floor(d * (1.0 / CHUNK))
        lo = d - CHUNK * hi
        values = [val_ref[q, part, :] for q in range(7)]
        left, right = [], []
        for j in range(8):
            at_hi = jnp.broadcast_to(hi[j : j + 1], (rows, CHUNK)).astype(BF) == hi_id
            at_lo = jnp.broadcast_to(lo[j : j + 1], (CHUNK, CHUNK)).astype(BF) == lo_id
            left.append(
                jnp.concatenate(
                    [
                        jnp.where(at_hi, jnp.broadcast_to(v[j : j + 1], (rows, CHUNK)).astype(BF), zero)
                        for v in values
                    ],
                    axis=0,
                )
            )
            right.append(jnp.where(at_lo, jnp.ones_like(lo_id), jnp.zeros_like(lo_id)))
        acc_ref[...] += lax.dot_general(
            jnp.concatenate(left, axis=1), jnp.concatenate(right, axis=1), NT, preferred_element_type=F32
        )
        return carry

    lax.fori_loop(0, rows // 8, body, 0)
    got = [acc_ref[q * rows : (q + 1) * rows] for q in range(7)]
    out_ref[0:rows] = got[0] + got[1]
    out_ref[rows : 2 * rows] = got[2] + got[3]
    out_ref[2 * rows : 3 * rows] = (got[4] * planes + got[5]) * LANES + got[6]
    out_ref[3 * rows : 3 * rows + 8] = plane_of


def sin_cos(x):
    y = x * x
    s = -1.0 / 39916800.0 + y * (1.0 / 6227020800.0)
    s = 1.0 / 362880.0 + y * s
    s = -1.0 / 5040.0 + y * s
    s = 1.0 / 120.0 + y * s
    s = -1.0 / 6.0 + y * s
    s = x + x * y * s
    c = 1.0 / 479001600.0 - y * (1.0 / 87178291200.0)
    c = -1.0 / 3628800.0 + y * c
    c = 1.0 / 40320.0 + y * c
    c = -1.0 / 720.0 + y * c
    c = 1.0 / 24.0 + y * c
    c = -0.5 + y * c
    c = 1.0 + y * c
    return s, c


def decode(cell, planes):
    line = jnp.floor(cell * (1.0 / LANES))
    gc = cell - LANES * line
    ga = floor_div(line, planes)
    gb = line - planes * ga
    freq = jnp.where(ga < 48, ga, ga - 96)
    return freq, gb, gc


def powers(freq, first, w_ref):
    turn = freq * first
    turn = turn - N * jnp.floor(turn * (1.0 / N) + 0.5)
    s, c = sin_cos(turn * (math.pi / N))
    w_ref[0] = 1.0 - 2.0 * s * s
    w_ref[1] = 2.0 * s * c
    s, c = sin_cos(freq * (2.0 * math.pi / N))
    for q in range(4):
        w_ref[2 + 2 * q] = c
        w_ref[3 + 2 * q] = s
        s, c = 2.0 * s * c, c * c - s * s


def rise(wr, wi, j):
    k = lax.broadcasted_iota(jnp.int32, (8, CHUNK), 0)
    shape = (8, CHUNK)
    er = ei = None
    for bit in range(3):
        on = (k & (1 << bit)) != 0
        fr = jnp.where(on, jnp.broadcast_to(wr[bit][j : j + 1], shape), 1.0)
        fi = jnp.where(on, jnp.broadcast_to(wi[bit][j : j + 1], shape), 0.0)
        if er is None:
            er, ei = fr, fi
        else:
            er, ei = er * fr - ei * fi, er * fi + ei * fr
    return er, ei


def one_hot(code_row):
    ident = lax.broadcasted_iota(jnp.int32, (LANES, CHUNK), 0).astype(F32).astype(BF)
    code = jnp.broadcast_to(code_row, (LANES, CHUNK)).astype(BF)
    return jnp.where(code == ident, jnp.ones_like(ident), jnp.zeros_like(ident))


def pair_of(pairs_ref, s, step, steps):
    g = pairs_ref[s, step]
    c = jnp.minimum(step - g, steps - 1)
    return g, c


def spread_kernel(planes, height, unroll, pairs_ref, first_ref, slab_ref, t_ref, w_ref, code_ref, a_ref):
    s = pl.program_id(0)
    rows = a_ref.shape[0]
    steps = rows + planes - 1
    first = first_ref[0].astype(F32)
    freq, gb, gc = decode(slab_ref[0, 2 * rows : 3 * rows], planes)
    code_ref[0] = gb
    code_ref[1] = gc
    powers(freq, first, w_ref)
    re, im = slab_ref[0, 0:rows], slab_ref[0, rows : 2 * rows]
    sr, si = w_ref[0], w_ref[1]
    w_ref[0] = re * sr - im * si
    w_ref[1] = re * si + im * sr
    shape = (8, CHUNK)

    def build(i, carry):
        part = pl.ds(pl.multiple_of(i * 8, 8), 8)
        w = [w_ref[q, part, :] for q in range(10)]
        for j in range(8):
            er, ei = rise(w[2:8:2], w[3:8:2], j)
            zr = jnp.broadcast_to(w[0][j : j + 1], shape)
            zi = jnp.broadcast_to(w[1][j : j + 1], shape)
            er, ei = er * zr - ei * zi, er * zi + ei * zr
            jr = jnp.broadcast_to(w[8][j : j + 1], shape)
            ji = jnp.broadcast_to(w[9][j : j + 1], shape)
            real, imag = [er], [ei]
            for _ in range(height // 8 - 1):
                er, ei = er * jr - ei * ji, er * ji + ei * jr
                real.append(er)
                imag.append(ei)
            high, low = split(jnp.concatenate(real + imag, axis=0))
            a_ref[i * 8 + j] = jnp.concatenate([high, low], axis=0)
        return carry

    lax.fori_loop(0, rows // 8, build, 0)
    t_ref[...] = jnp.zeros_like(t_ref)

    def visit(i, carry):
        for j in range(unroll):
            step = i * unroll + j
            g, c = pair_of(pairs_ref, s, step, rows)
            wanted = jnp.where(step < steps, g, -1).astype(F32)
            code = jnp.where(code_ref[0, pl.ds(c, 1), :] == wanted, code_ref[1, pl.ds(c, 1), :], -1.0)
            got = lax.dot_general(a_ref[c], one_hot(code), NT, preferred_element_type=F32)
            where = pl.ds(pl.multiple_of(g * (2 * height), 8), 2 * height)
            t_ref[0, where, :] += got[: 2 * height] + got[2 * height :]
        return carry

    lax.fori_loop(0, -(-steps // unroll), visit, 0)


def collect_kernel(planes, height, unroll, pairs_ref, first_ref, slab_ref, u_ref, h_ref, w_ref, code_ref, u2_ref, g_ref):
    s = pl.program_id(0)
    rows = g_ref.shape[0]
    steps = rows + planes - 1
    first = first_ref[0].astype(F32)
    freq, gb, gc = decode(slab_ref[0, 2 * rows : 3 * rows], planes)
    code_ref[0] = gb
    code_ref[1] = gc
    powers(freq, first, w_ref)
    for g in range(planes):
        high, low = split(u_ref[0, g * 2 * height : (g + 1) * 2 * height, :])
        u2_ref[g] = jnp.concatenate([high, low], axis=0)
    g_ref[...] = jnp.zeros_like(g_ref)

    def visit(i, carry):
        for j in range(unroll):
            step = i * unroll + j
            g, c = pair_of(pairs_ref, s, step, rows)
            wanted = jnp.where(step < steps, g, -1).astype(F32)
            code = jnp.where(code_ref[0, pl.ds(c, 1), :] == wanted, code_ref[1, pl.ds(c, 1), :], -1.0)
            got = mm(u2_ref[g], one_hot(code))
            g_ref[c] += got[: 2 * height] + got[2 * height :]
        return carry

    lax.fori_loop(0, -(-steps // unroll), visit, 0)
    shape = (8, CHUNK)

    def finish(i, carry):
        part = pl.ds(pl.multiple_of(i * 8, 8), 8)
        w = [w_ref[q, part, :] for q in range(10)]
        real, imag = [], []
        for j in range(8):
            jr = jnp.broadcast_to(w[8][j : j + 1], shape)
            ji = jnp.broadcast_to(w[9][j : j + 1], shape)
            value = g_ref[i * 8 + j]
            tiles = height // 8
            ar = value[height - 8 : height]
            ai = value[2 * height - 8 : 2 * height]
            for t in range(tiles - 2, -1, -1):
                ar, ai = (
                    ar * jr + ai * ji + value[8 * t : 8 * t + 8],
                    ai * jr - ar * ji + value[height + 8 * t : height + 8 * t + 8],
                )
            er, ei = rise(w[2:8:2], w[3:8:2], j)
            real.append(jnp.sum(ar * er + ai * ei, axis=0, keepdims=True))
            imag.append(jnp.sum(ai * er - ar * ei, axis=0, keepdims=True))
        hr = jnp.concatenate(real, axis=0)
        hi = jnp.concatenate(imag, axis=0)
        h_ref[0, part, :] = hr * w[0] + hi * w[1]
        h_ref[0, pl.ds(pl.multiple_of(rows + i * 8, 8), 8), :] = hi * w[0] - hr * w[1]
        return carry

    lax.fori_loop(0, rows // 8, finish, 0)


def potential_kernel(group, height, planes, t_ref, v_ref, bf_ref, cf_ref, ci_ref, bi_ref, u_ref):
    step = pl.program_id(0)
    if height > planes:

        @pl.when(step == 0)
        def _():
            u_ref[...] = jnp.zeros_like(u_ref)

    stride = 2 * height
    real, imag = [], []
    for j in range(group):
        k = step * group + j
        real.append(t_ref[pl.ds(k, N, stride=stride), :])
        imag.append(t_ref[pl.ds(k + height, N, stride=stride), :])
    x = jnp.concatenate([jnp.concatenate(real, axis=1), jnp.concatenate(imag, axis=1)], axis=0)
    high, low = split(x)
    x = mm(bf_ref[...], jnp.concatenate([high, high, low], axis=0))
    x = jnp.concatenate(
        [
            jnp.concatenate([x[:N, j * LANES : (j + 1) * LANES], x[N:, j * LANES : (j + 1) * LANES]], axis=1)
            for j in range(group)
        ],
        axis=0,
    )
    high, low = split(x)
    x = mm(jnp.concatenate([high, high, low], axis=1), cf_ref[...])
    v = jnp.concatenate([v_ref[j] for j in range(group)], axis=0)
    x = x * jnp.concatenate([v, v], axis=1)
    high, low = split(x)
    x = mm(jnp.concatenate([high, high, low], axis=1), ci_ref[...])
    x = jnp.concatenate(
        [
            jnp.concatenate([x[j * N : (j + 1) * N, q * LANES : (q + 1) * LANES] for j in range(group)], axis=1)
            for q in range(2)
        ],
        axis=0,
    )
    high, low = split(x)
    x = mm(bi_ref[...], jnp.concatenate([high, high, low], axis=0))
    for j in range(group):
        k = step * group + j
        u_ref[pl.ds(k, N, stride=stride), :] = x[:N, j * LANES : (j + 1) * LANES]
        u_ref[pl.ds(k + height, N, stride=stride), :] = x[N:, j * LANES : (j + 1) * LANES]


def unsort_kernel(bands, recv_ref, d_ref, *refs):
    coef_refs, (h_ref, part_ref, hl_ref) = refs[:bands], refs[bands:]
    rows = d_ref.shape[0]
    total = recv_ref[0]
    for s in range(1, recv_ref.shape[0]):
        total = total + recv_ref[s]
    high, low = split(total)
    hl_ref[0 : 2 * rows] = high
    hl_ref[2 * rows :] = low
    hi_id = lax.broadcasted_iota(jnp.int32, (rows, CHUNK), 0).astype(F32)
    lo_id = lax.broadcasted_iota(jnp.int32, (CHUNK, CHUNK), 0).astype(F32).astype(BF)

    def body(i, carry):
        part = pl.ds(pl.multiple_of(i * 8, 8), 8)
        d = d_ref[part, :]
        hi = jnp.floor(d * (1.0 / CHUNK))
        lo = d - CHUNK * hi
        real, imag = [], []
        for j in range(8):
            at_lo = jnp.broadcast_to(lo[j : j + 1], (CHUNK, CHUNK)).astype(BF) == lo_id
            got = mm(hl_ref[...], jnp.where(at_lo, jnp.ones_like(lo_id), jnp.zeros_like(lo_id)))
            got = got[: 2 * rows] + got[2 * rows :]
            at_hi = jnp.broadcast_to(hi[j : j + 1], (rows, CHUNK)) == hi_id
            real.append(jnp.sum(jnp.where(at_hi, got[:rows], 0.0), axis=0, keepdims=True))
            imag.append(jnp.sum(jnp.where(at_hi, got[rows:], 0.0), axis=0, keepdims=True))
        h_ref[0, part, :] = jnp.concatenate(real, axis=0)
        h_ref[1, part, :] = jnp.concatenate(imag, axis=0)
        return carry

    lax.fori_loop(0, rows // 8, body, 0)
    hr, hi = h_ref[0], h_ref[1]
    sums = []
    for coef in coef_refs:
        cr, ci = coef[0], coef[1]
        for value in (cr * hr + ci * hi, cr * hi - ci * hr):
            line = jnp.sum(value, axis=0, keepdims=True)
            sums.append(line[:, :LANES] + line[:, LANES:])
    part_ref[...] = jnp.concatenate(sums, axis=0)


def residual_kernel(bands, scale, sum_ref, h_ref, *refs):
    coef_refs, (out_ref, sub_ref) = refs[:bands], refs[bands:]
    sub = jnp.sum(sum_ref[...], axis=1, keepdims=True) * scale
    sub_ref[...] = jnp.broadcast_to(sub, sub_ref.shape)
    hr, hi = h_ref[0], h_ref[1]
    for i, coef in enumerate(coef_refs):
        sr, si = sub[2 * i : 2 * i + 1], sub[2 * i + 1 : 2 * i + 2]
        cr, ci = coef[0], coef[1]
        hr = hr - (sr * cr - si * ci)
        hi = hi - (si * cr + sr * ci)
    out_ref[0] = hr
    out_ref[1] = hi


def params(**extra):
    return pltpu.CompilerParams(vmem_limit_bytes=VMEM_BYTES, **extra)


def whole(shape):
    return pl.BlockSpec(shape, lambda *_: (0,) * len(shape))


def local(coefficients, index_map, potential):
    slabs = lax.axis_size("grid")
    bands = lax.axis_size("band")
    planes = potential.shape[0]
    count = coefficients.shape[2]
    rows = count // CHUNK
    height = -(-planes // 8) * 8
    group = 2 if planes % 2 == 0 else 1
    steps = rows + planes - 1
    unroll = 8
    me = lax.axis_index("grid")
    band = lax.axis_index("band")
    coef = coefficients.reshape(2, rows, CHUNK)
    sorted_pts, dest = pl.pallas_call(
        functools.partial(sort_kernel, planes),
        out_shape=(
            jax.ShapeDtypeStruct((3 * rows + 8, CHUNK), F32),
            jax.ShapeDtypeStruct((rows, CHUNK), F32),
        ),
        scratch_shapes=[
            pltpu.VMEM((7 * rows, CHUNK), F32),
            pltpu.VMEM((7, rows, CHUNK), F32),
            pltpu.VMEM((planes, rows, 2 * CHUNK), F32),
            pltpu.VMEM((planes, rows, CHUNK), F32),
            pltpu.VMEM((rows, CHUNK), F32),
        ],
        compiler_params=params(),
        name="sort_points",
    )(index_map.reshape(rows, CHUNK), coef)
    coefs = [coef]
    for shift in range(1, bands):
        coefs.append(lax.ppermute(coef, "band", [(i, (i + shift) % bands) for i in range(bands)]))
    points = lax.all_gather(sorted_pts, "grid")
    pairs = points[:, 3 * rows, :].astype(jnp.int32)
    first = (me * planes).astype(jnp.int32).reshape(1)
    slab_spec = pl.BlockSpec((1, 3 * rows + 8, CHUNK), lambda s, *_: (s, 0, 0))
    plane_rows = planes * 2 * height
    t_spec = pl.BlockSpec((1, plane_rows, LANES), lambda s, *_: (s, 0, 0))
    spectrum = pl.pallas_call(
        functools.partial(spread_kernel, planes, height, unroll),
        grid_spec=pltpu.PrefetchScalarGridSpec(
            num_scalar_prefetch=2,
            grid=(slabs,),
            in_specs=[slab_spec],
            out_specs=t_spec,
            scratch_shapes=[
                pltpu.VMEM((10, rows, CHUNK), F32),
                pltpu.VMEM((2, rows, CHUNK), F32),
                pltpu.VMEM((rows, 4 * height, CHUNK), BF),
            ],
        ),
        out_shape=jax.ShapeDtypeStruct((slabs, plane_rows, LANES), F32),
        compiler_params=params(),
        name="spread_points",
    )(pairs, first, points)
    b_fwd, c_fwd, c_inv, b_inv = (jnp.asarray(t) for t in tables())
    full = (slabs * plane_rows, LANES)
    weighted = pl.pallas_call(
        functools.partial(potential_kernel, group, height, planes),
        grid=(planes // group,),
        in_specs=[whole(full), pl.BlockSpec((group, N, N), lambda i: (i, 0, 0))]
        + [whole(t.shape) for t in (b_fwd, c_fwd, c_inv, b_inv)],
        out_specs=whole(full),
        out_shape=jax.ShapeDtypeStruct(full, F32),
        compiler_params=params(),
        name="apply_potential",
    )(spectrum.reshape(full), potential.reshape(planes, N, N), b_fwd, c_fwd, c_inv, b_inv)
    partial = pl.pallas_call(
        functools.partial(collect_kernel, planes, height, unroll),
        grid_spec=pltpu.PrefetchScalarGridSpec(
            num_scalar_prefetch=2,
            grid=(slabs,),
            in_specs=[slab_spec, t_spec],
            out_specs=pl.BlockSpec((1, 2 * rows, CHUNK), lambda s, *_: (s, 0, 0)),
            scratch_shapes=[
                pltpu.VMEM((10, rows, CHUNK), F32),
                pltpu.VMEM((2, rows, CHUNK), F32),
                pltpu.VMEM((planes, 4 * height, LANES), BF),
                pltpu.VMEM((rows, 2 * height, CHUNK), F32),
            ],
        ),
        out_shape=jax.ShapeDtypeStruct((slabs, 2 * rows, CHUNK), F32),
        compiler_params=params(),
        name="collect_points",
    )(pairs, first, points, weighted.reshape(slabs, plane_rows, LANES))
    arrived = lax.all_to_all(partial, "grid", split_axis=0, concat_axis=0, tiled=True)
    applied, part = pl.pallas_call(
        functools.partial(unsort_kernel, bands),
        out_shape=(
            jax.ShapeDtypeStruct((2, rows, CHUNK), F32),
            jax.ShapeDtypeStruct((2 * bands, LANES), F32),
        ),
        scratch_shapes=[pltpu.VMEM((4 * rows, CHUNK), BF)],
        compiler_params=params(),
        name="unsort_points",
    )(arrived, dest, *coefs)
    sums = lax.psum(part, "grid")
    resid, sub = pl.pallas_call(
        functools.partial(residual_kernel, bands, 1.0 / (count * slabs)),
        out_shape=(
            jax.ShapeDtypeStruct((2, rows, CHUNK), F32),
            jax.ShapeDtypeStruct((2 * bands, LANES), F32),
        ),
        compiler_params=params(),
        name="residual",
    )(sums, applied, *coefs)
    turned = sub[:, 0].reshape(bands, 2)
    ids = jnp.arange(bands)
    pick = (ids[None, :] == (band - ids[:, None]) % bands).astype(F32)
    ordered = jnp.sum(pick[:, :, None] * turned[None], axis=1)
    return ordered.T.reshape(2, bands, 1), resid.reshape(2, 1, count)


def solution(mesh):
    return jax.shard_map(
        local,
        mesh=mesh,
        in_specs=(P(None, "band", "grid"), P("grid"), P("grid", None)),
        out_specs=(P(None, None, "band"), P(None, "band", "grid")),
        check_vma=False,
    )
```

time: 995 us -> 224 us (0.23); the launches traced: 979 us -> 223 us
  local copies, waits for them, and re-layouts: 605 us -> 12.4 us
  matrix products: 183 us -> 0 us
  Pallas kernels: 0 us -> 139 us
  waiting for transfers between devices: 133 us -> 32.6 us
  blocking collectives: 29.1 us -> 12.7 us
  between operations: 1.36 us -> 14.1 us
  starting transfers between devices: 19.8 us -> 8.99 us
    gather x2 -> x0, local copies, waits for them, and re-layouts: 422 us -> none  [the longest x1 261 us: local(): jnp.take(spectrum[1].reshape(band_count, cell_total), index_map, axis=1)]
    dot_general x32 -> x0, matrix products: 183 us -> none  [the longest x6 47.3 us: transform(): imag_cos = jnp.einsum(pattern, imag_part, cos_table, precision=highest)]
    pallas_call x0 -> x6, Pallas kernels: none -> 139 us  [the longest x1 41.6 us: local(): pl.pallas_call(functools.partial(spread_kernel, planes, height, unroll),...]
    all_to_all x4 -> x1, waiting for transfers between devices: 133 us -> 2.02 us  [local(): lax.all_to_all(partial, 'grid', split_axis=0, concat_axis=0, tiled=True)]
    scatter x2 -> x0, local copies, waits for them, and re-layouts: 124 us -> none  [local(): jnp.zeros((band_count, cell_total), jnp.float32).at[:, index_map]]
    all_gather x0 -> x1, waiting for transfers between devices: none -> 22.8 us  [local(): points = lax.all_gather(sorted_pts, 'grid')]
    another operation x4 -> x0, local copies, waits for them, and re-layouts: 18.7 us -> none
    all_gather x1 -> x0, blocking collectives: 17.3 us -> none  [local(): all_coefs = lax.all_gather(coefficients, 'band', axis=1, tiled=True)]
  transfers between devices with their start and end apart: 4 -> 5, of which waited for: 4 -> 4; matrix products, arithmetic and copies ran while one was open for 7% -> 3% of each run, Pallas kernels for 0% -> 0%
where the time goes in v1:
time: 224 us; the launch traced here: 223 us
  Pallas kernels  139 us (62%)
  waiting for transfers between devices  32.6 us (15%)
  between operations  14.1 us (6%)
  blocking collectives  12.7 us (6%)
  local copies, waits for them, and re-layouts  12.4 us (6%)
  starting transfers between devices  8.99 us (4%)
  other arithmetic  2.87 us (1%)
    pallas_call x1, Pallas kernels, local(): pl.pallas_call(functools.partial(spread_kernel, planes, height, unroll),...  41.6 us
    pallas_call x1, Pallas kernels, local(): pl.pallas_call(functools.partial(collect_kernel, planes, height, unroll),...  39.6 us
    pallas_call x1, Pallas kernels, local(): pl.pallas_call(functools.partial(potential_kernel, group, height, planes)...  35.3 us
    all_gather x1, waiting for transfers between devices, local(): points = lax.all_gather(sorted_pts, 'grid')  22.8 us
    pallas_call x1, Pallas kernels, local(): pl.pallas_call(functools.partial(sort_kernel, planes), out_shape=(jax.Sha...  14.7 us
    psum x1, blocking collectives, local(): sums = lax.psum(part, 'grid')  12.7 us
    ppermute x3, waiting for transfers between devices, local(): lax.ppermute(coef, 'band', [(i, (i + shift) % bands) for i in range(bands)])  7.82 us
    reshape x1, local copies, waits for them, and re-layouts, local(): potential.reshape(planes, N, N)  6.05 us
  transfers between devices with their start and end apart: 5, of which 4 were waited for; matrix products, arithmetic and copies ran while one was open for 3% of the time, Pallas kernels for 0%

profile of v1, /device:TPU:0, one launch (start us, length us, event | category | flops | bytes accessed | tf_op | source)
XLA Modules:
  0.0 222.7 jit_solution(1220616425650968153)
XLA Ops:
  7.2 1.3 reduce
  8.5 0.7 copy.20
  9.2 1.5 reshape.73.m_ref
  10.7 14.7 %sort_points.1 = (f32[200,256]{1,0:T(8,128)}, f32[64,256]{1,0:T(8,128)}) custom-call(s32[64,256]{1,0:T(8,128)} %reshape.73.m_ref, f32[2,64,256]{2,1,0:T(8,128)} %bitcast.21), custom_call_target="tpu_custom_call" | custom-call | tf_op jit(solution)/shard_map/sort_points/pallas_call | solution.py:443
  25.4 6.1 %reshape.77.v_ref = f32[24,192,192]{2,1,0:T(8,128)} reshape(f32[24,36864]{1,0:T(8,128)} %param.9) | data formatting | bytes 7077888 | tf_op jit(solution)/shard_map/reshape | solution.py:496
  31.5 22.8 %all-gather.3.cloned.1.call-done = f32[1600,256]{1,0:T(8,128)} async-done(((f32[200,256]{1,0:T(8,128)}), f32[1600,256]{1,0:T(8,128)}) %all-gather.3.cloned.1.call-update) | async-done | bytes 1638416 | tf_op jit(solution)/shard_map/all_gather | solution.py:462
  54.2 0.8 slice_convert_fusion
  55.7 41.6 %spread_points.1 = f32[8,1152,128]{2,1,0:T(8,128)} custom-call(s32[8,256]{1,0:T(8,128)} %bitcast.28, s32[1]{0:T(128)} %bitcast.1.first_ref, f32[8,200,256]{2,1,0:T(8,128)} %bitcast.19), custom_call_target="tpu_custom_call" | custom-call | tf_op jit(solution)/shard_map/spread_points/pallas_call | solution.py:468
  97.3 35.3 %apply_potential.1 = f32[9216,128]{1,0:T(8,128)} custom-call(f32[9216,128]{1,0:T(8,128)} %bitcast.17, f32[24,192,192]{2,1,0:T(8,128)} %reshape.77.v_ref, bf16[384,1152]{1,0:T(8,128)(2,1)} %constant.36.clone.bf_ref, bf16[768,384]{1,0:T(8,128)(2,1)} %constant.37.clone.cf_ref, bf16[1152,256]{1,0:T(8,128)(2,1)} %constant.38.clone.ci_ref, ...), custom_call_target="tpu_custom_call" | custom-call | tf_op jit(solution)/shard_map/apply_potential/pallas_call | solution.py:487
  132.6 39.6 %collect_points.1 = f32[8,128,256]{2,1,0:T(8,128)} custom-call(s32[8,256]{1,0:T(8,128)} %bitcast.29, s32[1]{0:T(128)} %bitcast.1.first_ref, f32[8,200,256]{2,1,0:T(8,128)} %bitcast.20, f32[8,1152,128]{2,1,0:T(8,128)} %bitcast.16), custom_call_target="tpu_custom_call" | custom-call | tf_op jit(solution)/shard_map/collect_points/pallas_call | solution.py:497
  172.2 3.6 %all-to-all-start = ((f32[8,128,256]{2,1,0:T(8,128)}), f32[8,128,256]{2,1,0:T(8,128)S(1)}, u32[]{:S(2)}, u32[]{:S(2)}) async-start(f32[8,128,256]{2,1,0:T(8,128)} %collect_points.1), calls=%async_computation | async-start | bytes 2097152 | tf_op jit(solution)/shard_map/all_to_all | solution.py:515
  175.8 1.5 collective-permute-start
  177.3 2.4 %collective-permute-start.1 = (f32[2,64,256]{2,1,0:T(8,128)S(1)}, f32[2,64,256]{2,1,0:T(8,128)S(1)}, u32[]{:S(2)}, u32[]{:S(2)}) collective-permute-start(f32[2,64,256]{2,1,0:T(8,128)S(1)} %bitcast.25), channel_id=1, source_target_pairs={{0,2},{1,3},{2,0},{3,1},{4,6},{5,7},{6,4},{7,5},{8,10},{9,11},{10,... | collective-permute-start | bytes 393224 | tf_op jit(solution)/shard_map/ppermute | solution.py:461
  179.7 1.5 collective-permute-start.2
  181.2 2.8 %collective-permute-done.refs_1_ = f32[2,64,256]{2,1,0:T(8,128)S(1)} collective-permute-done((f32[2,64,256]{2,1,0:T(8,128)S(1)}, f32[2,64,256]{2,1,0:T(8,128)S(1)}, u32[]{:S(2)}, u32[]{:S(2)}) %collective-permute-start) | collective-permute-done | bytes 131104 | tf_op jit(solution)/shard_map/ppermute | solution.py:461
  184.0 5.0 %collective-permute-done.1.refs_2_ = f32[2,64,256]{2,1,0:T(8,128)S(1)} collective-permute-done((f32[2,64,256]{2,1,0:T(8,128)S(1)}, f32[2,64,256]{2,1,0:T(8,128)S(1)}, u32[]{:S(2)}, u32[]{:S(2)}) %collective-permute-start.1) | collective-permute-done | bytes 131104 | tf_op jit(solution)/shard_map/ppermute | solution.py:461
  189.1 2.0 all-to-all-done.recv_ref
  191.1 1.0 copy-done
  192.0 5.8 %unsort_points.1 = (f32[2,64,256]{2,1,0:T(8,128)}, f32[8,128]{1,0:T(8,128)}) custom-call(f32[8,128,256]{2,1,0:T(8,128)} %copy-done, f32[64,256]{1,0:T(8,128)} %get-tuple-element.9.d_ref, f32[2,64,256]{2,1,0:T(8,128)} %bitcast.22, f32[2,64,256]{2,1,0:T(8,128)} %copy-done.2, f32[2,64,256]{2,1,0:T(8,128)} %copy-done.3, f32[2,64,256]{2,1,0:T(8,128)} %copy-done.4), custom_call_target="tpu_custom_call" | custom-call | tf_op jit(solution)/shard_map/unsort_points/pallas_call | solution.py:516
  197.9 12.7 %psum.7.sum_ref = f32[8,128]{1,0:T(8,128)} all-reduce(f32[8,128]{1,0:T(8,128)} %get-tuple-element.10), channel_id=1, replica_groups=mesh['grid'=8,'band'=4] {'grid'}, use_global_device_ids=true, to_apply=%region_0.0 | all-reduce | flops 1024 | bytes 8192 | tf_op jit(solution)/shard_map/psum | solution.py:526
  210.6 2.0 residual.1
  212.6 1.7 reshape.82
  214.2 0.8 slice_reduce_fusion
  215.2 0.7 multiply_reduce_fusion
  (17 shorter events, 0.9 us)
Async XLA Ops:
  7.2 47.1 %all-gather.3.cloned.1.call-start = ((), (), s32[]{:S(2)}) async-start(), calls=%async_computation.1 | async-start | bytes 1843200 | tf_op jit(solution)/shard_map/all_gather | solution.py:462
  132.6 43.2 %copy-start.1 = (f32[1,2,64,256]{3,2,1,0:T(8,128)S(1)}, f32[1,2,64,256]{3,2,1,0:T(8,128)}, u32[]{:S(2)}) copy-start(f32[1,2,64,256]{3,2,1,0:T(8,128)} %copy.20) | copy-start | bytes 393220
  172.2 18.9 %all-to-all-start = ((f32[8,128,256]{2,1,0:T(8,128)}), f32[8,128,256]{2,1,0:T(8,128)S(1)}, u32[]{:S(2)}, u32[]{:S(2)}) async-start(f32[8,128,256]{2,1,0:T(8,128)} %collect_points.1), calls=%async_computation | async-start | bytes 2097152 | tf_op jit(solution)/shard_map/all_to_all | solution.py:515
  175.8 8.3 %collective-permute-start = (f32[2,64,256]{2,1,0:T(8,128)S(1)}, f32[2,64,256]{2,1,0:T(8,128)S(1)}, u32[]{:S(2)}, u32[]{:S(2)}) collective-permute-start(f32[2,64,256]{2,1,0:T(8,128)S(1)} %bitcast.24), channel_id=1, source_target_pairs={{0,1},{1,2},{2,3},{3,0},{4,5},{5,6},{6,7},{7,4},{8,9},{9,10},{10,1... | collective-permute-start | bytes 393224 | tf_op jit(solution)/shard_map/ppermute | solution.py:461
  177.3 11.8 %collective-permute-start.1 = (f32[2,64,256]{2,1,0:T(8,128)S(1)}, f32[2,64,256]{2,1,0:T(8,128)S(1)}, u32[]{:S(2)}, u32[]{:S(2)}) collective-permute-start(f32[2,64,256]{2,1,0:T(8,128)S(1)} %bitcast.25), channel_id=1, source_target_pairs={{0,2},{1,3},{2,0},{3,1},{4,6},{5,7},{6,4},{7,5},{8,10},{9,11},{10,... | collective-permute-start | bytes 393224 | tf_op jit(solution)/shard_map/ppermute | solution.py:461
  179.7 9.4 %collective-permute-start.2 = (f32[2,64,256]{2,1,0:T(8,128)S(1)}, f32[2,64,256]{2,1,0:T(8,128)S(1)}, u32[]{:S(2)}, u32[]{:S(2)}) collective-permute-start(f32[2,64,256]{2,1,0:T(8,128)S(1)} %bitcast.26), channel_id=1, source_target_pairs={{0,3},{1,0},{2,1},{3,2},{4,7},{5,4},{6,5},{7,6},{8,11},{9,8},{10,9... | collective-permute-start | bytes 393224 | tf_op jit(solution)/shard_map/ppermute | solution.py:461
  184.0 7.1 %copy-start.2 = (f32[2,64,256]{2,1,0:T(8,128)}, f32[2,64,256]{2,1,0:T(8,128)S(1)}, u32[]{:S(2)}) copy-start(f32[2,64,256]{2,1,0:T(8,128)S(1)} %collective-permute-done.refs_1_) | copy-start | bytes 393220
  189.1 2.0 copy-start.3
  189.1 2.0 copy-start.4
  191.1 1.0 copy-start
Sparse Core Ops, SparseCore 0:
  25.5 28.6 all-gather.2

commit v2 on v1

v2 whole, which is shorter than its diff:
```python
import functools
import math

import jax
import jax.numpy as jnp
import numpy as np
from jax import lax
from jax.experimental import pallas as pl
from jax.experimental.pallas import tpu as pltpu
from jax.sharding import PartitionSpec as P

N = 192
CHUNK = 256
LANES = 128
BF = jnp.bfloat16
F32 = jnp.float32
VMEM_BYTES = 56 * 1024 * 1024
NT = (((1,), (1,)), ((), ()))


def split(x):
    high = x.astype(BF)
    low = (x - high.astype(F32)).astype(BF)
    return high, low


def mm(a, b):
    return jnp.dot(a, b, preferred_element_type=F32)


def split_table(table):
    table = table.astype(np.float32)
    high = table.astype(BF)
    low = (table - high.astype(np.float32)).astype(BF)
    return high, low


@functools.cache
def tables():
    pos = np.arange(N)
    angle = 2.0 * math.pi * ((pos[:, None] * pos[None, :]) % N) / N
    cb, sb = np.cos(angle), np.sin(angle)
    b_fwd = np.block([[cb, -sb], [sb, cb]])
    b_inv = np.block([[cb, sb], [-sb, cb]])
    freq = np.arange(LANES)
    freq = np.where(freq < 64, freq, freq - LANES)
    keep = (np.abs(freq) < 48)[:, None]
    angle = 2.0 * math.pi * ((freq[:, None] * pos[None, :]) % N) / N
    cc, sc = np.cos(angle) * keep, np.sin(angle) * keep
    c_fwd = np.block([[cc, sc], [-sc, cc]])
    c_inv = np.block([[cc.T, -sc.T], [sc.T, cc.T]]) / float(N) ** 3
    bf_h, bf_l = split_table(b_fwd)
    bi_h, bi_l = split_table(b_inv)
    cf_h, cf_l = split_table(c_fwd)
    ci_h, ci_l = split_table(c_inv)
    return (
        np.concatenate([bf_h, bf_l, bf_h], axis=1),
        np.concatenate([cf_h, cf_l, cf_h], axis=0),
        np.concatenate([ci_h, ci_l, ci_h], axis=0),
        np.concatenate([bi_h, bi_l, bi_h], axis=1),
    )


def fold(x):
    half = x.shape[0] // 2
    return jnp.concatenate([x[:half], x[half:]], axis=1)


def unfold(x):
    return jnp.concatenate([x[:, :LANES], x[:, LANES:]], axis=0)


def floor_div(x, divisor):
    return jnp.floor((x + 0.5) * (1.0 / divisor))


def sort_kernel(planes, m_ref, c_ref, out_ref, d_ref, acc_ref, val_ref, sum_ref, above_ref, gb_ref):
    rows = m_ref.shape[0] // 2
    m = fold(m_ref[...]).astype(F32)
    line = floor_div(m, N)
    gc = m - N * line
    ga = floor_div(line, planes)
    gb = line - planes * ga
    ga = jnp.where(ga < 96, ga, ga - 96)
    gc = jnp.where(gc < 96, gc, gc - 64)
    lane_r = lax.broadcasted_iota(jnp.int32, (CHUNK, 2 * CHUNK), 0)
    lane_c = lax.broadcasted_iota(jnp.int32, (CHUNK, 2 * CHUNK), 1)
    tri = jnp.where((lane_r < lane_c) | (lane_c >= CHUNK), 1.0, 0.0).astype(BF)
    row_r = lax.broadcasted_iota(jnp.int32, (rows, rows), 0)
    row_c = lax.broadcasted_iota(jnp.int32, (rows, rows), 1)
    below = jnp.where(row_c < row_r, 1.0, 0.0).astype(BF)
    step_id = lax.broadcasted_iota(jnp.int32, (8, CHUNK), 1).astype(F32)
    base = jnp.zeros((1, CHUNK), F32)
    place = jnp.zeros((rows, CHUNK), F32)
    plane_of = jnp.zeros((8, CHUNK), F32)
    gb_ref[...] = gb

    def count(g, carry):
        inside = gb_ref[...] == g.astype(F32)
        sum_ref[g] = mm(jnp.where(inside, 1.0, 0.0).astype(BF), tri)
        return carry

    def climb(g, carry):
        above_ref[g] = mm(below, sum_ref[g, :, CHUNK:].astype(BF))
        return carry

    lax.fori_loop(0, planes, count, 0)
    lax.fori_loop(0, planes, climb, 0)
    for g in range(planes):
        above = above_ref[g]
        place = jnp.where(gb == float(g), sum_ref[g, :, :CHUNK] + above + base, place)
        base = base + above[rows - 1 : rows] + sum_ref[g, rows - 1 : rows, CHUNK:]
        if g < planes - 1:
            rank = g + jnp.floor((jnp.maximum(base, 1.0) - 1.0) * (1.0 / CHUNK))
            plane_of = plane_of + jnp.where(rank < step_id, 1.0, 0.0)
    d_ref[...] = place
    re_h, re_l = split(fold(c_ref[0]))
    im_h, im_l = split(fold(c_ref[1]))
    for q, value in enumerate((re_h, re_l, im_h, im_l, ga, gb, gc)):
        val_ref[q] = value.astype(F32)
    acc_ref[...] = jnp.zeros_like(acc_ref)
    hi_id = lax.broadcasted_iota(jnp.int32, (rows, CHUNK), 0).astype(F32).astype(BF)
    lo_id = lax.broadcasted_iota(jnp.int32, (CHUNK, CHUNK), 0).astype(F32).astype(BF)
    zero = jnp.zeros((rows, CHUNK), BF)

    def body(i, carry):
        part = pl.ds(pl.multiple_of(i * 8, 8), 8)
        d = d_ref[part, :]
        hi = jnp.floor(d * (1.0 / CHUNK))
        lo = d - CHUNK * hi
        values = [val_ref[q, part, :] for q in range(7)]
        left, right = [], []
        for j in range(8):
            at_hi = jnp.broadcast_to(hi[j : j + 1], (rows, CHUNK)).astype(BF) == hi_id
            at_lo = jnp.broadcast_to(lo[j : j + 1], (CHUNK, CHUNK)).astype(BF) == lo_id
            left.append(
                jnp.concatenate(
                    [
                        jnp.where(at_hi, jnp.broadcast_to(v[j : j + 1], (rows, CHUNK)).astype(BF), zero)
                        for v in values
                    ],
                    axis=0,
                )
            )
            right.append(jnp.where(at_lo, jnp.ones_like(lo_id), jnp.zeros_like(lo_id)))
        acc_ref[...] += lax.dot_general(
            jnp.concatenate(left, axis=1), jnp.concatenate(right, axis=1), NT, preferred_element_type=F32
        )
        return carry

    lax.fori_loop(0, rows // 8, body, 0)
    got = [acc_ref[q * rows : (q + 1) * rows] for q in range(7)]
    out_ref[0:rows] = got[0] + got[1]
    out_ref[rows : 2 * rows] = got[2] + got[3]
    out_ref[2 * rows : 3 * rows] = (got[4] * planes + got[5]) * LANES + got[6]
    out_ref[3 * rows : 3 * rows + 8] = plane_of


def sin_cos(x):
    y = x * x
    s = -1.0 / 39916800.0 + y * (1.0 / 6227020800.0)
    s = 1.0 / 362880.0 + y * s
    s = -1.0 / 5040.0 + y * s
    s = 1.0 / 120.0 + y * s
    s = -1.0 / 6.0 + y * s
    s = x + x * y * s
    c = 1.0 / 479001600.0 - y * (1.0 / 87178291200.0)
    c = -1.0 / 3628800.0 + y * c
    c = 1.0 / 40320.0 + y * c
    c = -1.0 / 720.0 + y * c
    c = 1.0 / 24.0 + y * c
    c = -0.5 + y * c
    c = 1.0 + y * c
    return s, c


def decode(cell, planes):
    line = jnp.floor(cell * (1.0 / LANES))
    gc = cell - LANES * line
    ga = floor_div(line, planes)
    gb = line - planes * ga
    freq = jnp.where(ga < 48, ga, ga - 96)
    return freq, gb, gc


def phase(freq, first):
    turn = freq * first
    turn = turn - N * jnp.floor(turn * (1.0 / N) + 0.5)
    s, c = sin_cos(turn * (math.pi / N))
    return 1.0 - 2.0 * s * s, 2.0 * s * c


def powers(freq, w_ref):
    s, c = sin_cos(freq * (2.0 * math.pi / N))
    for q in range(4):
        w_ref[4 + 2 * q] = c
        w_ref[5 + 2 * q] = s
        s, c = 2.0 * s * c, c * c - s * s


def rise(wr, wi, j):
    k = lax.broadcasted_iota(jnp.int32, (8, CHUNK), 0)
    shape = (8, CHUNK)
    er = ei = None
    for bit in range(3):
        on = (k & (1 << bit)) != 0
        fr = jnp.where(on, jnp.broadcast_to(wr[bit][j : j + 1], shape), 1.0)
        fi = jnp.where(on, jnp.broadcast_to(wi[bit][j : j + 1], shape), 0.0)
        if er is None:
            er, ei = fr, fi
        else:
            er, ei = er * fr - ei * fi, er * fi + ei * fr
    return er, ei


def one_hot(code_row):
    ident = lax.broadcasted_iota(jnp.int32, (LANES, CHUNK), 0).astype(F32).astype(BF)
    code = jnp.broadcast_to(code_row, (LANES, CHUNK)).astype(BF)
    return jnp.where(code == ident, jnp.ones_like(ident), jnp.zeros_like(ident))


def firsts(planes):
    me = lax.axis_index("grid")
    return (me * planes).astype(F32), ((me ^ 1) * planes).astype(F32)


def pair_code(planes, steps_ref, code_ref, rows, step):
    g = steps_ref[0, step].astype(jnp.int32)
    c = jnp.minimum(step - g, rows - 1)
    wanted = jnp.where(step < rows + planes - 1, g, -1).astype(F32)
    code = jnp.where(code_ref[0, pl.ds(c, 1), :] == wanted, code_ref[1, pl.ds(c, 1), :], -1.0)
    return g, c, code


def spread_kernel(planes, height, unroll, slab_ref, steps_ref, own_ref, sib_ref, w_ref, code_ref, a_ref):
    rows = a_ref.shape[0]
    freq, gb, gc = decode(slab_ref[0, 2 * rows : 3 * rows], planes)
    code_ref[0] = gb
    code_ref[1] = gc
    re, im = slab_ref[0, 0:rows], slab_ref[0, rows : 2 * rows]
    for q, first in enumerate(firsts(planes)):
        sr, si = phase(freq, first)
        w_ref[2 * q] = re * sr - im * si
        w_ref[2 * q + 1] = re * si + im * sr
    powers(freq, w_ref)
    shape = (8, CHUNK)

    def build(i, carry):
        part = pl.ds(pl.multiple_of(i * 8, 8), 8)
        w = [w_ref[q, part, :] for q in range(12)]
        for j in range(8):
            er, ei = rise(w[4:10:2], w[5:10:2], j)
            jr = jnp.broadcast_to(w[10][j : j + 1], shape)
            ji = jnp.broadcast_to(w[11][j : j + 1], shape)
            lines = []
            for q in range(2):
                zr = jnp.broadcast_to(w[2 * q][j : j + 1], shape)
                zi = jnp.broadcast_to(w[2 * q + 1][j : j + 1], shape)
                zr, zi = er * zr - ei * zi, er * zi + ei * zr
                real, imag = [zr], [zi]
                for _ in range(height // 8 - 1):
                    zr, zi = zr * jr - zi * ji, zr * ji + zi * jr
                    real.append(zr)
                    imag.append(zi)
                lines += real + imag
            high, low = split(jnp.concatenate(lines, axis=0))
            a_ref[i * 8 + j] = jnp.concatenate([high, low], axis=0)
        return carry

    lax.fori_loop(0, rows // 8, build, 0)
    own_ref[...] = jnp.zeros_like(own_ref)
    sib_ref[...] = jnp.zeros_like(sib_ref)

    def visit(i, carry):
        for j in range(unroll):
            g, c, code = pair_code(planes, steps_ref, code_ref, rows, i * unroll + j)
            got = lax.dot_general(a_ref[c], one_hot(code), NT, preferred_element_type=F32)
            got = got[: 4 * height] + got[4 * height :]
            where = pl.ds(pl.multiple_of(g * (2 * height), 8), 2 * height)
            own_ref[0, where, :] += got[: 2 * height]
            sib_ref[0, where, :] += got[2 * height :]
        return carry

    lax.fori_loop(0, -(-(rows + planes - 1) // unroll), visit, 0)


def collect_kernel(
    planes, height, unroll, slab_ref, steps_ref, own_ref, sib_ref, h_ref, w_ref, code_ref, u2_ref, g_ref
):
    rows = g_ref.shape[0]
    freq, gb, gc = decode(slab_ref[0, 2 * rows : 3 * rows], planes)
    code_ref[0] = gb
    code_ref[1] = gc
    for q, first in enumerate(firsts(planes)):
        w_ref[2 * q], w_ref[2 * q + 1] = phase(freq, first)
    powers(freq, w_ref)
    for g in range(planes):
        where = slice(g * 2 * height, (g + 1) * 2 * height)
        high, low = split(jnp.concatenate([own_ref[0, where, :], sib_ref[0, where, :]], axis=0))
        u2_ref[g] = jnp.concatenate([high, low], axis=0)
    g_ref[...] = jnp.zeros_like(g_ref)

    def visit(i, carry):
        for j in range(unroll):
            g, c, code = pair_code(planes, steps_ref, code_ref, rows, i * unroll + j)
            got = mm(u2_ref[g], one_hot(code))
            g_ref[c] += got[: 4 * height] + got[4 * height :]
        return carry

    lax.fori_loop(0, -(-(rows + planes - 1) // unroll), visit, 0)
    shape = (8, CHUNK)

    def finish(i, carry):
        part = pl.ds(pl.multiple_of(i * 8, 8), 8)
        w = [w_ref[q, part, :] for q in range(12)]
        real, imag = [], []
        for j in range(8):
            jr = jnp.broadcast_to(w[10][j : j + 1], shape)
            ji = jnp.broadcast_to(w[11][j : j + 1], shape)
            hr = hi = 0.0
            for q in range(2):
                value = g_ref[i * 8 + j, q * 2 * height : (q + 1) * 2 * height]
                ar = value[height - 8 : height]
                ai = value[2 * height - 8 : 2 * height]
                for t in range(height // 8 - 2, -1, -1):
                    ar, ai = (
                        ar * jr + ai * ji + value[8 * t : 8 * t + 8],
                        ai * jr - ar * ji + value[height + 8 * t : height + 8 * t + 8],
                    )
                zr = jnp.broadcast_to(w[2 * q][j : j + 1], shape)
                zi = jnp.broadcast_to(w[2 * q + 1][j : j + 1], shape)
                hr, hi = hr + ar * zr + ai * zi, hi + ai * zr - ar * zi
            er, ei = rise(w[4:10:2], w[5:10:2], j)
            real.append(jnp.sum(hr * er + hi * ei, axis=0, keepdims=True))
            imag.append(jnp.sum(hi * er - hr * ei, axis=0, keepdims=True))
        h_ref[0, part, :] = jnp.concatenate(real, axis=0)
        h_ref[0, pl.ds(pl.multiple_of(rows + i * 8, 8), 8), :] = jnp.concatenate(imag, axis=0)
        return carry

    lax.fori_loop(0, rows // 8, finish, 0)


def potential_kernel(group, height, planes, calls, *refs):
    own, sib = refs[:calls], refs[calls : 2 * calls]
    v_ref, bf_ref, cf_ref, ci_ref, bi_ref, keep_ref, send_ref, t_ref, u_ref, sems = refs[2 * calls :]
    step = pl.program_id(0)
    me = lax.axis_index("grid")
    lines = planes * 2 * height

    def place(j, mine):
        slab = me ^ (2 * j) if mine else me ^ (2 * j + 1)
        return pl.ds(pl.multiple_of(slab * lines, 8), lines)

    half = keep_ref.shape[0]
    per_call = half // calls

    def arrivals(j):
        for q, blocks in enumerate((own, sib)):
            yield pltpu.make_async_copy(
                blocks[j // per_call].at[j % per_call], t_ref.at[place(j, q == 0)], sems.at[q, j]
            )

    def departures(j):
        for q, block in enumerate((keep_ref, send_ref)):
            yield pltpu.make_async_copy(u_ref.at[place(j, q == 0)], block.at[j], sems.at[q, j])

    @pl.when(step == 0)
    def _():
        for j in range(half):
            for copy in arrivals(j):
                copy.start()
        for j in range(half):
            for copy in arrivals(j):
                copy.wait()

    if height > planes:

        @pl.when(step == 0)
        def _():
            u_ref[...] = jnp.zeros_like(u_ref)

    stride = 2 * height
    real, imag = [], []
    for j in range(group):
        k = step * group + j
        real.append(t_ref[pl.ds(k, N, stride=stride), :])
        imag.append(t_ref[pl.ds(k + height, N, stride=stride), :])
    x = jnp.concatenate([jnp.concatenate(real, axis=1), jnp.concatenate(imag, axis=1)], axis=0)
    high, low = split(x)
    x = mm(bf_ref[...], jnp.concatenate([high, high, low], axis=0))
    x = jnp.concatenate(
        [
            jnp.concatenate([x[:N, j * LANES : (j + 1) * LANES], x[N:, j * LANES : (j + 1) * LANES]], axis=1)
            for j in range(group)
        ],
        axis=0,
    )
    high, low = split(x)
    x = mm(jnp.concatenate([high, high, low], axis=1), cf_ref[...])
    v = jnp.concatenate([v_ref[j] for j in range(group)], axis=0)
    x = x * jnp.concatenate([v, v], axis=1)
    high, low = split(x)
    x = mm(jnp.concatenate([high, high, low], axis=1), ci_ref[...])
    x = jnp.concatenate(
        [
            jnp.concatenate([x[j * N : (j + 1) * N, q * LANES : (q + 1) * LANES] for j in range(group)], axis=1)
            for q in range(2)
        ],
        axis=0,
    )
    high, low = split(x)
    x = mm(bi_ref[...], jnp.concatenate([high, high, low], axis=0))
    for j in range(group):
        k = step * group + j
        u_ref[pl.ds(k, N, stride=stride), :] = x[:N, j * LANES : (j + 1) * LANES]
        u_ref[pl.ds(k + height, N, stride=stride), :] = x[N:, j * LANES : (j + 1) * LANES]

    @pl.when(step == pl.num_programs(0) - 1)
    def _():
        for j in range(half):
            for copy in departures(j):
                copy.start()
        for j in range(half):
            for copy in departures(j):
                copy.wait()


def unsort_kernel(arrivals, *refs):
    recv_refs = refs[:arrivals]
    d_ref, coef_ref, h_ref, part_ref, hl_ref, wide_ref = refs[arrivals:]
    rows = d_ref.shape[0]
    total = None
    for recv in recv_refs:
        for s in range(recv.shape[0]):
            total = recv[s] if total is None else total + recv[s]
    high, low = split(total)
    hl_ref[0 : 2 * rows] = high
    hl_ref[2 * rows :] = low
    hi_id = lax.broadcasted_iota(jnp.int32, (rows, CHUNK), 0).astype(F32)
    lo_id = lax.broadcasted_iota(jnp.int32, (CHUNK, CHUNK), 0).astype(F32).astype(BF)

    def body(i, carry):
        part = pl.ds(pl.multiple_of(i * 8, 8), 8)
        d = d_ref[part, :]
        hi = jnp.floor(d * (1.0 / CHUNK))
        lo = d - CHUNK * hi
        real, imag = [], []
        for j in range(8):
            at_lo = jnp.broadcast_to(lo[j : j + 1], (CHUNK, CHUNK)).astype(BF) == lo_id
            got = mm(hl_ref[...], jnp.where(at_lo, jnp.ones_like(lo_id), jnp.zeros_like(lo_id)))
            got = got[: 2 * rows] + got[2 * rows :]
            at_hi = jnp.broadcast_to(hi[j : j + 1], (rows, CHUNK)) == hi_id
            real.append(jnp.sum(jnp.where(at_hi, got[:rows], 0.0), axis=0, keepdims=True))
            imag.append(jnp.sum(jnp.where(at_hi, got[rows:], 0.0), axis=0, keepdims=True))
        wide_ref[0, part, :] = jnp.concatenate(real, axis=0)
        wide_ref[1, part, :] = jnp.concatenate(imag, axis=0)
        return carry

    lax.fori_loop(0, rows // 8, body, 0)
    hr, hi = unfold(wide_ref[0]), unfold(wide_ref[1])
    h_ref[0] = hr
    h_ref[1] = hi
    real, imag = [], []
    for i in range(coef_ref.shape[0]):
        cr, ci = coef_ref[i, 0], coef_ref[i, 1]
        real.append(jnp.sum(cr * hr + ci * hi, axis=0, keepdims=True))
        imag.append(jnp.sum(cr * hi - ci * hr, axis=0, keepdims=True))
    sums = jnp.concatenate(real + imag, axis=0)
    for s in range(part_ref.shape[0]):
        part_ref[s] = sums


def residual_kernel(scale, sum_ref, h_ref, coef_ref, out_ref, sub_ref):
    bands = coef_ref.shape[0]
    sub = sum_ref[0]
    for s in range(1, sum_ref.shape[0]):
        sub = sub + sum_ref[s]
    sub = jnp.sum(sub, axis=1, keepdims=True) * scale
    sub_ref[0] = sub[:bands]
    sub_ref[1] = sub[bands:]
    hr, hi = h_ref[0], h_ref[1]
    for i in range(bands):
        sr, si = sub[i : i + 1], sub[bands + i : bands + i + 1]
        cr, ci = coef_ref[i, 0], coef_ref[i, 1]
        hr = hr - (sr * cr - si * ci)
        hi = hi - (si * cr + sr * ci)
    out_ref[0] = hr
    out_ref[1] = hi


def params(**extra):
    return pltpu.CompilerParams(vmem_limit_bytes=VMEM_BYTES, **extra)


def whole(shape):
    return pl.BlockSpec(shape, lambda *_: (0,) * len(shape))


def local(coefficients, index_map, potential):
    slabs = lax.axis_size("grid")
    bands = lax.axis_size("band")
    planes = potential.shape[0]
    count = coefficients.shape[2]
    rows = count // CHUNK
    height = -(-planes // 8) * 8
    group = 2 if planes % 2 == 0 else 1
    unroll = 22
    me = lax.axis_index("grid")
    half = slabs // 2
    coef = coefficients.reshape(2, 2 * rows, LANES)
    coefs = lax.all_gather(coef, "band")
    table_rows = 3 * rows + 8
    sorted_pts, dest = pl.pallas_call(
        functools.partial(sort_kernel, planes),
        out_shape=(
            jax.ShapeDtypeStruct((table_rows, CHUNK), F32),
            jax.ShapeDtypeStruct((rows, CHUNK), F32),
        ),
        scratch_shapes=[
            pltpu.VMEM((7 * rows, CHUNK), F32),
            pltpu.VMEM((7, rows, CHUNK), F32),
            pltpu.VMEM((planes, rows, 2 * CHUNK), F32),
            pltpu.VMEM((planes, rows, CHUNK), F32),
            pltpu.VMEM((rows, CHUNK), F32),
        ],
        compiler_params=params(),
        name="sort_points",
    )(index_map.reshape(2 * rows, LANES), coef)

    def swap(x, bits):
        return lax.ppermute(x, "grid", [(i, i ^ bits) for i in range(slabs)])

    if half <= 4:
        points = [sorted_pts[None]] + [swap(sorted_pts, 2 * j)[None] for j in range(1, half)]
    else:
        everything = lax.all_gather(sorted_pts, "grid")
        points = [jnp.take(everything, me ^ (2 * jnp.arange(half)), axis=0)]
    calls = len(points)
    per_call = half // calls
    lines = planes * 2 * height
    slab_spec = pl.BlockSpec((1, table_rows, CHUNK), lambda s: (s, 0, 0))
    steps_spec = pl.BlockSpec((None, 8, CHUNK), lambda s: (s, table_rows // 8 - 1, 0), memory_space=pltpu.SMEM)
    block_spec = pl.BlockSpec((1, lines, LANES), lambda s: (s, 0, 0))
    point_scratch = [pltpu.VMEM((12, rows, CHUNK), F32), pltpu.VMEM((2, rows, CHUNK), F32)]
    spread = pl.pallas_call(
        functools.partial(spread_kernel, planes, height, unroll),
        grid=(per_call,),
        in_specs=[slab_spec, steps_spec],
        out_specs=(block_spec, block_spec),
        out_shape=(jax.ShapeDtypeStruct((per_call, lines, LANES), F32),) * 2,
        scratch_shapes=point_scratch + [pltpu.VMEM((rows, 8 * height, CHUNK), BF)],
        compiler_params=params(),
        name="spread_points",
    )
    own, sib = [], []
    for table in points:
        mine, theirs = spread(table, table)
        own.append(mine)
        sib.append(swap(theirs, 1))
    constants = [jnp.asarray(t) for t in tables()]
    anywhere = pl.BlockSpec(memory_space=pl.ANY)
    keep, send = pl.pallas_call(
        functools.partial(potential_kernel, group, height, planes, calls),
        grid=(planes // group,),
        in_specs=[anywhere] * (2 * calls)
        + [pl.BlockSpec((group, N, N), lambda i: (i, 0, 0))]
        + [whole(t.shape) for t in constants],
        out_specs=(anywhere, anywhere),
        out_shape=(jax.ShapeDtypeStruct((half, lines, LANES), F32),) * 2,
        scratch_shapes=[
            pltpu.VMEM((slabs * lines, LANES), F32),
            pltpu.VMEM((slabs * lines, LANES), F32),
            pltpu.SemaphoreType.DMA((2, half)),
        ],
        compiler_params=params(),
        name="apply_potential",
    )(*own, *sib, potential.reshape(planes, N, N), *constants)
    other = swap(send, 1)
    partial = []
    for call, table in enumerate(points):
        set_spec = pl.BlockSpec((1, lines, LANES), functools.partial(lambda call, s: (call * per_call + s, 0, 0), call))
        partial.append(
            pl.pallas_call(
                functools.partial(collect_kernel, planes, height, unroll),
                grid=(per_call,),
                in_specs=[slab_spec, steps_spec, set_spec, set_spec],
                out_specs=pl.BlockSpec((1, 2 * rows, CHUNK), lambda s: (s, 0, 0)),
                out_shape=jax.ShapeDtypeStruct((per_call, 2 * rows, CHUNK), F32),
                scratch_shapes=point_scratch
                + [
                    pltpu.VMEM((planes, 8 * height, LANES), BF),
                    pltpu.VMEM((rows, 4 * height, CHUNK), F32),
                ],
                compiler_params=params(),
                name="collect_points",
            )(table, table, keep, other)
        )
    if half <= 4:
        arrived = [partial[0]] + [swap(partial[j], 2 * j) for j in range(1, half)]
    else:
        ids = jnp.arange(slabs)
        blocks = jnp.take(partial[0], (ids ^ me) // 2, axis=0)
        blocks = jnp.where(((ids ^ me) % 2 == 0)[:, None, None], blocks, 0.0)
        arrived = [lax.all_to_all(blocks, "grid", split_axis=0, concat_axis=0, tiled=True)]
    applied, part = pl.pallas_call(
        functools.partial(unsort_kernel, len(arrived)),
        out_shape=(
            jax.ShapeDtypeStruct((2, 2 * rows, LANES), F32),
            jax.ShapeDtypeStruct((slabs, 2 * bands, LANES), F32),
        ),
        scratch_shapes=[pltpu.VMEM((4 * rows, CHUNK), BF), pltpu.VMEM((2, rows, CHUNK), F32)],
        compiler_params=params(),
        name="unsort_points",
    )(*arrived, dest, coefs)
    sums = lax.all_to_all(part, "grid", split_axis=0, concat_axis=0, tiled=True)
    resid, sub = pl.pallas_call(
        functools.partial(residual_kernel, 1.0 / (count * slabs)),
        out_shape=(
            jax.ShapeDtypeStruct((2, 2 * rows, LANES), F32),
            jax.ShapeDtypeStruct((2, bands, 1), F32),
        ),
        compiler_params=params(),
        name="residual",
    )(sums, applied, coefs)
    return sub, resid.reshape(2, 1, count)


def solution(mesh):
    return jax.shard_map(
        local,
        mesh=mesh,
        in_specs=(P(None, "band", "grid"), P("grid"), P("grid", None)),
        out_specs=(P(None, None, "band"), P(None, "band", "grid")),
        check_vma=False,
    )
```

time: 224 us -> 171 us (0.76)
  waiting for transfers between devices: 32.6 us -> 4.76 us
  Pallas kernels: 139 us -> 117 us
  between operations: 14.1 us -> 0.74 us
  blocking collectives: 12.7 us -> 25.6 us
  other arithmetic: 2.87 us -> 0 us
    all_gather x1 -> x0, waiting for transfers between devices: 22.8 us -> none  [local(): points = lax.all_gather(sorted_pts, 'grid')]
    all_gather x0 -> x1, blocking collectives: none -> 16.8 us  [local(): coefs = lax.all_gather(coef, 'band')]
    psum x1 -> x0, blocking collectives: 12.7 us -> none  [local(): sums = lax.psum(part, 'grid')]
    pallas_call x4 -> x7, Pallas kernels: 84.7 us -> 72.9 us  [the longest x1 36.9 us: local(): pl.pallas_call(functools.partial(potential_kernel, group, height, planes,...]
    pallas_call x1 -> x4, Pallas kernels: 39.6 us -> 29.5 us  [local(): pl.pallas_call(functools.partial(collect_kernel, planes, height, unroll),...]
    all_to_all x0 -> x1, blocking collectives: none -> 8.77 us  [local(): sums = lax.all_to_all(part, 'grid', split_axis=0, concat_axis=0, tiled=True)]
    unnamed x12 -> x25, local copies, waits for them, and re-layouts: 2.23 us -> 6.95 us
    ppermute x3 -> x11, starting transfers between devices: 5.39 us -> 9.07 us  [swap(): return lax.ppermute(x, 'grid', [(i, i ^ bits) for i in range(slabs)])]
  transfers between devices with their start and end apart: 5 -> 11, of which waited for: 4 -> 1; matrix products, arithmetic and copies ran while one was open for 3% -> 4% of each run, Pallas kernels for 0% -> 30%
where the time goes in v2:
time: 171 us; the launch traced here: 170 us
  Pallas kernels  117 us (68%)
  blocking collectives  25.6 us (15%)
  local copies, waits for them, and re-layouts  12.9 us (8%)
  starting transfers between devices  9.07 us (5%)
  waiting for transfers between devices  4.76 us (3%)
    pallas_call x1, Pallas kernels, local(): pl.pallas_call(functools.partial(potential_kernel, group, height, planes,...  36.9 us
    pallas_call x4, Pallas kernels, local(): pl.pallas_call(functools.partial(collect_kernel, planes, height, unroll),...  29.5 us
    pallas_call x4, Pallas kernels, local(): mine, theirs = spread(table, table)  28.3 us
    all_gather x1, blocking collectives, local(): coefs = lax.all_gather(coef, 'band')  16.8 us
    pallas_call x1, Pallas kernels, local(): pl.pallas_call(functools.partial(sort_kernel, planes), out_shape=(jax.Sha...  14.7 us
    ppermute x11, starting transfers between devices, swap(): return lax.ppermute(x, 'grid', [(i, i ^ bits) for i in range(slabs)])  9.07 us
    all_to_all x1, blocking collectives, local(): sums = lax.all_to_all(part, 'grid', split_axis=0, concat_axis=0, tiled=True)  8.77 us
    unnamed x25, local copies, waits for them, and re-layouts  6.95 us
  transfers between devices with their start and end apart: 11, of which 1 were waited for; matrix products, arithmetic and copies ran while one was open for 4% of the time, Pallas kernels for 30%

profile of v2, /device:TPU:0, one launch (start us, length us, event | category | flops | bytes accessed | tf_op | source)
XLA Modules:
  0.0 170.2 jit_solution(10584962449504913826)
XLA Ops:
  0.6 14.7 %sort_points.1 = (f32[200,256]{1,0:T(8,128)}, f32[64,256]{1,0:T(8,128)}) custom-call(s32[128,128]{1,0:T(8,128)} %bitcast.26, f32[2,128,128]{2,1,0:T(8,128)} %bitcast.24), custom_call_target="tpu_custom_call" | custom-call | tf_op jit(solution)/shard_map/sort_points/pallas_call | solution.py:513
  15.4 2.9 %collective-permute-start = (f32[200,256]{1,0:T(8,128)}, f32[200,256]{1,0:T(8,128)S(1)}, u32[]{:S(2)}, u32[]{:S(2)}) collective-permute-start(f32[200,256]{1,0:T(8,128)} %get-tuple-element.18), channel_id=1, source_target_pairs={{0,8},{4,12},{8,0},{12,4},{16,24},{20,28},{24,16},{28,20},{1,9},{5... | collective-permute-start | bytes 614408 | tf_op jit(solution)/shard_map/ppermute | solution.py:531
  18.3 1.5 collective-permute-start.1
  19.8 7.1 %spread_points.4 = (f32[1,1152,128]{2,1,0:T(8,128)}, f32[1,1152,128]{2,1,0:T(8,128)}) custom-call(f32[1,200,256]{2,1,0:T(8,128)} %bitcast.8, f32[1,200,256]{2,1,0:T(8,128)} %bitcast.9), custom_call_target="tpu_custom_call" | custom-call | tf_op jit(solution)/shard_map/spread_points/pallas_call | solution.py:557
  27.0 0.7 copy-done.1
  27.6 7.1 %spread_points.5 = (f32[1,1152,128]{2,1,0:T(8,128)}, f32[1,1152,128]{2,1,0:T(8,128)}) custom-call(f32[1,200,256]{2,1,0:T(8,128)} %bitcast.12, f32[1,200,256]{2,1,0:T(8,128)} %bitcast.13), custom_call_target="tpu_custom_call" | custom-call | tf_op jit(solution)/shard_map/spread_points/pallas_call | solution.py:557
  35.9 7.1 %spread_points.6 = (f32[1,1152,128]{2,1,0:T(8,128)}, f32[1,1152,128]{2,1,0:T(8,128)}) custom-call(f32[1,200,256]{2,1,0:T(8,128)} %bitcast.16, f32[1,200,256]{2,1,0:T(8,128)} %bitcast.17), custom_call_target="tpu_custom_call" | custom-call | tf_op jit(solution)/shard_map/spread_points/pallas_call | solution.py:557
  43.0 0.7 copy-done.3
  43.7 7.0 %spread_points.7 = (f32[1,1152,128]{2,1,0:T(8,128)}, f32[1,1152,128]{2,1,0:T(8,128)}) custom-call(f32[1,200,256]{2,1,0:T(8,128)} %bitcast.20, f32[1,200,256]{2,1,0:T(8,128)} %bitcast.21), custom_call_target="tpu_custom_call" | custom-call | tf_op jit(solution)/shard_map/spread_points/pallas_call | solution.py:557
  51.2 6.0 %reshape.18.refs_8_ = f32[24,192,192]{2,1,0:T(8,128)} reshape(f32[24,36864]{1,0:T(8,128)} %param.9) | data formatting | bytes 7077888 | tf_op jit(solution)/shard_map/reshape | solution.py:577
  57.3 0.8 copy-done.4
  58.7 36.9 %apply_potential.1 = (f32[4,1152,128]{2,1,0:T(8,128)}, f32[4,1152,128]{2,1,0:T(8,128)}) custom-call(f32[1,1152,128]{2,1,0:T(8,128)} %get-tuple-element.19.refs_0_, f32[1,1152,128]{2,1,0:T(8,128)} %get-tuple-element.20.refs_1_, f32[1,1152,128]{2,1,0:T(8,128)} %get-tuple-element.21.refs_2_, f32[1,1152,128]{2,1,0:T(8,128)} %get-tuple-element.22.refs_3_, ...), custom_call_target="tpu_custom_call" | custom-call | tf_op jit(solution)/shard_map/apply_potential/pallas_call | solution.py:562
  95.7 4.7 %collective-permute-done.7.sib_ref = f32[4,1152,128]{2,1,0:T(8,128)S(1)} collective-permute-done((f32[4,1152,128]{2,1,0:T(8,128)}, f32[4,1152,128]{2,1,0:T(8,128)S(1)}, u32[]{:S(2)}, u32[]{:S(2)}) %collective-permute-start.7) | collective-permute-done | bytes 2359328 | tf_op jit(solution)/shard_map/ppermute | solution.py:531
  100.4 1.4 copy-done
  101.8 7.3 %collect_points.7 = f32[1,128,256]{2,1,0:T(8,128)} custom-call(f32[1,200,256]{2,1,0:T(8,128)} %bitcast.22, f32[1,200,256]{2,1,0:T(8,128)} %bitcast.23, f32[4,1152,128]{2,1,0:T(8,128)} %get-tuple-element.27.own_ref, f32[4,1152,128]{2,1,0:T(8,128)} %copy-done), custom_call_target="tpu_custom_call" | custom-call | tf_op jit(solution)/shard_map/collect_points/pallas_call | solution.py:583
  109.1 2.9 %collective-permute-start.10 = (f32[1,128,256]{2,1,0:T(8,128)}, f32[1,128,256]{2,1,0:T(8,128)S(1)}, u32[]{:S(2)}, u32[]{:S(2)}) collective-permute-start(f32[1,128,256]{2,1,0:T(8,128)} %collect_points.7), channel_id=1, source_target_pairs={{0,24},{4,28},{8,16},{12,20},{16,8},{20,12},{24,0},{28,4},{1,25},{... | collective-permute-start | bytes 393224 | tf_op jit(solution)/shard_map/ppermute | solution.py:531
  112.0 7.5 %collect_points.6 = f32[1,128,256]{2,1,0:T(8,128)} custom-call(f32[1,200,256]{2,1,0:T(8,128)} %bitcast.18, f32[1,200,256]{2,1,0:T(8,128)} %bitcast.19, f32[4,1152,128]{2,1,0:T(8,128)} %get-tuple-element.27.own_ref, f32[4,1152,128]{2,1,0:T(8,128)} %copy-done), custom_call_target="tpu_custom_call" | custom-call | tf_op jit(solution)/shard_map/collect_points/pallas_call | solution.py:583
  120.0 7.3 %collect_points.5 = f32[1,128,256]{2,1,0:T(8,128)} custom-call(f32[1,200,256]{2,1,0:T(8,128)} %bitcast.14, f32[1,200,256]{2,1,0:T(8,128)} %bitcast.15, f32[4,1152,128]{2,1,0:T(8,128)} %get-tuple-element.27.own_ref, f32[4,1152,128]{2,1,0:T(8,128)} %copy-done), custom_call_target="tpu_custom_call" | custom-call | tf_op jit(solution)/shard_map/collect_points/pallas_call | solution.py:583
  127.5 16.8 %all_gather.3.refs_5_.coef_ref = f32[4,2,128,128]{3,2,1,0:T(8,128)} all-gather(f32[1,2,128,128]{3,2,1,0:T(8,128)S(1)} %bitcast.25), channel_id=1, replica_groups=mesh['grid'=8,'band'=4] {'band'}, dimensions={0}, use_global_device_ids=true | all-gather | bytes 655360 | tf_op jit(solution)/shard_map/all_gather | solution.py:511
  144.3 7.3 %collect_points.4.refs_0_ = f32[1,128,256]{2,1,0:T(8,128)} custom-call(f32[1,200,256]{2,1,0:T(8,128)} %bitcast.10, f32[1,200,256]{2,1,0:T(8,128)} %bitcast.11, f32[4,1152,128]{2,1,0:T(8,128)} %get-tuple-element.27.own_ref, f32[4,1152,128]{2,1,0:T(8,128)} %copy-done), custom_call_target="tpu_custom_call" | custom-call | tf_op jit(solution)/shard_map/collect_points/pallas_call | solution.py:583
  152.4 5.7 %unsort_points.1 = (f32[2,128,128]{2,1,0:T(8,128)}, f32[8,8,128]{2,1,0:T(8,128)}) custom-call(f32[1,128,256]{2,1,0:T(8,128)} %collect_points.4.refs_0_, f32[1,128,256]{2,1,0:T(8,128)} %copy-done.11, f32[1,128,256]{2,1,0:T(8,128)} %copy-done.10, f32[1,128,256]{2,1,0:T(8,128)} %copy-done.9, f32[64,256]{1,0:T(8,128)} %get-tuple-element.29.refs_4_, ...), custom_call_target="tpu_custom_call" | custom-call | tf_op jit(solution)/shard_map/unsort_points/pallas_call | solution.py:605
  158.1 8.8 %all_to_all.5.sum_ref = f32[8,8,128]{2,1,0:T(8,128)} all-to-all(f32[8,8,128]{2,1,0:T(8,128)} %get-tuple-element.30), channel_id=1, replica_groups=mesh['grid'=8,'band'=4] {'grid'}, dimensions={0} | all-to-all | bytes 65536 | tf_op jit(solution)/shard_map/all_to_all | solution.py:615
  166.9 2.0 %residual.1 = (f32[2,128,128]{2,1,0:T(8,128)}, f32[2,4,1]{2,1,0:T(4,128)}) custom-call(f32[8,8,128]{2,1,0:T(8,128)} %all_to_all.5.sum_ref, f32[2,128,128]{2,1,0:T(8,128)} %get-tuple-element.31.h_ref, f32[4,2,128,128]{3,2,1,0:T(8,128)} %all_gather.3.refs_5_.coef_ref), custom_call_target="tpu_custom_call" | custom-call | tf_op jit(solution)/shard_map/residual/pallas_call | solution.py:616
  168.8 1.3 copy.11
  (38 shorter events, 3.8 us)
Async XLA Ops:
  15.4 11.6 %collective-permute-start = (f32[200,256]{1,0:T(8,128)}, f32[200,256]{1,0:T(8,128)S(1)}, u32[]{:S(2)}, u32[]{:S(2)}) collective-permute-start(f32[200,256]{1,0:T(8,128)} %get-tuple-element.18), channel_id=1, source_target_pairs={{0,8},{4,12},{8,0},{12,4},{16,24},{20,28},{24,16},{28,20},{1,9},{5... | collective-permute-start | bytes 614408 | tf_op jit(solution)/shard_map/ppermute | solution.py:531
  18.3 16.9 %collective-permute-start.1 = (f32[200,256]{1,0:T(8,128)}, f32[200,256]{1,0:T(8,128)S(1)}, u32[]{:S(2)}, u32[]{:S(2)}) collective-permute-start(f32[200,256]{1,0:T(8,128)} %get-tuple-element.18), channel_id=1, source_target_pairs={{0,16},{4,20},{8,24},{12,28},{16,0},{20,4},{24,8},{28,12},{1,17},{... | collective-permute-start | bytes 614408 | tf_op jit(solution)/shard_map/ppermute | solution.py:531
  19.8 23.2 %collective-permute-start.2 = (f32[200,256]{1,0:T(8,128)}, f32[200,256]{1,0:T(8,128)S(1)}, u32[]{:S(2)}, u32[]{:S(2)}) collective-permute-start(f32[200,256]{1,0:T(8,128)} %get-tuple-element.18), channel_id=1, source_target_pairs={{0,24},{4,28},{8,16},{12,20},{16,8},{20,12},{24,0},{28,4},{1,25},{... | collective-permute-start | bytes 614408 | tf_op jit(solution)/shard_map/ppermute | solution.py:531
  26.9 30.3 %collective-permute-start.3 = (f32[1,1152,128]{2,1,0:T(8,128)}, f32[1,1152,128]{2,1,0:T(8,128)S(1)}, u32[]{:S(2)}, u32[]{:S(2)}) collective-permute-start(f32[1,1152,128]{2,1,0:T(8,128)} %get-tuple-element.23), channel_id=1, source_target_pairs={{0,4},{4,0},{8,12},{12,8},{16,20},{20,16},{24,28},{28,24},{1,5},{5... | collective-permute-start | bytes 1769480 | tf_op jit(solution)/shard_map/ppermute | solution.py:531
  27.0 0.7 copy-start.1
  34.7 22.5 %collective-permute-start.4 = (f32[1,1152,128]{2,1,0:T(8,128)}, f32[1,1152,128]{2,1,0:T(8,128)S(1)}, u32[]{:S(2)}, u32[]{:S(2)}) collective-permute-start(f32[1,1152,128]{2,1,0:T(8,128)} %get-tuple-element.24), channel_id=1, source_target_pairs={{0,4},{4,0},{8,12},{12,8},{16,20},{20,16},{24,28},{28,24},{1,5},{5... | collective-permute-start | bytes 1769480 | tf_op jit(solution)/shard_map/ppermute | solution.py:531
  35.2 0.7 copy-start.2
  43.0 14.3 %collective-permute-start.5 = (f32[1,1152,128]{2,1,0:T(8,128)}, f32[1,1152,128]{2,1,0:T(8,128)S(1)}, u32[]{:S(2)}, u32[]{:S(2)}) collective-permute-start(f32[1,1152,128]{2,1,0:T(8,128)} %get-tuple-element.25), channel_id=1, source_target_pairs={{0,4},{4,0},{8,12},{12,8},{16,20},{20,16},{24,28},{28,24},{1,5},{5... | collective-permute-start | bytes 1769480 | tf_op jit(solution)/shard_map/ppermute | solution.py:531
  43.0 0.7 copy-start.3
  50.7 6.6 %collective-permute-start.6 = (f32[1,1152,128]{2,1,0:T(8,128)}, f32[1,1152,128]{2,1,0:T(8,128)S(1)}, u32[]{:S(2)}, u32[]{:S(2)}) collective-permute-start(f32[1,1152,128]{2,1,0:T(8,128)} %get-tuple-element.26), channel_id=1, source_target_pairs={{0,4},{4,0},{8,12},{12,8},{16,20},{20,16},{24,28},{28,24},{1,5},{5... | collective-permute-start | bytes 1769480 | tf_op jit(solution)/shard_map/ppermute | solution.py:531
  57.2 0.8 copy-start.4
  57.2 1.1 copy-start.5
  57.3 1.3 copy-start.6
  57.3 1.4 copy-start.7
  95.6 4.8 %collective-permute-start.7 = (f32[4,1152,128]{2,1,0:T(8,128)}, f32[4,1152,128]{2,1,0:T(8,128)S(1)}, u32[]{:S(2)}, u32[]{:S(2)}) collective-permute-start(f32[4,1152,128]{2,1,0:T(8,128)} %get-tuple-element.28), channel_id=1, source_target_pairs={{0,4},{4,0},{8,12},{12,8},{16,20},{20,16},{24,28},{28,24},{1,5},{5... | collective-permute-start | bytes 7077896 | tf_op jit(solution)/shard_map/ppermute | solution.py:531
  100.4 1.4 copy-start
  109.1 42.5 %collective-permute-start.10 = (f32[1,128,256]{2,1,0:T(8,128)}, f32[1,128,256]{2,1,0:T(8,128)S(1)}, u32[]{:S(2)}, u32[]{:S(2)}) collective-permute-start(f32[1,128,256]{2,1,0:T(8,128)} %collect_points.7), channel_id=1, source_target_pairs={{0,24},{4,28},{8,16},{12,20},{16,8},{20,12},{24,0},{28,4},{1,25},{... | collective-permute-start | bytes 393224 | tf_op jit(solution)/shard_map/ppermute | solution.py:531
  119.5 7.9 %copy-start.8 = (f32[2,1,16384]{2,1,0:T(1,128)S(1)}, f32[2,1,16384]{2,1,0:T(1,128)}, u32[]{:S(2)}) copy-start(f32[2,1,16384]{2,1,0:T(1,128)} %param.7) | copy-start | bytes 393220
  119.5 32.1 %collective-permute-start.9 = (f32[1,128,256]{2,1,0:T(8,128)}, f32[1,128,256]{2,1,0:T(8,128)S(1)}, u32[]{:S(2)}, u32[]{:S(2)}) collective-permute-start(f32[1,128,256]{2,1,0:T(8,128)} %collect_points.6), channel_id=1, source_target_pairs={{0,16},{4,20},{8,24},{12,28},{16,0},{20,4},{24,8},{28,12},{1,17},{... | collective-permute-start | bytes 393224 | tf_op jit(solution)/shard_map/ppermute | solution.py:531
  127.4 24.3 %collective-permute-start.8 = (f32[1,128,256]{2,1,0:T(8,128)}, f32[1,128,256]{2,1,0:T(8,128)S(1)}, u32[]{:S(2)}, u32[]{:S(2)}) collective-permute-start(f32[1,128,256]{2,1,0:T(8,128)} %collect_points.5), channel_id=1, source_target_pairs={{0,8},{4,12},{8,0},{12,4},{16,24},{20,28},{24,16},{28,20},{1,9},{5... | collective-permute-start | bytes 393224 | tf_op jit(solution)/shard_map/ppermute | solution.py:531
  151.6 0.6 copy-start.9
  151.6 0.7 copy-start.10
  151.6 0.7 copy-start.11

commit v3 on v2

--- a/solution.py
+++ b/solution.py
@@ -14,7 +14,6 @@
 LANES = 128
 BF = jnp.bfloat16
 F32 = jnp.float32
-VMEM_BYTES = 56 * 1024 * 1024
 NT = (((1,), (1,)), ((), ()))
 
 
@@ -40,8 +39,10 @@
     pos = np.arange(N)
     angle = 2.0 * math.pi * ((pos[:, None] * pos[None, :]) % N) / N
     cb, sb = np.cos(angle), np.sin(angle)
-    b_fwd = np.block([[cb, -sb], [sb, cb]])
-    b_inv = np.block([[cb, sb], [-sb, cb]])
+    order = np.concatenate([pos[0::2], pos[1::2]])
+    co, so = cb[order], sb[order]
+    b_fwd = np.block([[co, -so], [so, co]])
+    b_inv = np.block([[co.T, so.T], [-so.T, co.T]])
     freq = np.arange(LANES)
     freq = np.where(freq < 64, freq, freq - LANES)
     keep = (np.abs(freq) < 48)[:, None]
@@ -70,12 +71,31 @@
     return jnp.concatenate([x[:, :LANES], x[:, LANES:]], axis=0)
 
 
+def wide(row, count):
+    tile = jnp.broadcast_to(row, (16, row.shape[1])).astype(BF)
+    return jnp.concatenate([tile] * (count // 16), axis=0)
+
+
+def ident(count):
+    return lax.broadcasted_iota(jnp.int32, (count, LANES), 0).astype(F32).astype(BF)
+
+
+def equal(row, ids):
+    code = wide(row, ids.shape[0])
+    return code == jnp.concatenate([ids, ids], axis=1)
+
+
+def one_hot(row, ids):
+    one = jnp.ones((ids.shape[0], CHUNK), BF)
+    return jnp.where(equal(row, ids), one, jnp.zeros_like(one))
+
+
 def floor_div(x, divisor):
     return jnp.floor((x + 0.5) * (1.0 / divisor))
 
 
-def sort_kernel(planes, m_ref, c_ref, out_ref, d_ref, acc_ref, val_ref, sum_ref, above_ref, gb_ref):
-    rows = m_ref.shape[0] // 2
+def sort_kernel(planes, m_ref, c_ref, out_ref, d_ref, acc_ref, val_ref, gb_ref, cum_ref, tot_ref, lane_ref):
+    rows = gb_ref.shape[0]
     m = fold(m_ref[...]).astype(F32)
     line = floor_div(m, N)
     gc = m - N * line
@@ -83,44 +103,58 @@
     gb = line - planes * ga
     ga = jnp.where(ga < 96, ga, ga - 96)
     gc = jnp.where(gc < 96, gc, gc - 64)
+    gb_ref[...] = gb
     lane_r = lax.broadcasted_iota(jnp.int32, (CHUNK, 2 * CHUNK), 0)
     lane_c = lax.broadcasted_iota(jnp.int32, (CHUNK, 2 * CHUNK), 1)
     tri = jnp.where((lane_r < lane_c) | (lane_c >= CHUNK), 1.0, 0.0).astype(BF)
-    row_r = lax.broadcasted_iota(jnp.int32, (rows, rows), 0)
-    row_c = lax.broadcasted_iota(jnp.int32, (rows, rows), 1)
+    row_r = lax.broadcasted_iota(jnp.int32, (rows + 16, rows), 0)
+    row_c = lax.broadcasted_iota(jnp.int32, (rows + 16, rows), 1)
     below = jnp.where(row_c < row_r, 1.0, 0.0).astype(BF)
+    masks = [jnp.where(gb == float(g), 1.0, 0.0).astype(BF) for g in range(planes)]
+    cum_ref[...] = mm(below, jnp.concatenate(masks, axis=1))
+    tot_ref[...] = jnp.zeros_like(tot_ref)
+    step = 3 if planes % 3 == 0 and planes > 3 else 1
+
+    def at(g):
+        return pl.ds(pl.multiple_of(g * CHUNK, CHUNK), CHUNK)
+
+    def gather(i, carry):
+        for j in range(step):
+            g = i * step + j
+            tot_ref[pl.ds(g, 1), :] = cum_ref[rows : rows + 8, at(g)][0:1]
+        return carry
+
+    lax.fori_loop(0, planes // step, gather, 0)
+    lane_ref[...] = mm(tot_ref[...].astype(BF), tri)
     step_id = lax.broadcasted_iota(jnp.int32, (8, CHUNK), 1).astype(F32)
-    base = jnp.zeros((1, CHUNK), F32)
-    place = jnp.zeros((rows, CHUNK), F32)
-    plane_of = jnp.zeros((8, CHUNK), F32)
-    gb_ref[...] = gb
-
-    def count(g, carry):
-        inside = gb_ref[...] == g.astype(F32)
-        sum_ref[g] = mm(jnp.where(inside, 1.0, 0.0).astype(BF), tri)
-        return carry
-
-    def climb(g, carry):
-        above_ref[g] = mm(below, sum_ref[g, :, CHUNK:].astype(BF))
-        return carry
-
-    lax.fori_loop(0, planes, count, 0)
-    lax.fori_loop(0, planes, climb, 0)
-    for g in range(planes):
-        above = above_ref[g]
-        place = jnp.where(gb == float(g), sum_ref[g, :, :CHUNK] + above + base, place)
-        base = base + above[rows - 1 : rows] + sum_ref[g, rows - 1 : rows, CHUNK:]
-        if g < planes - 1:
-            rank = g + jnp.floor((jnp.maximum(base, 1.0) - 1.0) * (1.0 / CHUNK))
-            plane_of = plane_of + jnp.where(rank < step_id, 1.0, 0.0)
+
+    def rank(i, carry):
+        base, place, plane_of = carry
+        for j in range(step):
+            g = i * step + j
+            gf = g.astype(F32)
+            lanes = lane_ref[pl.ds(g, 1), :]
+            here = cum_ref[0:rows, at(g)] + (lanes[:, :CHUNK] + base)
+            place = jnp.where(gb_ref[...] == gf, here, place)
+            base = base + lanes[:, CHUNK:]
+            end = gf + jnp.floor((jnp.maximum(base, 1.0) - 1.0) * (1.0 / CHUNK))
+            end = jnp.where(gf < planes - 1.0, end, 1e6)
+            plane_of = plane_of + jnp.where(end < step_id, 1.0, 0.0)
+        return base, place, plane_of
+
+    _, place, plane_of = lax.fori_loop(
+        0,
+        planes // step,
+        rank,
+        (jnp.zeros((1, CHUNK), F32), jnp.zeros((rows, CHUNK), F32), jnp.zeros((8, CHUNK), F32)),
+    )
     d_ref[...] = place
     re_h, re_l = split(fold(c_ref[0]))
     im_h, im_l = split(fold(c_ref[1]))
     for q, value in enumerate((re_h, re_l, im_h, im_l, ga, gb, gc)):
         val_ref[q] = value.astype(F32)
     acc_ref[...] = jnp.zeros_like(acc_ref)
-    hi_id = lax.broadcasted_iota(jnp.int32, (rows, CHUNK), 0).astype(F32).astype(BF)
-    lo_id = lax.broadcasted_iota(jnp.int32, (CHUNK, CHUNK), 0).astype(F32).astype(BF)
+    hi_id, lo_id = ident(rows), ident(CHUNK)
     zero = jnp.zeros((rows, CHUNK), BF)
 
     def body(i, carry):
@@ -131,18 +165,11 @@
         values = [val_ref[q, part, :] for q in range(7)]
         left, right = [], []
         for j in range(8):
-            at_hi = jnp.broadcast_to(hi[j : j + 1], (rows, CHUNK)).astype(BF) == hi_id
-            at_lo = jnp.broadcast_to(lo[j : j + 1], (CHUNK, CHUNK)).astype(BF) == lo_id
+            at_hi = equal(hi[j : j + 1], hi_id)
             left.append(
-                jnp.concatenate(
-                    [
-                        jnp.where(at_hi, jnp.broadcast_to(v[j : j + 1], (rows, CHUNK)).astype(BF), zero)
-                        for v in values
-                    ],
-                    axis=0,
-                )
+                jnp.concatenate([jnp.where(at_hi, wide(v[j : j + 1], rows), zero) for v in values], axis=0)
             )
-            right.append(jnp.where(at_lo, jnp.ones_like(lo_id), jnp.zeros_like(lo_id)))
+            right.append(one_hot(lo[j : j + 1], lo_id))
         acc_ref[...] += lax.dot_general(
             jnp.concatenate(left, axis=1), jnp.concatenate(right, axis=1), NT, preferred_element_type=F32
         )
@@ -213,12 +240,6 @@
     return er, ei
 
 
-def one_hot(code_row):
-    ident = lax.broadcasted_iota(jnp.int32, (LANES, CHUNK), 0).astype(F32).astype(BF)
-    code = jnp.broadcast_to(code_row, (LANES, CHUNK)).astype(BF)
-    return jnp.where(code == ident, jnp.ones_like(ident), jnp.zeros_like(ident))
-
-
 def firsts(planes):
     me = lax.axis_index("grid")
     return (me * planes).astype(F32), ((me ^ 1) * planes).astype(F32)
@@ -232,11 +253,12 @@
     return g, c, code
 
 
-def spread_kernel(planes, height, unroll, slab_ref, steps_ref, own_ref, sib_ref, w_ref, code_ref, a_ref):
+def spread_kernel(planes, height, unroll, slab_ref, steps_ref, own_ref, sib_ref, w_ref, code_ref, id_ref, a_ref):
     rows = a_ref.shape[0]
     freq, gb, gc = decode(slab_ref[0, 2 * rows : 3 * rows], planes)
     code_ref[0] = gb
     code_ref[1] = gc
+    id_ref[...] = ident(LANES)
     re, im = slab_ref[0, 0:rows], slab_ref[0, rows : 2 * rows]
     for q, first in enumerate(firsts(planes)):
         sr, si = phase(freq, first)
@@ -272,9 +294,10 @@
     sib_ref[...] = jnp.zeros_like(sib_ref)
 
     def visit(i, carry):
+        ids = id_ref[...]
         for j in range(unroll):
             g, c, code = pair_code(planes, steps_ref, code_ref, rows, i * unroll + j)
-            got = lax.dot_general(a_ref[c], one_hot(code), NT, preferred_element_type=F32)
+            got = lax.dot_general(a_ref[c], one_hot(code, ids), NT, preferred_element_type=F32)
             got = got[: 4 * height] + got[4 * height :]
             where = pl.ds(pl.multiple_of(g * (2 * height), 8), 2 * height)
             own_ref[0, where, :] += got[: 2 * height]
@@ -285,12 +308,13 @@
 
 
 def collect_kernel(
-    planes, height, unroll, slab_ref, steps_ref, own_ref, sib_ref, h_ref, w_ref, code_ref, u2_ref, g_ref
+    planes, height, unroll, slab_ref, steps_ref, own_ref, sib_ref, h_ref, w_ref, code_ref, id_ref, u2_ref, g_ref
 ):
     rows = g_ref.shape[0]
     freq, gb, gc = decode(slab_ref[0, 2 * rows : 3 * rows], planes)
     code_ref[0] = gb
     code_ref[1] = gc
+    id_ref[...] = ident(LANES)
     for q, first in enumerate(firsts(planes)):
         w_ref[2 * q], w_ref[2 * q + 1] = phase(freq, first)
     powers(freq, w_ref)
@@ -301,9 +325,10 @@
     g_ref[...] = jnp.zeros_like(g_ref)
 
     def visit(i, carry):
+        ids = id_ref[...]
         for j in range(unroll):
             g, c, code = pair_code(planes, steps_ref, code_ref, rows, i * unroll + j)
-            got = mm(u2_ref[g], one_hot(code))
+            got = mm(u2_ref[g], one_hot(code, ids))
             g_ref[c] += got[: 4 * height] + got[4 * height :]
         return carry
 
@@ -342,7 +367,8 @@
 
 def potential_kernel(group, height, planes, calls, *refs):
     own, sib = refs[:calls], refs[calls : 2 * calls]
-    v_ref, bf_ref, cf_ref, ci_ref, bi_ref, keep_ref, send_ref, t_ref, u_ref, sems = refs[2 * calls :]
+    v_ref, bf_ref, cf_ref, ci_ref, bi_ref = refs[2 * calls : 2 * calls + 5]
+    keep_ref, send_ref, t_ref, u_ref, sems = refs[-5:]
     step = pl.program_id(0)
     me = lax.axis_index("grid")
     lines = planes * 2 * height
@@ -397,7 +423,13 @@
     )
     high, low = split(x)
     x = mm(jnp.concatenate([high, high, low], axis=1), cf_ref[...])
-    v = jnp.concatenate([v_ref[j] for j in range(group)], axis=0)
+    v = []
+    for j in range(group):
+        line = (step * group + j) % 8
+        t = [v_ref[0, pl.ds(8 * q + line, N // 2, stride=24), :] for q in range(3)]
+        v.append(jnp.concatenate([t[0], t[1][:, :64]], axis=1))
+        v.append(jnp.concatenate([t[1][:, 64:], t[2]], axis=1))
+    v = jnp.concatenate(v, axis=0)
     x = x * jnp.concatenate([v, v], axis=1)
     high, low = split(x)
     x = mm(jnp.concatenate([high, high, low], axis=1), ci_ref[...])
@@ -425,9 +457,10 @@
                 copy.wait()
 
 
-def unsort_kernel(arrivals, *refs):
+def unsort_kernel(arrivals, bands, *refs):
     recv_refs = refs[:arrivals]
-    d_ref, coef_ref, h_ref, part_ref, hl_ref, wide_ref = refs[arrivals:]
+    d_ref, *coef_refs = refs[arrivals : arrivals + 1 + bands]
+    h_ref, part_ref, hl_ref, wide_ref = refs[arrivals + 1 + bands :]
     rows = d_ref.shape[0]
     total = None
     for recv in recv_refs:
@@ -437,7 +470,7 @@
     hl_ref[0 : 2 * rows] = high
     hl_ref[2 * rows :] = low
     hi_id = lax.broadcasted_iota(jnp.int32, (rows, CHUNK), 0).astype(F32)
-    lo_id = lax.broadcasted_iota(jnp.int32, (CHUNK, CHUNK), 0).astype(F32).astype(BF)
+    lo_id = ident(CHUNK)
 
     def body(i, carry):
         part = pl.ds(pl.multiple_of(i * 8, 8), 8)
@@ -446,8 +479,7 @@
         lo = d - CHUNK * hi
         real, imag = [], []
         for j in range(8):
-            at_lo = jnp.broadcast_to(lo[j : j + 1], (CHUNK, CHUNK)).astype(BF) == lo_id
-            got = mm(hl_ref[...], jnp.where(at_lo, jnp.ones_like(lo_id), jnp.zeros_like(lo_id)))
+            got = mm(hl_ref[...], one_hot(lo[j : j + 1], lo_id))
             got = got[: 2 * rows] + got[2 * rows :]
             at_hi = jnp.broadcast_to(hi[j : j + 1], (rows, CHUNK)) == hi_id
             real.append(jnp.sum(jnp.where(at_hi, got[:rows], 0.0), axis=0, keepdims=True))
@@ -461,8 +493,8 @@
     h_ref[0] = hr
     h_ref[1] = hi
     real, imag = [], []
-    for i in range(coef_ref.shape[0]):
-        cr, ci = coef_ref[i, 0], coef_ref[i, 1]
+    for coef in coef_refs:
+        cr, ci = coef[0], coef[1]
         real.append(jnp.sum(cr * hr + ci * hi, axis=0, keepdims=True))
         imag.append(jnp.sum(cr * hi - ci * hr, axis=0, keepdims=True))
     sums = jnp.concatenate(real + imag, axis=0)
@@ -470,26 +502,36 @@
         part_ref[s] = sums
 
 
-def residual_kernel(scale, sum_ref, h_ref, coef_ref, out_ref, sub_ref):
-    bands = coef_ref.shape[0]
+def residual_kernel(scale, bands, sum_ref, h_ref, *refs):
+    coef_refs, (out_ref, sub_ref) = refs[:bands], refs[bands:]
+    band = lax.axis_index("band")
     sub = sum_ref[0]
     for s in range(1, sum_ref.shape[0]):
         sub = sub + sum_ref[s]
     sub = jnp.sum(sub, axis=1, keepdims=True) * scale
-    sub_ref[0] = sub[:bands]
-    sub_ref[1] = sub[bands:]
+    lane = lax.broadcasted_iota(jnp.int32, (1, LANES), 1)
     hr, hi = h_ref[0], h_ref[1]
-    for i in range(bands):
-        sr, si = sub[i : i + 1], sub[bands + i : bands + i + 1]
-        cr, ci = coef_ref[i, 0], coef_ref[i, 1]
+    line_re = line_im = jnp.zeros((1, LANES), F32)
+    for shift, coef in enumerate(coef_refs):
+        sr, si = sub[shift : shift + 1], sub[bands + shift : bands + shift + 1]
+        here = lane == lax.rem(band + bands - shift, bands)
+        line_re = jnp.where(here, sr, line_re)
+        line_im = jnp.where(here, si, line_im)
+        cr, ci = coef[0], coef[1]
         hr = hr - (sr * cr - si * ci)
         hi = hi - (si * cr + sr * ci)
     out_ref[0] = hr
     out_ref[1] = hi
-
-
-def params(**extra):
-    return pltpu.CompilerParams(vmem_limit_bytes=VMEM_BYTES, **extra)
+    sub_ref[0] = line_re[:, :bands]
+    sub_ref[1] = line_im[:, :bands]
+
+
+def params(mib):
+    return pltpu.CompilerParams(vmem_limit_bytes=mib * 1024 * 1024)
+
+
+def cost(flops):
+    return pl.CostEstimate(flops=int(flops), bytes_accessed=0, transcendentals=0)
 
 
 def whole(shape):
@@ -503,12 +545,14 @@
     count = coefficients.shape[2]
     rows = count // CHUNK
     height = -(-planes // 8) * 8
-    group = 2 if planes % 2 == 0 else 1
+    group = 4 if planes % 4 == 0 else 1
     unroll = 22
     me = lax.axis_index("grid")
     half = slabs // 2
     coef = coefficients.reshape(2, 2 * rows, LANES)
-    coefs = lax.all_gather(coef, "band")
+    coefs = [coef]
+    for shift in range(1, bands):
+        coefs.append(lax.ppermute(coef, "band", [(i, (i + shift) % bands) for i in range(bands)]))
     table_rows = 3 * rows + 8
     sorted_pts, dest = pl.pallas_call(
         functools.partial(sort_kernel, planes),
@@ -519,11 +563,13 @@
         scratch_shapes=[
             pltpu.VMEM((7 * rows, CHUNK), F32),
             pltpu.VMEM((7, rows, CHUNK), F32),
-            pltpu.VMEM((planes, rows, 2 * CHUNK), F32),
-            pltpu.VMEM((planes, rows, CHUNK), F32),
             pltpu.VMEM((rows, CHUNK), F32),
+            pltpu.VMEM((rows + 16, planes * CHUNK), F32),
+            pltpu.VMEM((-(-planes // 16) * 16, CHUNK), F32),
+            pltpu.VMEM((-(-planes // 16) * 16, 2 * CHUNK), F32),
         ],
-        compiler_params=params(),
+        compiler_params=params(16),
+        cost_estimate=cost(1e10),
         name="sort_points",
     )(index_map.reshape(2 * rows, LANES), coef)
 
@@ -541,7 +587,7 @@
     slab_spec = pl.BlockSpec((1, table_rows, CHUNK), lambda s: (s, 0, 0))
     steps_spec = pl.BlockSpec((None, 8, CHUNK), lambda s: (s, table_rows // 8 - 1, 0), memory_space=pltpu.SMEM)
     block_spec = pl.BlockSpec((1, lines, LANES), lambda s: (s, 0, 0))
-    point_scratch = [pltpu.VMEM((12, rows, CHUNK), F32), pltpu.VMEM((2, rows, CHUNK), F32)]
+    point_scratch = [pltpu.VMEM((12, rows, CHUNK), F32), pltpu.VMEM((2, rows, CHUNK), F32), pltpu.VMEM((LANES, LANES), BF)]
     spread = pl.pallas_call(
         functools.partial(spread_kernel, planes, height, unroll),
         grid=(per_call,),
@@ -549,7 +595,8 @@
         out_specs=(block_spec, block_spec),
         out_shape=(jax.ShapeDtypeStruct((per_call, lines, LANES), F32),) * 2,
         scratch_shapes=point_scratch + [pltpu.VMEM((rows, 8 * height, CHUNK), BF)],
-        compiler_params=params(),
+        compiler_params=params(20),
+        cost_estimate=cost(8e9),
         name="spread_points",
     )
     own, sib = [], []
@@ -557,14 +604,18 @@
         mine, theirs = spread(table, table)
         own.append(mine)
         sib.append(swap(theirs, 1))
+    cells = potential if height == planes else jnp.pad(potential, ((0, height - planes), (0, 0)))
+    cells = cells.reshape(height // 8, 8, N * N // LANES, LANES).transpose(0, 2, 1, 3)
+    cells = cells.reshape(height // 8, N * N // 16, LANES)
     constants = [jnp.asarray(t) for t in tables()]
     anywhere = pl.BlockSpec(memory_space=pl.ANY)
     keep, send = pl.pallas_call(
         functools.partial(potential_kernel, group, height, planes, calls),
         grid=(planes // group,),
         in_specs=[anywhere] * (2 * calls)
-        + [pl.BlockSpec((group, N, N), lambda i: (i, 0, 0))]
-        + [whole(t.shape) for t in constants],
+        + [pl.BlockSpec((1, N * N // 16, LANES), lambda i: (i * group // 8, 0, 0))]
+        + [whole(t.shape) for t in constants]
+        + [anywhere] * (bands - 1),
         out_specs=(anywhere, anywhere),
         out_shape=(jax.ShapeDtypeStruct((half, lines, LANES), F32),) * 2,
         scratch_shapes=[
@@ -572,9 +623,10 @@
             pltpu.VMEM((slabs * lines, LANES), F32),
             pltpu.SemaphoreType.DMA((2, half)),
         ],
-        compiler_params=params(),
+        compiler_params=params(40),
+        cost_estimate=cost(4e10),
         name="apply_potential",
-    )(*own, *sib, potential.reshape(planes, N, N), *constants)
+    )(*own, *sib, cells, *constants, *coefs[1:])
     other = swap(send, 1)
     partial = []
     for call, table in enumerate(points):
@@ -591,7 +643,8 @@
                     pltpu.VMEM((planes, 8 * height, LANES), BF),
                     pltpu.VMEM((rows, 4 * height, CHUNK), F32),
                 ],
-                compiler_params=params(),
+                compiler_params=params(24),
+                cost_estimate=cost(8e9),
                 name="collect_points",
             )(table, table, keep, other)
         )
@@ -603,26 +656,28 @@
         blocks = jnp.where(((ids ^ me) % 2 == 0)[:, None, None], blocks, 0.0)
         arrived = [lax.all_to_all(blocks, "grid", split_axis=0, concat_axis=0, tiled=True)]
     applied, part = pl.pallas_call(
-        functools.partial(unsort_kernel, len(arrived)),
+        functools.partial(unsort_kernel, len(arrived), bands),
         out_shape=(
             jax.ShapeDtypeStruct((2, 2 * rows, LANES), F32),
             jax.ShapeDtypeStruct((slabs, 2 * bands, LANES), F32),
         ),
         scratch_shapes=[pltpu.VMEM((4 * rows, CHUNK), BF), pltpu.VMEM((2, rows, CHUNK), F32)],
-        compiler_params=params(),
+        compiler_params=params(12),
+        cost_estimate=cost(6e9),
         name="unsort_points",
-    )(*arrived, dest, coefs)
+    )(*arrived, dest, *coefs)
     sums = lax.all_to_all(part, "grid", split_axis=0, concat_axis=0, tiled=True)
     resid, sub = pl.pallas_call(
-        functools.partial(residual_kernel, 1.0 / (count * slabs)),
+        functools.partial(residual_kernel, 1.0 / (count * slabs), bands),
         out_shape=(
             jax.ShapeDtypeStruct((2, 2 * rows, LANES), F32),
-            jax.ShapeDtypeStruct((2, bands, 1), F32),
+            jax.ShapeDtypeStruct((2, 1, bands), F32),
         ),
-        compiler_params=params(),
+        compiler_params=params(8),
+        cost_estimate=cost(2e9),
         name="residual",
-    )(sums, applied, coefs)
-    return sub, resid.reshape(2, 1, count)
+    )(sums, applied, *coefs)
+    return sub.transpose(0, 2, 1), resid.reshape(2, 1, count)
 
 
 def solution(mesh):

time: 171 us -> 134 us (0.78)
  Pallas kernels: 117 us -> 84.2 us
  waiting for transfers between devices: 4.76 us -> 25.2 us
  blocking collectives: 25.6 us -> 7.38 us
  local copies, waits for them, and re-layouts: 12.9 us -> 1.76 us
  starting transfers between devices: 9.07 us -> 14.3 us
    ppermute x0 -> x3, waiting for transfers between devices: none -> 17.4 us  [local(): lax.ppermute(coef, 'band', [(i, (i + shift) % bands) for i in range(bands)])]
    all_gather x1 -> x0, blocking collectives: 16.8 us -> none  [local(): coefs = lax.all_gather(coef, 'band')]
    pallas_call x1, Pallas kernels: 36.9 us -> 25.7 us  [local(): pl.pallas_call(functools.partial(potential_kernel, group, height, planes,...]
    pallas_call x1, Pallas kernels: 14.7 us -> 6.63 us  [local(): pl.pallas_call(functools.partial(sort_kernel, planes), out_shape=(jax.Sha...]
    reshape x1 -> x0, local copies, waits for them, and re-layouts: 6 us -> none  [local(): potential.reshape(planes, N, N)]
    pallas_call x4, Pallas kernels: 29.5 us -> 24.1 us  [local(): pl.pallas_call(functools.partial(collect_kernel, planes, height, unroll),...]
    pallas_call x4, Pallas kernels: 28.3 us -> 23.1 us  [local(): mine, theirs = spread(table, table)]
    unnamed x25 -> x14, local copies, waits for them, and re-layouts: 6.95 us -> 1.76 us
  transfers between devices with their start and end apart: 11 -> 14, of which waited for: 1 -> 5; matrix products, arithmetic and copies ran while one was open for 4% -> 0% of each run, Pallas kernels for 30% -> 31%
where the time goes in v3:
time: 134 us
  Pallas kernels  84.2 us (63%)
  waiting for transfers between devices  25.2 us (19%)
  starting transfers between devices  14.3 us (11%)
  blocking collectives  7.38 us (6%)
  local copies, waits for them, and re-layouts  1.76 us (1%)
    pallas_call x1, Pallas kernels, local(): pl.pallas_call(functools.partial(potential_kernel, group, height, planes,...  25.7 us
    pallas_call x4, Pallas kernels, local(): pl.pallas_call(functools.partial(collect_kernel, planes, height, unroll),...  24.1 us
    pallas_call x4, Pallas kernels, local(): mine, theirs = spread(table, table)  23.1 us
    ppermute x3, waiting for transfers between devices, local(): lax.ppermute(coef, 'band', [(i, (i + shift) % bands) for i in range(bands)])  17.4 us
    ppermute x11, starting transfers between devices, swap(): return lax.ppermute(x, 'grid', [(i, i ^ bits) for i in range(slabs)])  9.16 us
    ppermute x11, waiting for transfers between devices, swap(): return lax.ppermute(x, 'grid', [(i, i ^ bits) for i in range(slabs)])  7.8 us
    all_to_all x1, blocking collectives, local(): sums = lax.all_to_all(part, 'grid', split_axis=0, concat_axis=0, tiled=True)  7.38 us
    pallas_call x1, Pallas kernels, local(): pl.pallas_call(functools.partial(sort_kernel, planes), out_shape=(jax.Sha...  6.63 us
  transfers between devices with their start and end apart: 14, of which 5 were waited for; matrix products, arithmetic and copies ran while one was open for 0% of the time, Pallas kernels for 31%

profile of v3, /device:TPU:0, one launch (start us, length us, event | category | flops | bytes accessed | tf_op | source)
XLA Modules:
  0.0 133.7 jit_solution(442945842710521513)
XLA Ops:
  0.6 0.9 copy-done
  1.5 0.8 copy-done.2
  2.4 6.6 %sort_points.1 = (f32[200,256]{1,0:T(8,128)S(1)}, f32[64,256]{1,0:T(8,128)S(1)}) custom-call(s32[128,128]{1,0:T(8,128)S(1)} %bitcast.37, f32[2,128,128]{2,1,0:T(8,128)S(1)} %bitcast.31), custom_call_target="tpu_custom_call" | custom-call | flops 10000000000 | tf_op jit(solution)/shard_map/sort_points/pallas_call | solution.py:557
  9.0 4.0 %collective-permute-start.2 = (f32[200,256]{1,0:T(8,128)S(1)}, f32[200,256]{1,0:T(8,128)S(1)}, u32[]{:S(2)}, u32[]{:S(2)}) collective-permute-start(f32[200,256]{1,0:T(8,128)S(1)} %get-tuple-element.18), channel_id=1, source_target_pairs={{0,24},{4,28},{8,16},{12,20},{16,8},{20,12},{24,0},{28,4},{1,25},{... | collective-permute-start | bytes 614408 | tf_op jit(solution)/shard_map/ppermute | solution.py:577
  13.6 5.8 %spread_points.4 = (f32[1,1152,128]{2,1,0:T(8,128)S(1)}, f32[1,1152,128]{2,1,0:T(8,128)S(1)}) custom-call(f32[1,200,256]{2,1,0:T(8,128)S(1)} %bitcast.15, f32[1,200,256]{2,1,0:T(8,128)S(1)} %bitcast.16), custom_call_target="tpu_custom_call" | custom-call | flops 8000000000 | tf_op jit(solution)/shard_map/spread_points/pallas_call | solution.py:604
  19.5 3.3 %collective-permute-done = f32[200,256]{1,0:T(8,128)S(1)} collective-permute-done((f32[200,256]{1,0:T(8,128)S(1)}, f32[200,256]{1,0:T(8,128)S(1)}, u32[]{:S(2)}, u32[]{:S(2)}) %collective-permute-start) | collective-permute-done | bytes 204832 | tf_op jit(solution)/shard_map/ppermute | solution.py:577
  22.7 5.8 %spread_points.5 = (f32[1,1152,128]{2,1,0:T(8,128)S(1)}, f32[1,1152,128]{2,1,0:T(8,128)S(1)}) custom-call(f32[1,200,256]{2,1,0:T(8,128)S(1)} %bitcast.27, f32[1,200,256]{2,1,0:T(8,128)S(1)} %bitcast.28), custom_call_target="tpu_custom_call" | custom-call | flops 8000000000 | tf_op jit(solution)/shard_map/spread_points/pallas_call | solution.py:604
  28.6 5.8 %spread_points.6 = (f32[1,1152,128]{2,1,0:T(8,128)S(1)}, f32[1,1152,128]{2,1,0:T(8,128)S(1)}) custom-call(f32[1,200,256]{2,1,0:T(8,128)S(1)} %bitcast.23, f32[1,200,256]{2,1,0:T(8,128)S(1)} %bitcast.24), custom_call_target="tpu_custom_call" | custom-call | flops 8000000000 | tf_op jit(solution)/shard_map/spread_points/pallas_call | solution.py:604
  35.0 5.8 %spread_points.7 = (f32[1,1152,128]{2,1,0:T(8,128)S(1)}, f32[1,1152,128]{2,1,0:T(8,128)S(1)}) custom-call(f32[1,200,256]{2,1,0:T(8,128)S(1)} %bitcast.19, f32[1,200,256]{2,1,0:T(8,128)S(1)} %bitcast.20), custom_call_target="tpu_custom_call" | custom-call | flops 8000000000 | tf_op jit(solution)/shard_map/spread_points/pallas_call | solution.py:604
  40.9 3.7 %collective-permute-start.9 = (f32[2,128,128]{2,1,0:T(8,128)S(1)}, f32[2,128,128]{2,1,0:T(8,128)S(1)}, u32[]{:S(2)}, u32[]{:S(2)}) collective-permute-start(f32[2,128,128]{2,1,0:T(8,128)S(1)} %bitcast.32), channel_id=1, source_target_pairs={{0,3},{1,0},{2,1},{3,2},{4,7},{5,4},{6,5},{7,6},{8,11},{9,8},{10,9... | collective-permute-start | bytes 393224 | tf_op jit(solution)/shard_map/ppermute | solution.py:555
  44.6 3.4 %collective-permute-done.9.refs_15_.refs_8_.refs_3_ = f32[2,128,128]{2,1,0:T(8,128)S(1)} collective-permute-done((f32[2,128,128]{2,1,0:T(8,128)S(1)}, f32[2,128,128]{2,1,0:T(8,128)S(1)}, u32[]{:S(2)}, u32[]{:S(2)}) %collective-permute-start.9) | collective-permute-done | bytes 131104 | tf_op jit(solution)/shard_map/ppermute | solution.py:555
  47.9 1.5 %collective-permute-start.8 = (f32[2,128,128]{2,1,0:T(8,128)S(1)}, f32[2,128,128]{2,1,0:T(8,128)S(1)}, u32[]{:S(2)}, u32[]{:S(2)}) collective-permute-start(f32[2,128,128]{2,1,0:T(8,128)S(1)} %bitcast.33), channel_id=1, source_target_pairs={{0,2},{1,3},{2,0},{3,1},{4,6},{5,7},{6,4},{7,5},{8,10},{9,11},{10,... | collective-permute-start | bytes 393224 | tf_op jit(solution)/shard_map/ppermute | solution.py:555
  49.4 7.3 %collective-permute-done.8.refs_14_.refs_7_.refs_2_ = f32[2,128,128]{2,1,0:T(8,128)S(1)} collective-permute-done((f32[2,128,128]{2,1,0:T(8,128)S(1)}, f32[2,128,128]{2,1,0:T(8,128)S(1)}, u32[]{:S(2)}, u32[]{:S(2)}) %collective-permute-start.8) | collective-permute-done | bytes 131104 | tf_op jit(solution)/shard_map/ppermute | solution.py:555
  56.7 6.8 %collective-permute-done.7.refs_13_.refs_6_.refs_1_ = f32[2,128,128]{2,1,0:T(8,128)S(1)} collective-permute-done((f32[2,128,128]{2,1,0:T(8,128)S(1)}, f32[2,128,128]{2,1,0:T(8,128)S(1)}, u32[]{:S(2)}, u32[]{:S(2)}) %collective-permute-start.7) | collective-permute-done | bytes 131104 | tf_op jit(solution)/shard_map/ppermute | solution.py:555
  63.5 25.7 %apply_potential.1 = (f32[4,1152,128]{2,1,0:T(8,128)S(1)}, f32[4,1152,128]{2,1,0:T(8,128)S(1)}) custom-call(f32[1,1152,128]{2,1,0:T(8,128)S(1)} %get-tuple-element.19.refs_0_, f32[1,1152,128]{2,1,0:T(8,128)S(1)} %get-tuple-element.20.refs_1_, f32[1,1152,128]{2,1,0:T(8,128)S(1)} %get-tuple-element.21.refs_2_, f32[1,1152,128]{2,1,0:T(8,128)S(1)} %get-tuple-element.22.refs_3_, ...), custom_call_target="tpu_custom_call" | custom-call | flops 40000000000 | tf_op jit(solution)/shard_map/apply_potential/pallas_call | solution.py:612
  89.3 4.5 %collective-permute-done.10.sib_ref = f32[4,1152,128]{2,1,0:T(8,128)S(1)} collective-permute-done((f32[4,1152,128]{2,1,0:T(8,128)S(1)}, f32[4,1152,128]{2,1,0:T(8,128)S(1)}, u32[]{:S(2)}, u32[]{:S(2)}) %collective-permute-start.10) | collective-permute-done | bytes 2359328 | tf_op jit(solution)/shard_map/ppermute | solution.py:577
  93.8 6.0 %collect_points.5 = f32[1,128,256]{2,1,0:T(8,128)S(1)} custom-call(f32[1,200,256]{2,1,0:T(8,128)S(1)} %bitcast.29, f32[1,200,256]{2,1,0:T(8,128)S(1)} %bitcast.30, f32[4,1152,128]{2,1,0:T(8,128)S(1)} %get-tuple-element.27.own_ref, f32[4,1152,128]{2,1,0:T(8,128)S(1)} %collective-permute-done.10.sib_ref), custom_call_target="tpu_custom_call" | custom-call | flops 8000000000 | tf_op jit(solution)/shard_map/collect_points/pallas_call | solution.py:635
  99.8 1.5 %collective-permute-start.11 = (f32[1,128,256]{2,1,0:T(8,128)S(1)}, f32[1,128,256]{2,1,0:T(8,128)S(1)}, u32[]{:S(2)}, u32[]{:S(2)}) collective-permute-start(f32[1,128,256]{2,1,0:T(8,128)S(1)} %collect_points.5), channel_id=1, source_target_pairs={{0,8},{4,12},{8,0},{12,4},{16,24},{20,28},{24,16},{28,20},{1,9},{5... | collective-permute-start | bytes 393224 | tf_op jit(solution)/shard_map/ppermute | solution.py:577
  101.4 6.0 %collect_points.6 = f32[1,128,256]{2,1,0:T(8,128)S(1)} custom-call(f32[1,200,256]{2,1,0:T(8,128)S(1)} %bitcast.25, f32[1,200,256]{2,1,0:T(8,128)S(1)} %bitcast.26, f32[4,1152,128]{2,1,0:T(8,128)S(1)} %get-tuple-element.27.own_ref, f32[4,1152,128]{2,1,0:T(8,128)S(1)} %collective-permute-done.10.sib_ref), custom_call_target="tpu_custom_call" | custom-call | flops 8000000000 | tf_op jit(solution)/shard_map/collect_points/pallas_call | solution.py:635
  108.0 6.0 %collect_points.7 = f32[1,128,256]{2,1,0:T(8,128)S(1)} custom-call(f32[1,200,256]{2,1,0:T(8,128)S(1)} %bitcast.21, f32[1,200,256]{2,1,0:T(8,128)S(1)} %bitcast.22, f32[4,1152,128]{2,1,0:T(8,128)S(1)} %get-tuple-element.27.own_ref, f32[4,1152,128]{2,1,0:T(8,128)S(1)} %collective-permute-done.10.sib_ref), custom_call_target="tpu_custom_call" | custom-call | flops 8000000000 | tf_op jit(solution)/shard_map/collect_points/pallas_call | solution.py:635
  114.0 1.6 %collective-permute-start.13 = (f32[1,128,256]{2,1,0:T(8,128)S(1)}, f32[1,128,256]{2,1,0:T(8,128)S(1)}, u32[]{:S(2)}, u32[]{:S(2)}) collective-permute-start(f32[1,128,256]{2,1,0:T(8,128)S(1)} %collect_points.7), channel_id=1, source_target_pairs={{0,24},{4,28},{8,16},{12,20},{16,8},{20,12},{24,0},{28,4},{1,25},{... | collective-permute-start | bytes 393224 | tf_op jit(solution)/shard_map/ppermute | solution.py:577
  115.6 6.0 %collect_points.4.refs_0_ = f32[1,128,256]{2,1,0:T(8,128)S(1)} custom-call(f32[1,200,256]{2,1,0:T(8,128)S(1)} %bitcast.17, f32[1,200,256]{2,1,0:T(8,128)S(1)} %bitcast.18, f32[4,1152,128]{2,1,0:T(8,128)S(1)} %get-tuple-element.27.own_ref, f32[4,1152,128]{2,1,0:T(8,128)S(1)} %collective-permute-done.10.sib_ref), custom_call_target="tpu_custom_call" | custom-call | flops 8000000000 | tf_op jit(solution)/shard_map/collect_points/pallas_call | solution.py:635
  121.6 3.8 %unsort_points.1 = (f32[2,128,128]{2,1,0:T(8,128)S(1)}, f32[8,8,128]{2,1,0:T(8,128)S(1)}) custom-call(f32[1,128,256]{2,1,0:T(8,128)S(1)} %collect_points.4.refs_0_, f32[1,128,256]{2,1,0:T(8,128)S(1)} %collective-permute-done.11.refs_1_, f32[1,128,256]{2,1,0:T(8,128)S(1)} %collective-permute-done.12.refs_2_, ...), custom_call_target="tpu_custom_call" | custom-call | flops 6000000000 | tf_op jit(solution)/shard_map/unsort_points/pallas_call | solution.py:658
  125.5 7.4 %all_to_all.5.sum_ref = f32[8,8,128]{2,1,0:T(8,128)S(1)} all-to-all(f32[8,8,128]{2,1,0:T(8,128)S(1)} %get-tuple-element.30), channel_id=1, replica_groups=mesh['grid'=8,'band'=4] {'grid'}, dimensions={0} | all-to-all | bytes 65536 | tf_op jit(solution)/shard_map/all_to_all | solution.py:669
  (31 shorter events, 3.0 us)
Async XLA Ops:
  0.6 0.9 copy-start
  1.5 0.8 copy-start.2
  9.0 25.9 %collective-permute-start.2 = (f32[200,256]{1,0:T(8,128)S(1)}, f32[200,256]{1,0:T(8,128)S(1)}, u32[]{:S(2)}, u32[]{:S(2)}) collective-permute-start(f32[200,256]{1,0:T(8,128)S(1)} %get-tuple-element.18), channel_id=1, source_target_pairs={{0,24},{4,28},{8,16},{12,20},{16,8},{20,12},{24,0},{28,4},{1,25},{... | collective-permute-start | bytes 614408 | tf_op jit(solution)/shard_map/ppermute | solution.py:577
  13.0 15.6 %collective-permute-start.1 = (f32[200,256]{1,0:T(8,128)S(1)}, f32[200,256]{1,0:T(8,128)S(1)}, u32[]{:S(2)}, u32[]{:S(2)}) collective-permute-start(f32[200,256]{1,0:T(8,128)S(1)} %get-tuple-element.18), channel_id=1, source_target_pairs={{0,16},{4,20},{8,24},{12,28},{16,0},{20,4},{24,8},{28,12},{1,17},{... | collective-permute-start | bytes 614408 | tf_op jit(solution)/shard_map/ppermute | solution.py:577
  13.5 9.3 %collective-permute-start = (f32[200,256]{1,0:T(8,128)S(1)}, f32[200,256]{1,0:T(8,128)S(1)}, u32[]{:S(2)}, u32[]{:S(2)}) collective-permute-start(f32[200,256]{1,0:T(8,128)S(1)} %get-tuple-element.18), channel_id=1, source_target_pairs={{0,8},{4,12},{8,0},{12,4},{16,24},{20,28},{24,16},{28,20},{1,9},{5... | collective-permute-start | bytes 614408 | tf_op jit(solution)/shard_map/ppermute | solution.py:577
  19.4 44.0 %collective-permute-start.3 = (f32[1,1152,128]{2,1,0:T(8,128)S(1)}, f32[1,1152,128]{2,1,0:T(8,128)S(1)}, u32[]{:S(2)}, u32[]{:S(2)}) collective-permute-start(f32[1,1152,128]{2,1,0:T(8,128)S(1)} %get-tuple-element.23), channel_id=1, source_target_pairs={{0,4},{4,0},{8,12},{12,8},{16,20},{20,16},{24,28},{28,24},{1,5},{5... | collective-permute-start | bytes 1769480 | tf_op jit(solution)/shard_map/ppermute | solution.py:577
  28.5 34.9 %collective-permute-start.4 = (f32[1,1152,128]{2,1,0:T(8,128)S(1)}, f32[1,1152,128]{2,1,0:T(8,128)S(1)}, u32[]{:S(2)}, u32[]{:S(2)}) collective-permute-start(f32[1,1152,128]{2,1,0:T(8,128)S(1)} %get-tuple-element.24), channel_id=1, source_target_pairs={{0,4},{4,0},{8,12},{12,8},{16,20},{20,16},{24,28},{28,24},{1,5},{5... | collective-permute-start | bytes 1769480 | tf_op jit(solution)/shard_map/ppermute | solution.py:577
  34.4 29.0 %collective-permute-start.5 = (f32[1,1152,128]{2,1,0:T(8,128)S(1)}, f32[1,1152,128]{2,1,0:T(8,128)S(1)}, u32[]{:S(2)}, u32[]{:S(2)}) collective-permute-start(f32[1,1152,128]{2,1,0:T(8,128)S(1)} %get-tuple-element.25), channel_id=1, source_target_pairs={{0,4},{4,0},{8,12},{12,8},{16,20},{20,16},{24,28},{28,24},{1,5},{5... | collective-permute-start | bytes 1769480 | tf_op jit(solution)/shard_map/ppermute | solution.py:577
  35.0 5.9 %copy-start.1 = (f32[2,1,16384]{2,1,0:T(1,128)S(1)}, f32[2,1,16384]{2,1,0:T(1,128)}, u32[]{:S(2)}) copy-start(f32[2,1,16384]{2,1,0:T(1,128)} %param.7) | copy-start | bytes 393220
  35.0 28.5 %copy-start.3 = (bf16[384,1152]{1,0:T(8,128)(2,1)S(1)}, bf16[384,1152]{1,0:T(8,128)(2,1)}, u32[]{:S(2)}) copy-start(bf16[384,1152]{1,0:T(8,128)(2,1)} %constant.11.clone.refs_12_) | copy-start | bytes 2654212
  35.0 28.5 %copy-start.4 = (bf16[384,1152]{1,0:T(8,128)(2,1)S(1)}, bf16[384,1152]{1,0:T(8,128)(2,1)}, u32[]{:S(2)}) copy-start(bf16[384,1152]{1,0:T(8,128)(2,1)} %constant.8.clone.refs_9_) | copy-start | bytes 2654212
  35.0 28.5 %copy-start.5 = (bf16[1152,256]{1,0:T(8,128)(2,1)S(1)}, bf16[1152,256]{1,0:T(8,128)(2,1)}, u32[]{:S(2)}) copy-start(bf16[1152,256]{1,0:T(8,128)(2,1)} %constant.10.clone.refs_11_) | copy-start | bytes 1769476
  35.0 28.5 %copy-start.6 = (bf16[768,384]{1,0:T(8,128)(2,1)S(1)}, bf16[768,384]{1,0:T(8,128)(2,1)}, u32[]{:S(2)}) copy-start(bf16[768,384]{1,0:T(8,128)(2,1)} %constant.9.clone.refs_10_) | copy-start | bytes 1769476
  40.8 22.7 %collective-permute-start.6 = (f32[1,1152,128]{2,1,0:T(8,128)S(1)}, f32[1,1152,128]{2,1,0:T(8,128)S(1)}, u32[]{:S(2)}, u32[]{:S(2)}) collective-permute-start(f32[1,1152,128]{2,1,0:T(8,128)S(1)} %get-tuple-element.26), channel_id=1, source_target_pairs={{0,4},{4,0},{8,12},{12,8},{16,20},{20,16},{24,28},{28,24},{1,5},{5... | collective-permute-start | bytes 1769480 | tf_op jit(solution)/shard_map/ppermute | solution.py:577
  40.9 7.0 %collective-permute-start.9 = (f32[2,128,128]{2,1,0:T(8,128)S(1)}, f32[2,128,128]{2,1,0:T(8,128)S(1)}, u32[]{:S(2)}, u32[]{:S(2)}) collective-permute-start(f32[2,128,128]{2,1,0:T(8,128)S(1)} %bitcast.32), channel_id=1, source_target_pairs={{0,3},{1,0},{2,1},{3,2},{4,7},{5,4},{6,5},{7,6},{8,11},{9,8},{10,9... | collective-permute-start | bytes 393224 | tf_op jit(solution)/shard_map/ppermute | solution.py:555
  47.9 8.8 %collective-permute-start.8 = (f32[2,128,128]{2,1,0:T(8,128)S(1)}, f32[2,128,128]{2,1,0:T(8,128)S(1)}, u32[]{:S(2)}, u32[]{:S(2)}) collective-permute-start(f32[2,128,128]{2,1,0:T(8,128)S(1)} %bitcast.33), channel_id=1, source_target_pairs={{0,2},{1,3},{2,0},{3,1},{4,6},{5,7},{6,4},{7,5},{8,10},{9,11},{10,... | collective-permute-start | bytes 393224 | tf_op jit(solution)/shard_map/ppermute | solution.py:555
  56.7 6.8 %collective-permute-start.7 = (f32[2,128,128]{2,1,0:T(8,128)S(1)}, f32[2,128,128]{2,1,0:T(8,128)S(1)}, u32[]{:S(2)}, u32[]{:S(2)}) collective-permute-start(f32[2,128,128]{2,1,0:T(8,128)S(1)} %bitcast.34), channel_id=1, source_target_pairs={{0,1},{1,2},{2,3},{3,0},{4,5},{5,6},{6,7},{7,4},{8,9},{9,10},{10,1... | collective-permute-start | bytes 393224 | tf_op jit(solution)/shard_map/ppermute | solution.py:555
  89.2 4.6 %collective-permute-start.10 = (f32[4,1152,128]{2,1,0:T(8,128)S(1)}, f32[4,1152,128]{2,1,0:T(8,128)S(1)}, u32[]{:S(2)}, u32[]{:S(2)}) collective-permute-start(f32[4,1152,128]{2,1,0:T(8,128)S(1)} %get-tuple-element.28), channel_id=1, source_target_pairs={{0,4},{4,0},{8,12},{12,8},{16,20},{20,16},{24,28},{28,24},{1,5},{5... | collective-permute-start | bytes 7077896 | tf_op jit(solution)/shard_map/ppermute | solution.py:577
  99.8 21.8 %collective-permute-start.11 = (f32[1,128,256]{2,1,0:T(8,128)S(1)}, f32[1,128,256]{2,1,0:T(8,128)S(1)}, u32[]{:S(2)}, u32[]{:S(2)}) collective-permute-start(f32[1,128,256]{2,1,0:T(8,128)S(1)} %collect_points.5), channel_id=1, source_target_pairs={{0,8},{4,12},{8,0},{12,4},{16,24},{20,28},{24,16},{28,20},{1,9},{5... | collective-permute-start | bytes 393224 | tf_op jit(solution)/shard_map/ppermute | solution.py:577
  107.4 14.2 %collective-permute-start.12 = (f32[1,128,256]{2,1,0:T(8,128)S(1)}, f32[1,128,256]{2,1,0:T(8,128)S(1)}, u32[]{:S(2)}, u32[]{:S(2)}) collective-permute-start(f32[1,128,256]{2,1,0:T(8,128)S(1)} %collect_points.6), channel_id=1, source_target_pairs={{0,16},{4,20},{8,24},{12,28},{16,0},{20,4},{24,8},{28,12},{1,17},{... | collective-permute-start | bytes 393224 | tf_op jit(solution)/shard_map/ppermute | solution.py:577
  114.0 7.6 %collective-permute-start.13 = (f32[1,128,256]{2,1,0:T(8,128)S(1)}, f32[1,128,256]{2,1,0:T(8,128)S(1)}, u32[]{:S(2)}, u32[]{:S(2)}) collective-permute-start(f32[1,128,256]{2,1,0:T(8,128)S(1)} %collect_points.7), channel_id=1, source_target_pairs={{0,24},{4,28},{8,16},{12,20},{16,8},{20,12},{24,0},{28,4},{1,25},{... | collective-permute-start | bytes 393224 | tf_op jit(solution)/shard_map/ppermute | solution.py:577

commit v4 on v3

--- a/solution.py
+++ b/solution.py
@@ -225,21 +225,6 @@
         s, c = 2.0 * s * c, c * c - s * s
 
 
-def rise(wr, wi, j):
-    k = lax.broadcasted_iota(jnp.int32, (8, CHUNK), 0)
-    shape = (8, CHUNK)
-    er = ei = None
-    for bit in range(3):
-        on = (k & (1 << bit)) != 0
-        fr = jnp.where(on, jnp.broadcast_to(wr[bit][j : j + 1], shape), 1.0)
-        fi = jnp.where(on, jnp.broadcast_to(wi[bit][j : j + 1], shape), 0.0)
-        if er is None:
-            er, ei = fr, fi
-        else:
-            er, ei = er * fr - ei * fi, er * fi + ei * fr
-    return er, ei
-
-
 def firsts(planes):
     me = lax.axis_index("grid")
     return (me * planes).astype(F32), ((me ^ 1) * planes).astype(F32)
@@ -253,31 +238,54 @@
     return g, c, code
 
 
-def spread_kernel(planes, height, unroll, slab_ref, steps_ref, own_ref, sib_ref, w_ref, code_ref, id_ref, a_ref):
-    rows = a_ref.shape[0]
-    freq, gb, gc = decode(slab_ref[0, 2 * rows : 3 * rows], planes)
+def row_of(ref, index, c):
+    return jnp.broadcast_to(ref[index, pl.ds(c, 1), :], (8, CHUNK))
+
+
+def rise(w_ref, c):
+    k = lax.broadcasted_iota(jnp.int32, (8, CHUNK), 0)
+    er = ei = None
+    for bit in range(3):
+        on = (k & (1 << bit)) != 0
+        fr = jnp.where(on, row_of(w_ref, 4 + 2 * bit, c), 1.0)
+        fi = jnp.where(on, row_of(w_ref, 5 + 2 * bit, c), 0.0)
+        if er is None:
+            er, ei = fr, fi
+        else:
+            er, ei = er * fr - ei * fi, er * fi + ei * fr
+    return er, ei
+
+
+def prepare(planes, cell, w_ref, code_ref, id_ref):
+    freq, gb, gc = decode(cell, planes)
     code_ref[0] = gb
     code_ref[1] = gc
     id_ref[...] = ident(LANES)
+    for q, first in enumerate(firsts(planes)):
+        w_ref[2 * q], w_ref[2 * q + 1] = phase(freq, first)
+    powers(freq, w_ref)
+
+
+def spread_kernel(planes, height, unroll, slab_ref, steps_ref, own_ref, sib_ref, w_ref, code_ref, id_ref):
+    rows = w_ref.shape[1]
+    prepare(planes, slab_ref[0, 2 * rows : 3 * rows], w_ref, code_ref, id_ref)
     re, im = slab_ref[0, 0:rows], slab_ref[0, rows : 2 * rows]
-    for q, first in enumerate(firsts(planes)):
-        sr, si = phase(freq, first)
+    for q in range(2):
+        sr, si = w_ref[2 * q], w_ref[2 * q + 1]
         w_ref[2 * q] = re * sr - im * si
         w_ref[2 * q + 1] = re * si + im * sr
-    powers(freq, w_ref)
-    shape = (8, CHUNK)
-
-    def build(i, carry):
-        part = pl.ds(pl.multiple_of(i * 8, 8), 8)
-        w = [w_ref[q, part, :] for q in range(12)]
-        for j in range(8):
-            er, ei = rise(w[4:10:2], w[5:10:2], j)
-            jr = jnp.broadcast_to(w[10][j : j + 1], shape)
-            ji = jnp.broadcast_to(w[11][j : j + 1], shape)
+    own_ref[...] = jnp.zeros_like(own_ref)
+    sib_ref[...] = jnp.zeros_like(sib_ref)
+
+    def visit(i, carry):
+        ids = id_ref[...]
+        for j in range(unroll):
+            g, c, code = pair_code(planes, steps_ref, code_ref, rows, i * unroll + j)
+            er, ei = rise(w_ref, c)
+            jr, ji = row_of(w_ref, 10, c), row_of(w_ref, 11, c)
             lines = []
             for q in range(2):
-                zr = jnp.broadcast_to(w[2 * q][j : j + 1], shape)
-                zi = jnp.broadcast_to(w[2 * q + 1][j : j + 1], shape)
+                zr, zi = row_of(w_ref, 2 * q, c), row_of(w_ref, 2 * q + 1, c)
                 zr, zi = er * zr - ei * zi, er * zi + ei * zr
                 real, imag = [zr], [zi]
                 for _ in range(height // 8 - 1):
@@ -286,18 +294,9 @@
                     imag.append(zi)
                 lines += real + imag
             high, low = split(jnp.concatenate(lines, axis=0))
-            a_ref[i * 8 + j] = jnp.concatenate([high, low], axis=0)
-        return carry
-
-    lax.fori_loop(0, rows // 8, build, 0)
-    own_ref[...] = jnp.zeros_like(own_ref)
-    sib_ref[...] = jnp.zeros_like(sib_ref)
-
-    def visit(i, carry):
-        ids = id_ref[...]
-        for j in range(unroll):
-            g, c, code = pair_code(planes, steps_ref, code_ref, rows, i * unroll + j)
-            got = lax.dot_general(a_ref[c], one_hot(code, ids), NT, preferred_element_type=F32)
+            got = lax.dot_general(
+                jnp.concatenate([high, low], axis=0), one_hot(code, ids), NT, preferred_element_type=F32
+            )
             got = got[: 4 * height] + got[4 * height :]
             where = pl.ds(pl.multiple_of(g * (2 * height), 8), 2 * height)
             own_ref[0, where, :] += got[: 2 * height]
@@ -308,43 +307,26 @@
 
 
 def collect_kernel(
-    planes, height, unroll, slab_ref, steps_ref, own_ref, sib_ref, h_ref, w_ref, code_ref, id_ref, u2_ref, g_ref
+    planes, height, unroll, slab_ref, steps_ref, own_ref, sib_ref, h_ref, w_ref, code_ref, id_ref, u2_ref
 ):
-    rows = g_ref.shape[0]
-    freq, gb, gc = decode(slab_ref[0, 2 * rows : 3 * rows], planes)
-    code_ref[0] = gb
-    code_ref[1] = gc
-    id_ref[...] = ident(LANES)
-    for q, first in enumerate(firsts(planes)):
-        w_ref[2 * q], w_ref[2 * q + 1] = phase(freq, first)
-    powers(freq, w_ref)
+    rows = w_ref.shape[1]
+    prepare(planes, slab_ref[0, 2 * rows : 3 * rows], w_ref, code_ref, id_ref)
     for g in range(planes):
         where = slice(g * 2 * height, (g + 1) * 2 * height)
         high, low = split(jnp.concatenate([own_ref[0, where, :], sib_ref[0, where, :]], axis=0))
         u2_ref[g] = jnp.concatenate([high, low], axis=0)
-    g_ref[...] = jnp.zeros_like(g_ref)
+    h_ref[...] = jnp.zeros_like(h_ref)
 
     def visit(i, carry):
         ids = id_ref[...]
         for j in range(unroll):
             g, c, code = pair_code(planes, steps_ref, code_ref, rows, i * unroll + j)
             got = mm(u2_ref[g], one_hot(code, ids))
-            g_ref[c] += got[: 4 * height] + got[4 * height :]
-        return carry
-
-    lax.fori_loop(0, -(-(rows + planes - 1) // unroll), visit, 0)
-    shape = (8, CHUNK)
-
-    def finish(i, carry):
-        part = pl.ds(pl.multiple_of(i * 8, 8), 8)
-        w = [w_ref[q, part, :] for q in range(12)]
-        real, imag = [], []
-        for j in range(8):
-            jr = jnp.broadcast_to(w[10][j : j + 1], shape)
-            ji = jnp.broadcast_to(w[11][j : j + 1], shape)
+            got = got[: 4 * height] + got[4 * height :]
+            jr, ji = row_of(w_ref, 10, c), row_of(w_ref, 11, c)
             hr = hi = 0.0
             for q in range(2):
-                value = g_ref[i * 8 + j, q * 2 * height : (q + 1) * 2 * height]
+                value = got[q * 2 * height : (q + 1) * 2 * height]
                 ar = value[height - 8 : height]
                 ai = value[2 * height - 8 : 2 * height]
                 for t in range(height // 8 - 2, -1, -1):
@@ -352,17 +334,14 @@
                         ar * jr + ai * ji + value[8 * t : 8 * t + 8],
                         ai * jr - ar * ji + value[height + 8 * t : height + 8 * t + 8],
                     )
-                zr = jnp.broadcast_to(w[2 * q][j : j + 1], shape)
-                zi = jnp.broadcast_to(w[2 * q + 1][j : j + 1], shape)
+                zr, zi = row_of(w_ref, 2 * q, c), row_of(w_ref, 2 * q + 1, c)
                 hr, hi = hr + ar * zr + ai * zi, hi + ai * zr - ar * zi
-            er, ei = rise(w[4:10:2], w[5:10:2], j)
-            real.append(jnp.sum(hr * er + hi * ei, axis=0, keepdims=True))
-            imag.append(jnp.sum(hi * er - hr * ei, axis=0, keepdims=True))
-        h_ref[0, part, :] = jnp.concatenate(real, axis=0)
-        h_ref[0, pl.ds(pl.multiple_of(rows + i * 8, 8), 8), :] = jnp.concatenate(imag, axis=0)
+            er, ei = rise(w_ref, c)
+            h_ref[0, pl.ds(c, 1), :] += jnp.sum(hr * er + hi * ei, axis=0, keepdims=True)
+            h_ref[0, pl.ds(rows + c, 1), :] += jnp.sum(hi * er - hr * ei, axis=0, keepdims=True)
         return carry
 
-    lax.fori_loop(0, rows // 8, finish, 0)
+    lax.fori_loop(0, -(-(rows + planes - 1) // unroll), visit, 0)
 
 
 def potential_kernel(group, height, planes, calls, *refs):
@@ -545,14 +524,11 @@
     count = coefficients.shape[2]
     rows = count // CHUNK
     height = -(-planes // 8) * 8
-    group = 4 if planes % 4 == 0 else 1
+    group = 8 if planes % 8 == 0 else 1
     unroll = 22
     me = lax.axis_index("grid")
     half = slabs // 2
     coef = coefficients.reshape(2, 2 * rows, LANES)
-    coefs = [coef]
-    for shift in range(1, bands):
-        coefs.append(lax.ppermute(coef, "band", [(i, (i + shift) % bands) for i in range(bands)]))
     table_rows = 3 * rows + 8
     sorted_pts, dest = pl.pallas_call(
         functools.partial(sort_kernel, planes),
@@ -594,7 +570,7 @@
         in_specs=[slab_spec, steps_spec],
         out_specs=(block_spec, block_spec),
         out_shape=(jax.ShapeDtypeStruct((per_call, lines, LANES), F32),) * 2,
-        scratch_shapes=point_scratch + [pltpu.VMEM((rows, 8 * height, CHUNK), BF)],
+        scratch_shapes=point_scratch,
         compiler_params=params(20),
         cost_estimate=cost(8e9),
         name="spread_points",
@@ -607,6 +583,10 @@
     cells = potential if height == planes else jnp.pad(potential, ((0, height - planes), (0, 0)))
     cells = cells.reshape(height // 8, 8, N * N // LANES, LANES).transpose(0, 2, 1, 3)
     cells = cells.reshape(height // 8, N * N // 16, LANES)
+    *sib, mine = lax.optimization_barrier((*sib, coef))
+    coefs = [coef]
+    for shift in range(1, bands):
+        coefs.append(lax.ppermute(mine, "band", [(i, (i + shift) % bands) for i in range(bands)]))
     constants = [jnp.asarray(t) for t in tables()]
     anywhere = pl.BlockSpec(memory_space=pl.ANY)
     keep, send = pl.pallas_call(
@@ -614,8 +594,7 @@
         grid=(planes // group,),
         in_specs=[anywhere] * (2 * calls)
         + [pl.BlockSpec((1, N * N // 16, LANES), lambda i: (i * group // 8, 0, 0))]
-        + [whole(t.shape) for t in constants]
-        + [anywhere] * (bands - 1),
+        + [whole(t.shape) for t in constants],
         out_specs=(anywhere, anywhere),
         out_shape=(jax.ShapeDtypeStruct((half, lines, LANES), F32),) * 2,
         scratch_shapes=[
@@ -626,7 +605,8 @@
         compiler_params=params(40),
         cost_estimate=cost(4e10),
         name="apply_potential",
-    )(*own, *sib, cells, *constants, *coefs[1:])
+    )(*own, *sib, cells, *constants)
+    send, *coefs = lax.optimization_barrier((send, *coefs))
     other = swap(send, 1)
     partial = []
     for call, table in enumerate(points):
@@ -638,11 +618,7 @@
                 in_specs=[slab_spec, steps_spec, set_spec, set_spec],
                 out_specs=pl.BlockSpec((1, 2 * rows, CHUNK), lambda s: (s, 0, 0)),
                 out_shape=jax.ShapeDtypeStruct((per_call, 2 * rows, CHUNK), F32),
-                scratch_shapes=point_scratch
-                + [
-                    pltpu.VMEM((planes, 8 * height, LANES), BF),
-                    pltpu.VMEM((rows, 4 * height, CHUNK), F32),
-                ],
+                scratch_shapes=point_scratch + [pltpu.VMEM((planes, 8 * height, LANES), BF)],
                 compiler_params=params(24),
                 cost_estimate=cost(8e9),
                 name="collect_points",

time: 134 us -> 106 us (0.79)
  waiting for transfers between devices: 25.2 us -> 10.8 us
  Pallas kernels: 84.2 us -> 71.4 us
    ppermute x3, waiting for transfers between devices: 17.4 us -> 0.01 us  [local(): lax.ppermute(mine, 'band', [(i, (i + shift) % bands) for i in range(bands)])]
    pallas_call x4, Pallas kernels: 24.1 us -> 17.1 us  [local(): pl.pallas_call(functools.partial(collect_kernel, planes, height, unroll),...]
    pallas_call x4, Pallas kernels: 23.1 us -> 19.2 us  [local(): mine, theirs = spread(table, table)]
    ppermute x11, waiting for transfers between devices: 7.8 us -> 10.8 us  [swap(): return lax.ppermute(x, 'grid', [(i, i ^ bits) for i in range(slabs)])]
    pallas_call x1, Pallas kernels: 25.7 us -> 23.9 us  [local(): pl.pallas_call(functools.partial(potential_kernel, group, height, planes,...]
  transfers between devices with their start and end apart: 14 -> 14, of which waited for: 5 -> 4; matrix products, arithmetic and copies ran while one was open for 0% -> 0% of each run, Pallas kernels for 31% -> 53%
where the time goes in v4:
time: 106 us
  Pallas kernels  71.4 us (67%)
  starting transfers between devices  13.8 us (13%)
  waiting for transfers between devices  10.8 us (10%)
  blocking collectives  7.43 us (7%)
  local copies, waits for them, and re-layouts  1.76 us (2%)
    pallas_call x1, Pallas kernels, local(): pl.pallas_call(functools.partial(potential_kernel, group, height, planes,...  23.9 us
    pallas_call x4, Pallas kernels, local(): mine, theirs = spread(table, table)  19.2 us
    pallas_call x4, Pallas kernels, local(): pl.pallas_call(functools.partial(collect_kernel, planes, height, unroll),...  17.1 us
    ppermute x11, waiting for transfers between devices, swap(): return lax.ppermute(x, 'grid', [(i, i ^ bits) for i in range(slabs)])  10.8 us
    ppermute x11, starting transfers between devices, swap(): return lax.ppermute(x, 'grid', [(i, i ^ bits) for i in range(slabs)])  9.17 us
    all_to_all x1, blocking collectives, local(): sums = lax.all_to_all(part, 'grid', split_axis=0, concat_axis=0, tiled=True)  7.43 us
    pallas_call x1, Pallas kernels, local(): pl.pallas_call(functools.partial(sort_kernel, planes), out_shape=(jax.Sha...  6.63 us
    ppermute x3, starting transfers between devices, local(): lax.ppermute(mine, 'band', [(i, (i + shift) % bands) for i in range(bands)])  4.62 us
  transfers between devices with their start and end apart: 14, of which 4 were waited for; matrix products, arithmetic and copies ran while one was open for 0% of the time, Pallas kernels for 53%

profile of v4, /device:TPU:0, one launch (start us, length us, event | category | flops | bytes accessed | tf_op | source)
XLA Modules:
  0.0 106.0 jit_solution(11402208108323199489)
XLA Ops:
  0.6 0.9 copy-done
  1.5 0.8 copy-done.2
  2.4 6.6 %sort_points.1 = (f32[200,256]{1,0:T(8,128)S(1)}, f32[64,256]{1,0:T(8,128)S(1)}) custom-call(s32[128,128]{1,0:T(8,128)S(1)} %bitcast.37, f32[2,128,128]{2,1,0:T(8,128)S(1)} %bitcast.31), custom_call_target="tpu_custom_call" | custom-call | flops 10000000000 | tf_op jit(solution)/shard_map/sort_points/pallas_call | solution.py:533
  9.0 4.0 %collective-permute-start.2 = (f32[200,256]{1,0:T(8,128)S(1)}, f32[200,256]{1,0:T(8,128)S(1)}, u32[]{:S(2)}, u32[]{:S(2)}) collective-permute-start(f32[200,256]{1,0:T(8,128)S(1)} %get-tuple-element.28), channel_id=1, source_target_pairs={{0,24},{4,28},{8,16},{12,20},{16,8},{20,12},{24,0},{28,4},{1,25},{... | collective-permute-start | bytes 614408 | tf_op jit(solution)/shard_map/ppermute | solution.py:553
  13.6 4.8 %spread_points.4 = (f32[1,1152,128]{2,1,0:T(8,128)S(1)}, f32[1,1152,128]{2,1,0:T(8,128)S(1)}) custom-call(f32[1,200,256]{2,1,0:T(8,128)S(1)} %bitcast.15, f32[1,200,256]{2,1,0:T(8,128)S(1)} %bitcast.16), custom_call_target="tpu_custom_call" | custom-call | flops 8000000000 | tf_op jit(solution)/shard_map/spread_points/pallas_call | solution.py:580
  18.5 4.2 %collective-permute-done = f32[200,256]{1,0:T(8,128)S(1)} collective-permute-done((f32[200,256]{1,0:T(8,128)S(1)}, f32[200,256]{1,0:T(8,128)S(1)}, u32[]{:S(2)}, u32[]{:S(2)}) %collective-permute-start) | collective-permute-done | bytes 204832 | tf_op jit(solution)/shard_map/ppermute | solution.py:553
  22.7 4.8 %spread_points.5 = (f32[1,1152,128]{2,1,0:T(8,128)S(1)}, f32[1,1152,128]{2,1,0:T(8,128)S(1)}) custom-call(f32[1,200,256]{2,1,0:T(8,128)S(1)} %bitcast.27, f32[1,200,256]{2,1,0:T(8,128)S(1)} %bitcast.28), custom_call_target="tpu_custom_call" | custom-call | flops 8000000000 | tf_op jit(solution)/shard_map/spread_points/pallas_call | solution.py:580
  27.6 4.8 %spread_points.6 = (f32[1,1152,128]{2,1,0:T(8,128)S(1)}, f32[1,1152,128]{2,1,0:T(8,128)S(1)}) custom-call(f32[1,200,256]{2,1,0:T(8,128)S(1)} %bitcast.23, f32[1,200,256]{2,1,0:T(8,128)S(1)} %bitcast.24), custom_call_target="tpu_custom_call" | custom-call | flops 8000000000 | tf_op jit(solution)/shard_map/spread_points/pallas_call | solution.py:580
  33.0 4.8 %spread_points.7 = (f32[1,1152,128]{2,1,0:T(8,128)S(1)}, f32[1,1152,128]{2,1,0:T(8,128)S(1)}) custom-call(f32[1,200,256]{2,1,0:T(8,128)S(1)} %bitcast.19, f32[1,200,256]{2,1,0:T(8,128)S(1)} %bitcast.20), custom_call_target="tpu_custom_call" | custom-call | flops 8000000000 | tf_op jit(solution)/shard_map/spread_points/pallas_call | solution.py:580
  38.0 1.9 %collective-permute-done.6.refs_7_ = f32[1,1152,128]{2,1,0:T(8,128)S(1)} collective-permute-done((f32[1,1152,128]{2,1,0:T(8,128)S(1)}, f32[1,1152,128]{2,1,0:T(8,128)S(1)}, u32[]{:S(2)}, u32[]{:S(2)}) %collective-permute-start.6) | collective-permute-done | bytes 589856 | tf_op jit(solution)/shard_map/ppermute | solution.py:553
  39.9 3.6 %collective-permute-start.9 = (f32[2,128,128]{2,1,0:T(8,128)S(1)}, f32[2,128,128]{2,1,0:T(8,128)S(1)}, u32[]{:S(2)}, u32[]{:S(2)}) collective-permute-start(f32[2,128,128]{2,1,0:T(8,128)S(1)} %bitcast.32), channel_id=1, source_target_pairs={{0,3},{1,0},{2,1},{3,2},{4,7},{5,4},{6,5},{7,6},{8,11},{9,8},{10,9... | collective-permute-start | bytes 393224 | tf_op jit(solution)/shard_map/ppermute | solution.py:589
  43.5 1.0 collective-permute-start.7
  44.5 23.9 %apply_potential.1 = (f32[4,1152,128]{2,1,0:T(8,128)S(1)}, f32[4,1152,128]{2,1,0:T(8,128)S(1)}) custom-call(f32[1,1152,128]{2,1,0:T(8,128)S(1)} %get-tuple-element.29.refs_0_, f32[1,1152,128]{2,1,0:T(8,128)S(1)} %get-tuple-element.30.refs_1_, f32[1,1152,128]{2,1,0:T(8,128)S(1)} %get-tuple-element.31.refs_2_, f32[1,1152,128]{2,1,0:T(8,128)S(1)} %get-tuple-element.32.refs_3_, ...), custom_call_target="tpu_custom_call" | custom-call | flops 40000000000 | tf_op jit(solution)/shard_map/apply_potential/pallas_call | solution.py:592
  68.5 4.5 %collective-permute-done.10.sib_ref = f32[4,1152,128]{2,1,0:T(8,128)S(1)} collective-permute-done((f32[4,1152,128]{2,1,0:T(8,128)S(1)}, f32[4,1152,128]{2,1,0:T(8,128)S(1)}, u32[]{:S(2)}, u32[]{:S(2)}) %collective-permute-start.10) | collective-permute-done | bytes 2359328 | tf_op jit(solution)/shard_map/ppermute | solution.py:553
  73.0 4.3 %collect_points.5 = f32[1,128,256]{2,1,0:T(8,128)S(1)} custom-call(f32[1,200,256]{2,1,0:T(8,128)S(1)} %bitcast.29, f32[1,200,256]{2,1,0:T(8,128)S(1)} %bitcast.30, f32[4,1152,128]{2,1,0:T(8,128)S(1)} %get-tuple-element.41.own_ref, f32[4,1152,128]{2,1,0:T(8,128)S(1)} %collective-permute-done.10.sib_ref), custom_call_target="tpu_custom_call" | custom-call | flops 8000000000 | tf_op jit(solution)/shard_map/collect_points/pallas_call | solution.py:615
  77.3 1.6 %collective-permute-start.11 = (f32[1,128,256]{2,1,0:T(8,128)S(1)}, f32[1,128,256]{2,1,0:T(8,128)S(1)}, u32[]{:S(2)}, u32[]{:S(2)}) collective-permute-start(f32[1,128,256]{2,1,0:T(8,128)S(1)} %collect_points.5), channel_id=1, source_target_pairs={{0,8},{4,12},{8,0},{12,4},{16,24},{20,28},{24,16},{28,20},{1,9},{5... | collective-permute-start | bytes 393224 | tf_op jit(solution)/shard_map/ppermute | solution.py:553
  78.9 4.3 %collect_points.6 = f32[1,128,256]{2,1,0:T(8,128)S(1)} custom-call(f32[1,200,256]{2,1,0:T(8,128)S(1)} %bitcast.25, f32[1,200,256]{2,1,0:T(8,128)S(1)} %bitcast.26, f32[4,1152,128]{2,1,0:T(8,128)S(1)} %get-tuple-element.41.own_ref, f32[4,1152,128]{2,1,0:T(8,128)S(1)} %collective-permute-done.10.sib_ref), custom_call_target="tpu_custom_call" | custom-call | flops 8000000000 | tf_op jit(solution)/shard_map/collect_points/pallas_call | solution.py:615
  83.1 0.6 collective-permute-start.12
  83.7 4.3 %collect_points.7 = f32[1,128,256]{2,1,0:T(8,128)S(1)} custom-call(f32[1,200,256]{2,1,0:T(8,128)S(1)} %bitcast.21, f32[1,200,256]{2,1,0:T(8,128)S(1)} %bitcast.22, f32[4,1152,128]{2,1,0:T(8,128)S(1)} %get-tuple-element.41.own_ref, f32[4,1152,128]{2,1,0:T(8,128)S(1)} %collective-permute-done.10.sib_ref), custom_call_target="tpu_custom_call" | custom-call | flops 8000000000 | tf_op jit(solution)/shard_map/collect_points/pallas_call | solution.py:615
  88.0 1.5 %collective-permute-start.13 = (f32[1,128,256]{2,1,0:T(8,128)S(1)}, f32[1,128,256]{2,1,0:T(8,128)S(1)}, u32[]{:S(2)}, u32[]{:S(2)}) collective-permute-start(f32[1,128,256]{2,1,0:T(8,128)S(1)} %collect_points.7), channel_id=1, source_target_pairs={{0,24},{4,28},{8,16},{12,20},{16,8},{20,12},{24,0},{28,4},{1,25},{... | collective-permute-start | bytes 393224 | tf_op jit(solution)/shard_map/ppermute | solution.py:553
  89.5 4.3 %collect_points.4.refs_0_ = f32[1,128,256]{2,1,0:T(8,128)S(1)} custom-call(f32[1,200,256]{2,1,0:T(8,128)S(1)} %bitcast.17, f32[1,200,256]{2,1,0:T(8,128)S(1)} %bitcast.18, f32[4,1152,128]{2,1,0:T(8,128)S(1)} %get-tuple-element.41.own_ref, f32[4,1152,128]{2,1,0:T(8,128)S(1)} %collective-permute-done.10.sib_ref), custom_call_target="tpu_custom_call" | custom-call | flops 8000000000 | tf_op jit(solution)/shard_map/collect_points/pallas_call | solution.py:615
  93.9 3.8 %unsort_points.1 = (f32[2,128,128]{2,1,0:T(8,128)S(1)}, f32[8,8,128]{2,1,0:T(8,128)S(1)}) custom-call(f32[1,128,256]{2,1,0:T(8,128)S(1)} %collect_points.4.refs_0_, f32[1,128,256]{2,1,0:T(8,128)S(1)} %collective-permute-done.11.refs_1_, f32[1,128,256]{2,1,0:T(8,128)S(1)} %collective-permute-done.12.refs_2_, ...), custom_call_target="tpu_custom_call" | custom-call | flops 6000000000 | tf_op jit(solution)/shard_map/unsort_points/pallas_call | solution.py:634
  97.8 7.4 %all_to_all.5.sum_ref = f32[8,8,128]{2,1,0:T(8,128)S(1)} all-to-all(f32[8,8,128]{2,1,0:T(8,128)S(1)} %get-tuple-element.50), channel_id=1, replica_groups=mesh['grid'=8,'band'=4] {'grid'}, dimensions={0} | all-to-all | bytes 65536 | tf_op jit(solution)/shard_map/all_to_all | solution.py:645
  105.2 0.8 residual.1
  (31 shorter events, 1.7 us)
Async XLA Ops:
  0.6 0.9 copy-start
  1.5 0.8 copy-start.2
  9.0 24.0 %collective-permute-start.2 = (f32[200,256]{1,0:T(8,128)S(1)}, f32[200,256]{1,0:T(8,128)S(1)}, u32[]{:S(2)}, u32[]{:S(2)}) collective-permute-start(f32[200,256]{1,0:T(8,128)S(1)} %get-tuple-element.28), channel_id=1, source_target_pairs={{0,24},{4,28},{8,16},{12,20},{16,8},{20,12},{24,0},{28,4},{1,25},{... | collective-permute-start | bytes 614408 | tf_op jit(solution)/shard_map/ppermute | solution.py:553
  13.0 14.6 %collective-permute-start.1 = (f32[200,256]{1,0:T(8,128)S(1)}, f32[200,256]{1,0:T(8,128)S(1)}, u32[]{:S(2)}, u32[]{:S(2)}) collective-permute-start(f32[200,256]{1,0:T(8,128)S(1)} %get-tuple-element.28), channel_id=1, source_target_pairs={{0,16},{4,20},{8,24},{12,28},{16,0},{20,4},{24,8},{28,12},{1,17},{... | collective-permute-start | bytes 614408 | tf_op jit(solution)/shard_map/ppermute | solution.py:553
  13.5 9.3 %collective-permute-start = (f32[200,256]{1,0:T(8,128)S(1)}, f32[200,256]{1,0:T(8,128)S(1)}, u32[]{:S(2)}, u32[]{:S(2)}) collective-permute-start(f32[200,256]{1,0:T(8,128)S(1)} %get-tuple-element.28), channel_id=1, source_target_pairs={{0,8},{4,12},{8,0},{12,4},{16,24},{20,28},{24,16},{28,20},{1,9},{5... | collective-permute-start | bytes 614408 | tf_op jit(solution)/shard_map/ppermute | solution.py:553
  18.4 19.5 %collective-permute-start.3 = (f32[1,1152,128]{2,1,0:T(8,128)S(1)}, f32[1,1152,128]{2,1,0:T(8,128)S(1)}, u32[]{:S(2)}, u32[]{:S(2)}) collective-permute-start(f32[1,1152,128]{2,1,0:T(8,128)S(1)} %get-tuple-element.33), channel_id=1, source_target_pairs={{0,4},{4,0},{8,12},{12,8},{16,20},{20,16},{24,28},{28,24},{1,5},{5... | collective-permute-start | bytes 1769480 | tf_op jit(solution)/shard_map/ppermute | solution.py:553
  27.5 10.4 %collective-permute-start.4 = (f32[1,1152,128]{2,1,0:T(8,128)S(1)}, f32[1,1152,128]{2,1,0:T(8,128)S(1)}, u32[]{:S(2)}, u32[]{:S(2)}) collective-permute-start(f32[1,1152,128]{2,1,0:T(8,128)S(1)} %get-tuple-element.34), channel_id=1, source_target_pairs={{0,4},{4,0},{8,12},{12,8},{16,20},{20,16},{24,28},{28,24},{1,5},{5... | collective-permute-start | bytes 1769480 | tf_op jit(solution)/shard_map/ppermute | solution.py:553
  32.4 5.5 %collective-permute-start.5 = (f32[1,1152,128]{2,1,0:T(8,128)S(1)}, f32[1,1152,128]{2,1,0:T(8,128)S(1)}, u32[]{:S(2)}, u32[]{:S(2)}) collective-permute-start(f32[1,1152,128]{2,1,0:T(8,128)S(1)} %get-tuple-element.35), channel_id=1, source_target_pairs={{0,4},{4,0},{8,12},{12,8},{16,20},{20,16},{24,28},{28,24},{1,5},{5... | collective-permute-start | bytes 1769480 | tf_op jit(solution)/shard_map/ppermute | solution.py:553
  33.0 6.9 %copy-start.1 = (f32[2,1,16384]{2,1,0:T(1,128)S(1)}, f32[2,1,16384]{2,1,0:T(1,128)}, u32[]{:S(2)}) copy-start(f32[2,1,16384]{2,1,0:T(1,128)} %param.7) | copy-start | bytes 393220
  33.0 11.5 %copy-start.3 = (bf16[384,1152]{1,0:T(8,128)(2,1)S(1)}, bf16[384,1152]{1,0:T(8,128)(2,1)}, u32[]{:S(2)}) copy-start(bf16[384,1152]{1,0:T(8,128)(2,1)} %constant.11.clone.refs_12_) | copy-start | bytes 2654212
  33.0 11.5 %copy-start.4 = (bf16[384,1152]{1,0:T(8,128)(2,1)S(1)}, bf16[384,1152]{1,0:T(8,128)(2,1)}, u32[]{:S(2)}) copy-start(bf16[384,1152]{1,0:T(8,128)(2,1)} %constant.8.clone.refs_9_) | copy-start | bytes 2654212
  33.0 11.5 %copy-start.5 = (bf16[1152,256]{1,0:T(8,128)(2,1)S(1)}, bf16[1152,256]{1,0:T(8,128)(2,1)}, u32[]{:S(2)}) copy-start(bf16[1152,256]{1,0:T(8,128)(2,1)} %constant.10.clone.refs_11_) | copy-start | bytes 1769476
  33.0 11.5 %copy-start.6 = (bf16[768,384]{1,0:T(8,128)(2,1)S(1)}, bf16[768,384]{1,0:T(8,128)(2,1)}, u32[]{:S(2)}) copy-start(bf16[768,384]{1,0:T(8,128)(2,1)} %constant.9.clone.refs_10_) | copy-start | bytes 1769476
  37.8 2.1 %collective-permute-start.6 = (f32[1,1152,128]{2,1,0:T(8,128)S(1)}, f32[1,1152,128]{2,1,0:T(8,128)S(1)}, u32[]{:S(2)}, u32[]{:S(2)}) collective-permute-start(f32[1,1152,128]{2,1,0:T(8,128)S(1)} %get-tuple-element.36), channel_id=1, source_target_pairs={{0,4},{4,0},{8,12},{12,8},{16,20},{20,16},{24,28},{28,24},{1,5},{5... | collective-permute-start | bytes 1769480 | tf_op jit(solution)/shard_map/ppermute | solution.py:553
  39.9 28.5 %collective-permute-start.9 = (f32[2,128,128]{2,1,0:T(8,128)S(1)}, f32[2,128,128]{2,1,0:T(8,128)S(1)}, u32[]{:S(2)}, u32[]{:S(2)}) collective-permute-start(f32[2,128,128]{2,1,0:T(8,128)S(1)} %bitcast.32), channel_id=1, source_target_pairs={{0,3},{1,0},{2,1},{3,2},{4,7},{5,4},{6,5},{7,6},{8,11},{9,8},{10,9... | collective-permute-start | bytes 393224 | tf_op jit(solution)/shard_map/ppermute | solution.py:589
  43.5 24.9 %collective-permute-start.8 = (f32[2,128,128]{2,1,0:T(8,128)S(1)}, f32[2,128,128]{2,1,0:T(8,128)S(1)}, u32[]{:S(2)}, u32[]{:S(2)}) collective-permute-start(f32[2,128,128]{2,1,0:T(8,128)S(1)} %bitcast.33), channel_id=1, source_target_pairs={{0,2},{1,3},{2,0},{3,1},{4,6},{5,7},{6,4},{7,5},{8,10},{9,11},{10,... | collective-permute-start | bytes 393224 | tf_op jit(solution)/shard_map/ppermute | solution.py:589
  43.5 24.9 %collective-permute-start.7 = (f32[2,128,128]{2,1,0:T(8,128)S(1)}, f32[2,128,128]{2,1,0:T(8,128)S(1)}, u32[]{:S(2)}, u32[]{:S(2)}) collective-permute-start(f32[2,128,128]{2,1,0:T(8,128)S(1)} %bitcast.34), channel_id=1, source_target_pairs={{0,1},{1,2},{2,3},{3,0},{4,5},{5,6},{6,7},{7,4},{8,9},{9,10},{10,1... | collective-permute-start | bytes 393224 | tf_op jit(solution)/shard_map/ppermute | solution.py:589
  68.4 4.6 %collective-permute-start.10 = (f32[4,1152,128]{2,1,0:T(8,128)S(1)}, f32[4,1152,128]{2,1,0:T(8,128)S(1)}, u32[]{:S(2)}, u32[]{:S(2)}) collective-permute-start(f32[4,1152,128]{2,1,0:T(8,128)S(1)} %get-tuple-element.44), channel_id=1, source_target_pairs={{0,4},{4,0},{8,12},{12,8},{16,20},{20,16},{24,28},{28,24},{1,5},{5... | collective-permute-start | bytes 7077896 | tf_op jit(solution)/shard_map/ppermute | solution.py:553
  77.3 16.5 %collective-permute-start.11 = (f32[1,128,256]{2,1,0:T(8,128)S(1)}, f32[1,128,256]{2,1,0:T(8,128)S(1)}, u32[]{:S(2)}, u32[]{:S(2)}) collective-permute-start(f32[1,128,256]{2,1,0:T(8,128)S(1)} %collect_points.5), channel_id=1, source_target_pairs={{0,8},{4,12},{8,0},{12,4},{16,24},{20,28},{24,16},{28,20},{1,9},{5... | collective-permute-start | bytes 393224 | tf_op jit(solution)/shard_map/ppermute | solution.py:553
  83.1 10.7 %collective-permute-start.12 = (f32[1,128,256]{2,1,0:T(8,128)S(1)}, f32[1,128,256]{2,1,0:T(8,128)S(1)}, u32[]{:S(2)}, u32[]{:S(2)}) collective-permute-start(f32[1,128,256]{2,1,0:T(8,128)S(1)} %collect_points.6), channel_id=1, source_target_pairs={{0,16},{4,20},{8,24},{12,28},{16,0},{20,4},{24,8},{28,12},{1,17},{... | collective-permute-start | bytes 393224 | tf_op jit(solution)/shard_map/ppermute | solution.py:553
  88.0 5.9 %collective-permute-start.13 = (f32[1,128,256]{2,1,0:T(8,128)S(1)}, f32[1,128,256]{2,1,0:T(8,128)S(1)}, u32[]{:S(2)}, u32[]{:S(2)}) collective-permute-start(f32[1,128,256]{2,1,0:T(8,128)S(1)} %collect_points.7), channel_id=1, source_target_pairs={{0,24},{4,28},{8,16},{12,20},{16,8},{20,12},{24,0},{28,4},{1,25},{... | collective-permute-start | bytes 393224 | tf_op jit(solution)/shard_map/ppermute | solution.py:553

commit v5 on v4

--- a/solution.py
+++ b/solution.py
@@ -94,8 +94,15 @@
     return jnp.floor((x + 0.5) * (1.0 / divisor))
 
 
-def sort_kernel(planes, m_ref, c_ref, out_ref, d_ref, acc_ref, val_ref, gb_ref, cum_ref, tot_ref, lane_ref):
+def sort_kernel(
+    planes, m_hbm, c_hbm, out_ref, d_ref, acc_ref, val_ref, gb_ref, cum_ref, tot_ref, lane_ref, m_ref, c_ref, sems
+):
     rows = gb_ref.shape[0]
+    fetch_m = pltpu.make_async_copy(m_hbm, m_ref, sems.at[0])
+    fetch_c = pltpu.make_async_copy(c_hbm, c_ref, sems.at[1])
+    fetch_m.start()
+    fetch_c.start()
+    fetch_m.wait()
     m = fold(m_ref[...]).astype(F32)
     line = floor_div(m, N)
     gc = m - N * line
@@ -149,6 +156,7 @@
         (jnp.zeros((1, CHUNK), F32), jnp.zeros((rows, CHUNK), F32), jnp.zeros((8, CHUNK), F32)),
     )
     d_ref[...] = place
+    fetch_c.wait()
     re_h, re_l = split(fold(c_ref[0]))
     im_h, im_l = split(fold(c_ref[1]))
     for q, value in enumerate((re_h, re_l, im_h, im_l, ga, gb, gc)):
@@ -344,45 +352,63 @@
     lax.fori_loop(0, -(-(rows + planes - 1) // unroll), visit, 0)
 
 
-def potential_kernel(group, height, planes, calls, *refs):
+def potential_kernel(group, height, planes, calls, parts, *refs):
     own, sib = refs[:calls], refs[calls : 2 * calls]
-    v_ref, bf_ref, cf_ref, ci_ref, bi_ref = refs[2 * calls : 2 * calls + 5]
-    keep_ref, send_ref, t_ref, u_ref, sems = refs[-5:]
+    v_ref, *tables_hbm = refs[2 * calls : 2 * calls + 5]
+    keep_ref = refs[2 * calls + 5]
+    send_refs = refs[2 * calls + 6 : 2 * calls + 6 + len(parts)]
+    t_ref, u_ref, bf_ref, cf_ref, ci_ref, bi_ref, in_sems, out_sems, table_sems = refs[2 * calls + 6 + len(parts) :]
     step = pl.program_id(0)
     me = lax.axis_index("grid")
-    lines = planes * 2 * height
-
-    def place(j, mine):
-        slab = me ^ (2 * j) if mine else me ^ (2 * j + 1)
-        return pl.ds(pl.multiple_of(slab * lines, 8), lines)
-
     half = keep_ref.shape[0]
     per_call = half // calls
-
-    def arrivals(j):
+    tiles = height // 8
+    shape = (N, 2, tiles, 8, LANES)
+    t_tiles, u_tiles = t_ref.reshape(shape), u_ref.reshape(shape)
+    last = planes // group - 1
+
+    def place(j, q):
+        return pl.ds((me ^ (2 * j + q)) * planes, planes)
+
+    def arrivals(t):
         for q, blocks in enumerate((own, sib)):
+            for j in range(half):
+                yield pltpu.make_async_copy(
+                    blocks[j // per_call].at[j % per_call, :, :, t], t_tiles.at[place(j, q), :, t], in_sems.at[t, q, j]
+                )
+
+    def departures(t):
+        for j in range(half):
             yield pltpu.make_async_copy(
-                blocks[j // per_call].at[j % per_call], t_ref.at[place(j, q == 0)], sems.at[q, j]
+                u_tiles.at[place(j, 0), :, t], keep_ref.at[j, :, :, t], out_sems.at[t, 0, j]
             )
-
-    def departures(j):
-        for q, block in enumerate((keep_ref, send_ref)):
-            yield pltpu.make_async_copy(u_ref.at[place(j, q == 0)], block.at[j], sems.at[q, j])
+        for ref, part in zip(send_refs, parts):
+            for i, j in enumerate(part):
+                yield pltpu.make_async_copy(
+                    u_tiles.at[place(j, 1), :, t], ref.at[i, :, :, t], out_sems.at[t, 1, j]
+                )
+
+    def fetches():
+        for q, (source, target) in enumerate(zip(tables_hbm, (bf_ref, cf_ref, ci_ref, bi_ref))):
+            yield pltpu.make_async_copy(source, target, table_sems.at[q])
 
     @pl.when(step == 0)
     def _():
-        for j in range(half):
-            for copy in arrivals(j):
+        for copies in (arrivals(0), fetches(), *(arrivals(t) for t in range(1, tiles))):
+            for copy in copies:
                 copy.start()
-        for j in range(half):
-            for copy in arrivals(j):
+        for copies in (arrivals(0), fetches()):
+            for copy in copies:
                 copy.wait()
-
-    if height > planes:
-
-        @pl.when(step == 0)
-        def _():
+        if height > planes:
             u_ref[...] = jnp.zeros_like(u_ref)
+
+    for t in range(1, tiles):
+
+        @pl.when(step == t * 8 // group)
+        def _(t=t):
+            for copy in arrivals(t):
+                copy.wait()
 
     stride = 2 * height
     real, imag = [], []
@@ -426,13 +452,17 @@
         u_ref[pl.ds(k, N, stride=stride), :] = x[:N, j * LANES : (j + 1) * LANES]
         u_ref[pl.ds(k + height, N, stride=stride), :] = x[N:, j * LANES : (j + 1) * LANES]
 
-    @pl.when(step == pl.num_programs(0) - 1)
+    for t in range(tiles):
+
+        @pl.when(step == min((t + 1) * 8 // group - 1, last))
+        def _(t=t):
+            for copy in departures(t):
+                copy.start()
+
+    @pl.when(step == last)
     def _():
-        for j in range(half):
-            for copy in departures(j):
-                copy.start()
-        for j in range(half):
-            for copy in departures(j):
+        for t in range(tiles):
+            for copy in departures(t):
                 copy.wait()
 
 
@@ -525,13 +555,15 @@
     rows = count // CHUNK
     height = -(-planes // 8) * 8
     group = 8 if planes % 8 == 0 else 1
-    unroll = 22
+    unroll = 44
     me = lax.axis_index("grid")
     half = slabs // 2
+    anywhere = pl.BlockSpec(memory_space=pl.ANY)
     coef = coefficients.reshape(2, 2 * rows, LANES)
     table_rows = 3 * rows + 8
     sorted_pts, dest = pl.pallas_call(
         functools.partial(sort_kernel, planes),
+        in_specs=[pl.BlockSpec(memory_space=pltpu.HBM)] * 2,
         out_shape=(
             jax.ShapeDtypeStruct((table_rows, CHUNK), F32),
             jax.ShapeDtypeStruct((rows, CHUNK), F32),
@@ -543,8 +575,11 @@
             pltpu.VMEM((rows + 16, planes * CHUNK), F32),
             pltpu.VMEM((-(-planes // 16) * 16, CHUNK), F32),
             pltpu.VMEM((-(-planes // 16) * 16, 2 * CHUNK), F32),
+            pltpu.VMEM((2 * rows, LANES), jnp.int32),
+            pltpu.VMEM((2, 2 * rows, LANES), F32),
+            pltpu.SemaphoreType.DMA((2,)),
         ],
-        compiler_params=params(16),
+        compiler_params=params(58),
         cost_estimate=cost(1e10),
         name="sort_points",
     )(index_map.reshape(2 * rows, LANES), coef)
@@ -553,11 +588,11 @@
         return lax.ppermute(x, "grid", [(i, i ^ bits) for i in range(slabs)])
 
     if half <= 4:
-        points = [sorted_pts[None]] + [swap(sorted_pts, 2 * j)[None] for j in range(1, half)]
+        points = [sorted_pts[None]] + [swap(sorted_pts, 2 * j)[None] for j in range(1, min(half, 3))]
     else:
         everything = lax.all_gather(sorted_pts, "grid")
         points = [jnp.take(everything, me ^ (2 * jnp.arange(half)), axis=0)]
-    calls = len(points)
+    calls = half if half <= 4 else 1
     per_call = half // calls
     lines = planes * 2 * height
     slab_spec = pl.BlockSpec((1, table_rows, CHUNK), lambda s: (s, 0, 0))
@@ -576,8 +611,11 @@
         name="spread_points",
     )
     own, sib = [], []
-    for table in points:
-        mine, theirs = spread(table, table)
+    for call in range(calls):
+        mine, theirs = spread(points[call], points[call])
+        if call == 0 and half == 4:
+            sorted_pts, theirs = lax.optimization_barrier((sorted_pts, theirs))
+            points.append(swap(sorted_pts, 6)[None])
         own.append(mine)
         sib.append(swap(theirs, 1))
     cells = potential if height == planes else jnp.pad(potential, ((0, height - planes), (0, 0)))
@@ -588,41 +626,57 @@
     for shift in range(1, bands):
         coefs.append(lax.ppermute(mine, "band", [(i, (i + shift) % bands) for i in range(bands)]))
     constants = [jnp.asarray(t) for t in tables()]
-    anywhere = pl.BlockSpec(memory_space=pl.ANY)
-    keep, send = pl.pallas_call(
-        functools.partial(potential_kernel, group, height, planes, calls),
+    parts = [[1], [0, *range(2, half)]] if 2 <= half <= 4 else [list(range(half))]
+    cube = (planes, 2, height // 8, 8, LANES)
+    keep, *send = pl.pallas_call(
+        functools.partial(potential_kernel, group, height, planes, calls, parts),
         grid=(planes // group,),
         in_specs=[anywhere] * (2 * calls)
         + [pl.BlockSpec((1, N * N // 16, LANES), lambda i: (i * group // 8, 0, 0))]
-        + [whole(t.shape) for t in constants],
-        out_specs=(anywhere, anywhere),
-        out_shape=(jax.ShapeDtypeStruct((half, lines, LANES), F32),) * 2,
+        + [anywhere] * 4,
+        out_specs=[anywhere] * (1 + len(parts)),
+        out_shape=[jax.ShapeDtypeStruct((count_of, *cube), F32) for count_of in (half, *map(len, parts))],
         scratch_shapes=[
             pltpu.VMEM((slabs * lines, LANES), F32),
             pltpu.VMEM((slabs * lines, LANES), F32),
-            pltpu.SemaphoreType.DMA((2, half)),
+            *(pltpu.VMEM(t.shape, BF) for t in constants),
+            pltpu.SemaphoreType.DMA((height // 8, 2, half)),
+            pltpu.SemaphoreType.DMA((height // 8, 2, half)),
+            pltpu.SemaphoreType.DMA((4,)),
         ],
         compiler_params=params(40),
         cost_estimate=cost(4e10),
         name="apply_potential",
-    )(*own, *sib, cells, *constants)
-    send, *coefs = lax.optimization_barrier((send, *coefs))
-    other = swap(send, 1)
+    )(*(x.reshape(per_call, *cube) for x in (*own, *sib)), cells, *constants)
+    tied = lax.optimization_barrier((*send, *coefs))
+    coefs = tied[len(parts) :]
+    keep = keep.reshape(half, lines, LANES)
+    other = []
+    for x in tied[: len(parts)]:
+        if other:
+            other[-1], x = lax.optimization_barrier((other[-1], x))
+        other.append(swap(x, 1))
+    other = [x.reshape(-1, lines, LANES) for x in other]
+
+    def block_at(first):
+        return pl.BlockSpec((1, lines, LANES), lambda s: (first + s, 0, 0))
+
     partial = []
     for call, table in enumerate(points):
-        set_spec = pl.BlockSpec((1, lines, LANES), functools.partial(lambda call, s: (call * per_call + s, 0, 0), call))
+        first = call * per_call
+        number, part = next((i, part) for i, part in enumerate(parts) if first in part)
         partial.append(
             pl.pallas_call(
                 functools.partial(collect_kernel, planes, height, unroll),
                 grid=(per_call,),
-                in_specs=[slab_spec, steps_spec, set_spec, set_spec],
+                in_specs=[slab_spec, steps_spec, block_at(first), block_at(part.index(first))],
                 out_specs=pl.BlockSpec((1, 2 * rows, CHUNK), lambda s: (s, 0, 0)),
                 out_shape=jax.ShapeDtypeStruct((per_call, 2 * rows, CHUNK), F32),
                 scratch_shapes=point_scratch + [pltpu.VMEM((planes, 8 * height, LANES), BF)],
                 compiler_params=params(24),
                 cost_estimate=cost(8e9),
                 name="collect_points",
-            )(table, table, keep, other)
+            )(table, table, keep, other[number])
         )
     if half <= 4:
         arrived = [partial[0]] + [swap(partial[j], 2 * j) for j in range(1, half)]

time: 106 us -> 100 us (0.943)
  waiting for transfers between devices: 10.8 us -> 6.1 us
  local copies, waits for them, and re-layouts: 1.76 us -> 0.03 us
    ppermute x11 -> x12, waiting for transfers between devices: 10.8 us -> 6.1 us  [swap(): return lax.ppermute(x, 'grid', [(i, i ^ bits) for i in range(slabs)])]
    unnamed x14 -> x12, local copies, waits for them, and re-layouts: 1.76 us -> 0.03 us
    ppermute x11 -> x12, starting transfers between devices: 9.17 us -> 9.43 us  [swap(): return lax.ppermute(x, 'grid', [(i, i ^ bits) for i in range(slabs)])]
  transfers between devices with their start and end apart: 14 -> 15, of which waited for: 4 -> 4; matrix products, arithmetic and copies ran while one was open for 0% -> 0% of each run, Pallas kernels for 53% -> 58%
where the time goes in v5:
time: 100 us; the launch traced here: 99.9 us
  Pallas kernels  71.2 us (71%)
  starting transfers between devices  14.3 us (14%)
  blocking collectives  7.43 us (7%)
  waiting for transfers between devices  6.1 us (6%)
    pallas_call x1, Pallas kernels, local(): pl.pallas_call(functools.partial(potential_kernel, group, height, planes,...  23.7 us
    pallas_call x4, Pallas kernels, local(): mine, theirs = spread(points[call], points[call])  18.3 us
    pallas_call x4, Pallas kernels, local(): pl.pallas_call(functools.partial(collect_kernel, planes, height, unroll),...  16.3 us
    ppermute x12, starting transfers between devices, swap(): return lax.ppermute(x, 'grid', [(i, i ^ bits) for i in range(slabs)])  9.43 us
    pallas_call x1, Pallas kernels, local(): pl.pallas_call(functools.partial(sort_kernel, planes), in_specs=[pl.Block...  8.2 us
    all_to_all x1, blocking collectives, local(): sums = lax.all_to_all(part, 'grid', split_axis=0, concat_axis=0, tiled=True)  7.43 us
    ppermute x12, waiting for transfers between devices, swap(): return lax.ppermute(x, 'grid', [(i, i ^ bits) for i in range(slabs)])  6.1 us
    ppermute x3, starting transfers between devices, local(): lax.ppermute(mine, 'band', [(i, (i + shift) % bands) for i in range(bands)])  4.89 us
  transfers between devices with their start and end apart: 15, of which 4 were waited for; matrix products, arithmetic and copies ran while one was open for 0% of the time, Pallas kernels for 58%

profile of v5, /device:TPU:0, one launch (start us, length us, event | category | flops | bytes accessed | tf_op | source)
XLA Modules:
  0.0 99.9 jit_solution(13306271777486431940)
XLA Ops:
  0.6 8.2 %sort_points.1 = (f32[200,256]{1,0:T(8,128)}, f32[64,256]{1,0:T(8,128)}) custom-call(s32[128,128]{1,0:T(8,128)} %bitcast.61, f32[2,128,128]{2,1,0:T(8,128)} %bitcast.46), custom_call_target="tpu_custom_call" | custom-call | flops 10000000000 | tf_op jit(solution)/shard_map/sort_points/pallas_call | solution.py:564
  8.8 3.0 %collective-permute-start.1 = (f32[200,256]{1,0:T(8,128)}, f32[200,256]{1,0:T(8,128)S(1)}, u32[]{:S(2)}, u32[]{:S(2)}) collective-permute-start(f32[200,256]{1,0:T(8,128)} %get-tuple-element.39), channel_id=1, source_target_pairs={{0,16},{4,20},{8,24},{12,28},{16,0},{20,4},{24,8},{28,12},{1,17},{... | collective-permute-start | bytes 614408 | tf_op jit(solution)/shard_map/ppermute | solution.py:588
  11.9 1.5 %collective-permute-start = (f32[200,256]{1,0:T(8,128)}, f32[200,256]{1,0:T(8,128)S(1)}, u32[]{:S(2)}, u32[]{:S(2)}) collective-permute-start(f32[200,256]{1,0:T(8,128)} %get-tuple-element.39), channel_id=1, source_target_pairs={{0,8},{4,12},{8,0},{12,4},{16,24},{20,28},{24,16},{28,20},{1,9},{5... | collective-permute-start | bytes 614408 | tf_op jit(solution)/shard_map/ppermute | solution.py:588
  13.4 4.8 %spread_points.4 = (f32[1,1152,128]{2,1,0:T(8,128)S(1)}, f32[1,1152,128]{2,1,0:T(8,128)S(1)}) custom-call(f32[1,200,256]{2,1,0:T(8,128)} %bitcast.2.slab_ref.steps_ref, f32[1,200,256]{2,1,0:T(8,128)} %bitcast.2.slab_ref.steps_ref), custom_call_target="tpu_custom_call" | custom-call | flops 8000000000 | tf_op jit(solution)/shard_map/spread_points/pallas_call | solution.py:615
  18.6 4.5 %spread_points.5 = (f32[1,1152,128]{2,1,0:T(8,128)S(1)}, f32[1,1152,128]{2,1,0:T(8,128)S(1)}) custom-call(f32[1,200,256]{2,1,0:T(8,128)S(1)} %bitcast.42, f32[1,200,256]{2,1,0:T(8,128)S(1)} %bitcast.43), custom_call_target="tpu_custom_call" | custom-call | flops 8000000000 | tf_op jit(solution)/shard_map/spread_points/pallas_call | solution.py:615
  23.4 4.5 %spread_points.6 = (f32[1,1152,128]{2,1,0:T(8,128)S(1)}, f32[1,1152,128]{2,1,0:T(8,128)S(1)}) custom-call(f32[1,200,256]{2,1,0:T(8,128)S(1)} %bitcast.34, f32[1,200,256]{2,1,0:T(8,128)S(1)} %bitcast.35), custom_call_target="tpu_custom_call" | custom-call | flops 8000000000 | tf_op jit(solution)/shard_map/spread_points/pallas_call | solution.py:615
  27.9 0.4 collective-permute-start.5
  28.3 4.5 %spread_points.7 = (f32[1,1152,128]{2,1,0:T(8,128)S(1)}, f32[1,1152,128]{2,1,0:T(8,128)S(1)}) custom-call(f32[1,200,256]{2,1,0:T(8,128)S(1)} %bitcast.38, f32[1,200,256]{2,1,0:T(8,128)S(1)} %bitcast.39), custom_call_target="tpu_custom_call" | custom-call | flops 8000000000 | tf_op jit(solution)/shard_map/spread_points/pallas_call | solution.py:615
  33.1 1.8 %collective-permute-done.6 = f32[1,1152,128]{2,1,0:T(8,128)S(1)} collective-permute-done((f32[1,1152,128]{2,1,0:T(8,128)S(1)}, f32[1,1152,128]{2,1,0:T(8,128)S(1)}, u32[]{:S(2)}, u32[]{:S(2)}) %collective-permute-start.6) | collective-permute-done | bytes 589856 | tf_op jit(solution)/shard_map/ppermute | solution.py:588
  34.9 3.9 %collective-permute-start.9 = (f32[2,128,128]{2,1,0:T(8,128)S(1)}, f32[2,128,128]{2,1,0:T(8,128)S(1)}, u32[]{:S(2)}, u32[]{:S(2)}) collective-permute-start(f32[2,128,128]{2,1,0:T(8,128)S(1)} %bitcast.47), channel_id=1, source_target_pairs={{0,3},{1,0},{2,1},{3,2},{4,7},{5,4},{6,5},{7,6},{8,11},{9,8},{10,9... | collective-permute-start | bytes 393224 | tf_op jit(solution)/shard_map/ppermute | solution.py:627
  38.8 1.0 %collective-permute-start.7 = (f32[2,128,128]{2,1,0:T(8,128)S(1)}, f32[2,128,128]{2,1,0:T(8,128)S(1)}, u32[]{:S(2)}, u32[]{:S(2)}) collective-permute-start(f32[2,128,128]{2,1,0:T(8,128)S(1)} %bitcast.49), channel_id=1, source_target_pairs={{0,1},{1,2},{2,3},{3,0},{4,5},{5,6},{6,7},{7,4},{8,9},{9,10},{10,1... | collective-permute-start | bytes 393224 | tf_op jit(solution)/shard_map/ppermute | solution.py:627
  39.8 23.7 %apply_potential.1 = (f32[4,24,2,3,8,128]{5,4,3,2,1,0:T(8,128)S(1)}, f32[1,24,2,3,8,128]{5,4,3,2,1,0:T(8,128)S(1)}, f32[3,24,2,3,8,128]{5,4,3,2,1,0:T(8,128)S(1)}) custom-call(f32[1,24,2,3,8,128]{5,4,3,2,1,0:T(8,128)S(1)} %bitcast.56, f32[1,24,2,3,8,128]{5,4,3,2,1,0:T(8,128)S(1)} %bitcast.57, f32[1,24,2,3,8,128]{5,4,3,2,1,0:T(8,128)S(1)} %bitcast.58, ...), custom_call_target="tpu_custom_call" | custom-call | flops 40000000000 | tf_op jit(solution)/shard_map/apply_potential/pallas_call | solution.py:631
  63.6 2.0 %collective-permute-done.10 = f32[1,24,2,3,8,128]{5,4,3,2,1,0:T(8,128)S(1)} collective-permute-done((f32[1,24,2,3,8,128]{5,4,3,2,1,0:T(8,128)S(1)}, f32[1,24,2,3,8,128]{5,4,3,2,1,0:T(8,128)S(1)}, u32[]{:S(2)}, u32[]{:S(2)}) %collective-permute-start.10) | collective-permute-done | bytes 589856 | tf_op jit(solution)/shard_map/ppermute | solution.py:588
  65.8 4.0 %collect_points.5 = f32[1,128,256]{2,1,0:T(8,128)S(1)} custom-call(f32[1,200,256]{2,1,0:T(8,128)S(1)} %bitcast.44, f32[1,200,256]{2,1,0:T(8,128)S(1)} %bitcast.45, f32[4,1152,128]{2,1,0:T(8,128)S(1)} %bitcast.52, f32[1,1152,128]{2,1,0:T(8,128)S(1)} %bitcast.33), custom_call_target="tpu_custom_call" | custom-call | flops 8000000000 | tf_op jit(solution)/shard_map/collect_points/pallas_call | solution.py:669
  69.7 1.5 %collective-permute-start.12 = (f32[1,128,256]{2,1,0:T(8,128)S(1)}, f32[1,128,256]{2,1,0:T(8,128)S(1)}, u32[]{:S(2)}, u32[]{:S(2)}) collective-permute-start(f32[1,128,256]{2,1,0:T(8,128)S(1)} %collect_points.5), channel_id=1, source_target_pairs={{0,8},{4,12},{8,0},{12,4},{16,24},{20,28},{24,16},{28,20},{1,9},{5... | collective-permute-start | bytes 393224 | tf_op jit(solution)/shard_map/ppermute | solution.py:588
  71.3 4.0 %collect_points.7 = f32[1,128,256]{2,1,0:T(8,128)S(1)} custom-call(f32[1,200,256]{2,1,0:T(8,128)S(1)} %bitcast.40, f32[1,200,256]{2,1,0:T(8,128)S(1)} %bitcast.41, f32[4,1152,128]{2,1,0:T(8,128)S(1)} %bitcast.53, f32[3,1152,128]{2,1,0:T(8,128)S(1)} %bitcast.26), custom_call_target="tpu_custom_call" | custom-call | flops 8000000000 | tf_op jit(solution)/shard_map/collect_points/pallas_call | solution.py:669
  75.2 4.2 %collect_points.6 = f32[1,128,256]{2,1,0:T(8,128)S(1)} custom-call(f32[1,200,256]{2,1,0:T(8,128)S(1)} %bitcast.36, f32[1,200,256]{2,1,0:T(8,128)S(1)} %bitcast.37, f32[4,1152,128]{2,1,0:T(8,128)S(1)} %bitcast.54, f32[3,1152,128]{2,1,0:T(8,128)S(1)} %bitcast.27), custom_call_target="tpu_custom_call" | custom-call | flops 8000000000 | tf_op jit(solution)/shard_map/collect_points/pallas_call | solution.py:669
  79.4 1.6 %collective-permute-start.13 = (f32[1,128,256]{2,1,0:T(8,128)S(1)}, f32[1,128,256]{2,1,0:T(8,128)S(1)}, u32[]{:S(2)}, u32[]{:S(2)}) collective-permute-start(f32[1,128,256]{2,1,0:T(8,128)S(1)} %collect_points.6), channel_id=1, source_target_pairs={{0,16},{4,20},{8,24},{12,28},{16,0},{20,4},{24,8},{28,12},{1,17},{... | collective-permute-start | bytes 393224 | tf_op jit(solution)/shard_map/ppermute | solution.py:588
  81.0 0.5 collective-permute-start.14
  81.5 4.2 %collect_points.4.refs_0_ = f32[1,128,256]{2,1,0:T(8,128)S(1)} custom-call(f32[1,200,256]{2,1,0:T(8,128)} %bitcast.2.slab_ref.steps_ref, f32[1,200,256]{2,1,0:T(8,128)} %bitcast.2.slab_ref.steps_ref, f32[4,1152,128]{2,1,0:T(8,128)S(1)} %bitcast.55, f32[3,1152,128]{2,1,0:T(8,128)S(1)} %bitcast.28), custom_call_target="tpu_custom_call" | custom-call | flops 8000000000 | tf_op jit(solution)/shard_map/collect_points/pallas_call | solution.py:669
  85.8 2.0 %collective-permute-done.13.refs_2_ = f32[1,128,256]{2,1,0:T(8,128)S(1)} collective-permute-done((f32[1,128,256]{2,1,0:T(8,128)S(1)}, f32[1,128,256]{2,1,0:T(8,128)S(1)}, u32[]{:S(2)}, u32[]{:S(2)}) %collective-permute-start.13) | collective-permute-done | bytes 131104 | tf_op jit(solution)/shard_map/ppermute | solution.py:588
  87.8 3.8 %unsort_points.1 = (f32[2,128,128]{2,1,0:T(8,128)S(1)}, f32[8,8,128]{2,1,0:T(8,128)S(1)}) custom-call(f32[1,128,256]{2,1,0:T(8,128)S(1)} %collect_points.4.refs_0_, f32[1,128,256]{2,1,0:T(8,128)S(1)} %collective-permute-done.12.refs_1_, f32[1,128,256]{2,1,0:T(8,128)S(1)} %collective-permute-done.13.refs_2_, ...), custom_call_target="tpu_custom_call" | custom-call | flops 6000000000 | tf_op jit(solution)/shard_map/unsort_points/pallas_call | solution.py:688
  91.6 7.4 %all_to_all.5.sum_ref = f32[8,8,128]{2,1,0:T(8,128)S(1)} all-to-all(f32[8,8,128]{2,1,0:T(8,128)S(1)} %get-tuple-element.62), channel_id=1, replica_groups=mesh['grid'=8,'band'=4] {'grid'}, dimensions={0} | all-to-all | bytes 65536 | tf_op jit(solution)/shard_map/all_to_all | solution.py:699
  99.1 0.8 residual.1
  (31 shorter events, 1.3 us)
Async XLA Ops:
  8.8 14.6 %collective-permute-start.1 = (f32[200,256]{1,0:T(8,128)}, f32[200,256]{1,0:T(8,128)S(1)}, u32[]{:S(2)}, u32[]{:S(2)}) collective-permute-start(f32[200,256]{1,0:T(8,128)} %get-tuple-element.39), channel_id=1, source_target_pairs={{0,16},{4,20},{8,24},{12,28},{16,0},{20,4},{24,8},{28,12},{1,17},{... | collective-permute-start | bytes 614408 | tf_op jit(solution)/shard_map/ppermute | solution.py:588
  11.9 6.7 %collective-permute-start = (f32[200,256]{1,0:T(8,128)}, f32[200,256]{1,0:T(8,128)S(1)}, u32[]{:S(2)}, u32[]{:S(2)}) collective-permute-start(f32[200,256]{1,0:T(8,128)} %get-tuple-element.39), channel_id=1, source_target_pairs={{0,8},{4,12},{8,0},{12,4},{16,24},{20,28},{24,16},{28,20},{1,9},{5... | collective-permute-start | bytes 614408 | tf_op jit(solution)/shard_map/ppermute | solution.py:588
  18.2 10.1 %collective-permute-start.2 = (f32[200,256]{1,0:T(8,128)}, f32[200,256]{1,0:T(8,128)S(1)}, u32[]{:S(2)}, u32[]{:S(2)}) collective-permute-start(f32[200,256]{1,0:T(8,128)} %get-tuple-element.39), channel_id=1, source_target_pairs={{0,24},{4,28},{8,16},{12,20},{16,8},{20,12},{24,0},{28,4},{1,25},{... | collective-permute-start | bytes 614408 | tf_op jit(solution)/shard_map/ppermute | solution.py:588
  18.3 14.8 %collective-permute-start.3 = (f32[1,1152,128]{2,1,0:T(8,128)S(1)}, f32[1,1152,128]{2,1,0:T(8,128)S(1)}, u32[]{:S(2)}, u32[]{:S(2)}) collective-permute-start(f32[1,1152,128]{2,1,0:T(8,128)S(1)} %get-tuple-element.41), channel_id=1, source_target_pairs={{0,4},{4,0},{8,12},{12,8},{16,20},{20,16},{24,28},{28,24},{1,5},{5... | collective-permute-start | bytes 1769480 | tf_op jit(solution)/shard_map/ppermute | solution.py:588
  23.1 10.0 %collective-permute-start.4 = (f32[1,1152,128]{2,1,0:T(8,128)S(1)}, f32[1,1152,128]{2,1,0:T(8,128)S(1)}, u32[]{:S(2)}, u32[]{:S(2)}) collective-permute-start(f32[1,1152,128]{2,1,0:T(8,128)S(1)} %get-tuple-element.42), channel_id=1, source_target_pairs={{0,4},{4,0},{8,12},{12,8},{16,20},{20,16},{24,28},{28,24},{1,5},{5... | collective-permute-start | bytes 1769480 | tf_op jit(solution)/shard_map/ppermute | solution.py:588
  27.9 5.2 %collective-permute-start.5 = (f32[1,1152,128]{2,1,0:T(8,128)S(1)}, f32[1,1152,128]{2,1,0:T(8,128)S(1)}, u32[]{:S(2)}, u32[]{:S(2)}) collective-permute-start(f32[1,1152,128]{2,1,0:T(8,128)S(1)} %get-tuple-element.43), channel_id=1, source_target_pairs={{0,4},{4,0},{8,12},{12,8},{16,20},{20,16},{24,28},{28,24},{1,5},{5... | collective-permute-start | bytes 1769480 | tf_op jit(solution)/shard_map/ppermute | solution.py:588
  28.3 6.6 %copy-start = (f32[2,1,16384]{2,1,0:T(1,128)S(1)}, f32[2,1,16384]{2,1,0:T(1,128)}, u32[]{:S(2)}) copy-start(f32[2,1,16384]{2,1,0:T(1,128)} %param.7) | copy-start | bytes 393220
  28.3 11.5 %copy-start.1 = (bf16[384,1152]{1,0:T(8,128)(2,1)S(1)}, bf16[384,1152]{1,0:T(8,128)(2,1)}, u32[]{:S(2)}) copy-start(bf16[384,1152]{1,0:T(8,128)(2,1)} %constant.11.clone.refs_12_) | copy-start | bytes 2654212
  28.3 11.5 %copy-start.2 = (bf16[384,1152]{1,0:T(8,128)(2,1)S(1)}, bf16[384,1152]{1,0:T(8,128)(2,1)}, u32[]{:S(2)}) copy-start(bf16[384,1152]{1,0:T(8,128)(2,1)} %constant.8.clone.refs_9_) | copy-start | bytes 2654212
  28.3 11.5 %copy-start.3 = (bf16[1152,256]{1,0:T(8,128)(2,1)S(1)}, bf16[1152,256]{1,0:T(8,128)(2,1)}, u32[]{:S(2)}) copy-start(bf16[1152,256]{1,0:T(8,128)(2,1)} %constant.10.clone.refs_11_) | copy-start | bytes 1769476
  28.3 11.5 %copy-start.4 = (bf16[768,384]{1,0:T(8,128)(2,1)S(1)}, bf16[768,384]{1,0:T(8,128)(2,1)}, u32[]{:S(2)}) copy-start(bf16[768,384]{1,0:T(8,128)(2,1)} %constant.9.clone.refs_10_) | copy-start | bytes 1769476
  32.8 2.1 %collective-permute-start.6 = (f32[1,1152,128]{2,1,0:T(8,128)S(1)}, f32[1,1152,128]{2,1,0:T(8,128)S(1)}, u32[]{:S(2)}, u32[]{:S(2)}) collective-permute-start(f32[1,1152,128]{2,1,0:T(8,128)S(1)} %get-tuple-element.44), channel_id=1, source_target_pairs={{0,4},{4,0},{8,12},{12,8},{16,20},{20,16},{24,28},{28,24},{1,5},{5... | collective-permute-start | bytes 1769480 | tf_op jit(solution)/shard_map/ppermute | solution.py:588
  34.9 28.6 %collective-permute-start.9 = (f32[2,128,128]{2,1,0:T(8,128)S(1)}, f32[2,128,128]{2,1,0:T(8,128)S(1)}, u32[]{:S(2)}, u32[]{:S(2)}) collective-permute-start(f32[2,128,128]{2,1,0:T(8,128)S(1)} %bitcast.47), channel_id=1, source_target_pairs={{0,3},{1,0},{2,1},{3,2},{4,7},{5,4},{6,5},{7,6},{8,11},{9,8},{10,9... | collective-permute-start | bytes 393224 | tf_op jit(solution)/shard_map/ppermute | solution.py:627
  38.8 24.7 %collective-permute-start.8 = (f32[2,128,128]{2,1,0:T(8,128)S(1)}, f32[2,128,128]{2,1,0:T(8,128)S(1)}, u32[]{:S(2)}, u32[]{:S(2)}) collective-permute-start(f32[2,128,128]{2,1,0:T(8,128)S(1)} %bitcast.48), channel_id=1, source_target_pairs={{0,2},{1,3},{2,0},{3,1},{4,6},{5,7},{6,4},{7,5},{8,10},{9,11},{10,... | collective-permute-start | bytes 393224 | tf_op jit(solution)/shard_map/ppermute | solution.py:627
  38.8 24.7 %collective-permute-start.7 = (f32[2,128,128]{2,1,0:T(8,128)S(1)}, f32[2,128,128]{2,1,0:T(8,128)S(1)}, u32[]{:S(2)}, u32[]{:S(2)}) collective-permute-start(f32[2,128,128]{2,1,0:T(8,128)S(1)} %bitcast.49), channel_id=1, source_target_pairs={{0,1},{1,2},{2,3},{3,0},{4,5},{5,6},{6,7},{7,4},{8,9},{9,10},{10,1... | collective-permute-start | bytes 393224 | tf_op jit(solution)/shard_map/ppermute | solution.py:627
  63.5 2.1 %collective-permute-start.10 = (f32[1,24,2,3,8,128]{5,4,3,2,1,0:T(8,128)S(1)}, f32[1,24,2,3,8,128]{5,4,3,2,1,0:T(8,128)S(1)}, u32[]{:S(2)}, u32[]{:S(2)}) collective-permute-start(f32[1,24,2,3,8,128]{5,4,3,2,1,0:T(8,128)S(1)} %get-tuple-element.53), channel_id=1, source_target_pairs={{0,4},{4,0},{8,12},{12,8},{16,20},{20,16},{24,28},{28,24},{1,5},{5... | collective-permute-start | bytes 1769480 | tf_op jit(solution)/shard_map/ppermute | solution.py:588
  65.6 5.7 %collective-permute-start.11 = (f32[3,24,2,3,8,128]{5,4,3,2,1,0:T(8,128)S(1)}, f32[3,24,2,3,8,128]{5,4,3,2,1,0:T(8,128)S(1)}, u32[]{:S(2)}, u32[]{:S(2)}) collective-permute-start(f32[3,24,2,3,8,128]{5,4,3,2,1,0:T(8,128)S(1)} %get-tuple-element.55), channel_id=1, source_target_pairs={{0,4},{4,0},{8,12},{12,8},{16,20},{20,16},{24,28},{28,24},{1,5},{5... | collective-permute-start | bytes 5308424 | tf_op jit(solution)/shard_map/ppermute | solution.py:588
  69.7 16.0 %collective-permute-start.12 = (f32[1,128,256]{2,1,0:T(8,128)S(1)}, f32[1,128,256]{2,1,0:T(8,128)S(1)}, u32[]{:S(2)}, u32[]{:S(2)}) collective-permute-start(f32[1,128,256]{2,1,0:T(8,128)S(1)} %collect_points.5), channel_id=1, source_target_pairs={{0,8},{4,12},{8,0},{12,4},{16,24},{20,28},{24,16},{28,20},{1,9},{5... | collective-permute-start | bytes 393224 | tf_op jit(solution)/shard_map/ppermute | solution.py:588
  79.4 8.4 %copy-start.5 = (f32[64,256]{1,0:T(8,128)S(1)}, f32[64,256]{1,0:T(8,128)}, u32[]{:S(2)}) copy-start(f32[64,256]{1,0:T(8,128)} %get-tuple-element.57.refs_4_) | copy-start | bytes 196612
  79.4 8.4 %collective-permute-start.13 = (f32[1,128,256]{2,1,0:T(8,128)S(1)}, f32[1,128,256]{2,1,0:T(8,128)S(1)}, u32[]{:S(2)}, u32[]{:S(2)}) collective-permute-start(f32[1,128,256]{2,1,0:T(8,128)S(1)} %collect_points.6), channel_id=1, source_target_pairs={{0,16},{4,20},{8,24},{12,28},{16,0},{20,4},{24,8},{28,12},{1,17},{... | collective-permute-start | bytes 393224 | tf_op jit(solution)/shard_map/ppermute | solution.py:588
  81.0 6.8 %collective-permute-start.14 = (f32[1,128,256]{2,1,0:T(8,128)S(1)}, f32[1,128,256]{2,1,0:T(8,128)S(1)}, u32[]{:S(2)}, u32[]{:S(2)}) collective-permute-start(f32[1,128,256]{2,1,0:T(8,128)S(1)} %collect_points.7), channel_id=1, source_target_pairs={{0,24},{4,28},{8,16},{12,20},{16,8},{20,12},{24,0},{28,4},{1,25},{... | collective-permute-start | bytes 393224 | tf_op jit(solution)/shard_map/ppermute | solution.py:588

commit v6 on v5

--- a/solution.py
+++ b/solution.py
@@ -352,7 +352,7 @@
     lax.fori_loop(0, -(-(rows + planes - 1) // unroll), visit, 0)
 
 
-def potential_kernel(group, height, planes, calls, parts, *refs):
+def potential_kernel(planes, calls, parts, *refs):
     own, sib = refs[:calls], refs[calls : 2 * calls]
     v_ref, *tables_hbm = refs[2 * calls : 2 * calls + 5]
     keep_ref = refs[2 * calls + 5]
@@ -362,10 +362,8 @@
     me = lax.axis_index("grid")
     half = keep_ref.shape[0]
     per_call = half // calls
-    tiles = height // 8
-    shape = (N, 2, tiles, 8, LANES)
-    t_tiles, u_tiles = t_ref.reshape(shape), u_ref.reshape(shape)
-    last = planes // group - 1
+    tiles = t_ref.shape[2]
+    last = tiles - 1
 
     def place(j, q):
         return pl.ds((me ^ (2 * j + q)) * planes, planes)
@@ -374,18 +372,18 @@
         for q, blocks in enumerate((own, sib)):
             for j in range(half):
                 yield pltpu.make_async_copy(
-                    blocks[j // per_call].at[j % per_call, :, :, t], t_tiles.at[place(j, q), :, t], in_sems.at[t, q, j]
+                    blocks[j // per_call].at[j % per_call, :, :, t], t_ref.at[place(j, q), :, t], in_sems.at[t, q, j]
                 )
 
     def departures(t):
         for j in range(half):
             yield pltpu.make_async_copy(
-                u_tiles.at[place(j, 0), :, t], keep_ref.at[j, :, :, t], out_sems.at[t, 0, j]
+                u_ref.at[place(j, 0), :, t], keep_ref.at[j, :, :, t], out_sems.at[t, 0, j]
             )
         for ref, part in zip(send_refs, parts):
             for i, j in enumerate(part):
                 yield pltpu.make_async_copy(
-                    u_tiles.at[place(j, 1), :, t], ref.at[i, :, :, t], out_sems.at[t, 1, j]
+                    u_ref.at[place(j, 1), :, t], ref.at[i, :, :, t], out_sems.at[t, 1, j]
                 )
 
     def fetches():
@@ -400,23 +398,23 @@
         for copies in (arrivals(0), fetches()):
             for copy in copies:
                 copy.wait()
-        if height > planes:
-            u_ref[...] = jnp.zeros_like(u_ref)
 
     for t in range(1, tiles):
 
-        @pl.when(step == t * 8 // group)
+        @pl.when(step == t)
         def _(t=t):
             for copy in arrivals(t):
                 copy.wait()
 
-    stride = 2 * height
-    real, imag = [], []
-    for j in range(group):
-        k = step * group + j
-        real.append(t_ref[pl.ds(k, N, stride=stride), :])
-        imag.append(t_ref[pl.ds(k + height, N, stride=stride), :])
-    x = jnp.concatenate([jnp.concatenate(real, axis=1), jnp.concatenate(imag, axis=1)], axis=0)
+    group = 8
+
+    def turn(x):
+        return jnp.transpose(x, (1, 0, 2))
+
+    def abreast(x):
+        return jnp.concatenate([x[j] for j in range(group)], axis=1)
+
+    x = jnp.concatenate([abreast(turn(t_ref[:, q, step])) for q in range(2)], axis=0)
     high, low = split(x)
     x = mm(bf_ref[...], jnp.concatenate([high, high, low], axis=0))
     x = jnp.concatenate(
@@ -428,10 +426,10 @@
     )
     high, low = split(x)
     x = mm(jnp.concatenate([high, high, low], axis=1), cf_ref[...])
+    cells = [turn(v_ref[0, :, q]) for q in range(3)]
     v = []
     for j in range(group):
-        line = (step * group + j) % 8
-        t = [v_ref[0, pl.ds(8 * q + line, N // 2, stride=24), :] for q in range(3)]
+        t = [cell[j] for cell in cells]
         v.append(jnp.concatenate([t[0], t[1][:, :64]], axis=1))
         v.append(jnp.concatenate([t[1][:, 64:], t[2]], axis=1))
     v = jnp.concatenate(v, axis=0)
@@ -447,14 +445,13 @@
     )
     high, low = split(x)
     x = mm(bi_ref[...], jnp.concatenate([high, high, low], axis=0))
-    for j in range(group):
-        k = step * group + j
-        u_ref[pl.ds(k, N, stride=stride), :] = x[:N, j * LANES : (j + 1) * LANES]
-        u_ref[pl.ds(k + height, N, stride=stride), :] = x[N:, j * LANES : (j + 1) * LANES]
+    for q in range(2):
+        part = x[q * N : (q + 1) * N]
+        u_ref[:, q, step] = turn(jnp.stack([part[:, j * LANES : (j + 1) * LANES] for j in range(group)]))
 
     for t in range(tiles):
 
-        @pl.when(step == min((t + 1) * 8 // group - 1, last))
+        @pl.when(step == t)
         def _(t=t):
             for copy in departures(t):
                 copy.start()
@@ -554,7 +551,6 @@
     count = coefficients.shape[2]
     rows = count // CHUNK
     height = -(-planes // 8) * 8
-    group = 8 if planes % 8 == 0 else 1
     unroll = 44
     me = lax.axis_index("grid")
     half = slabs // 2
@@ -620,7 +616,7 @@
         sib.append(swap(theirs, 1))
     cells = potential if height == planes else jnp.pad(potential, ((0, height - planes), (0, 0)))
     cells = cells.reshape(height // 8, 8, N * N // LANES, LANES).transpose(0, 2, 1, 3)
-    cells = cells.reshape(height // 8, N * N // 16, LANES)
+    cells = cells.reshape(height // 8, N // 2, 3, 8, LANES)
     *sib, mine = lax.optimization_barrier((*sib, coef))
     coefs = [coef]
     for shift in range(1, bands):
@@ -629,16 +625,16 @@
     parts = [[1], [0, *range(2, half)]] if 2 <= half <= 4 else [list(range(half))]
     cube = (planes, 2, height // 8, 8, LANES)
     keep, *send = pl.pallas_call(
-        functools.partial(potential_kernel, group, height, planes, calls, parts),
-        grid=(planes // group,),
+        functools.partial(potential_kernel, planes, calls, parts),
+        grid=(height // 8,),
         in_specs=[anywhere] * (2 * calls)
-        + [pl.BlockSpec((1, N * N // 16, LANES), lambda i: (i * group // 8, 0, 0))]
+        + [pl.BlockSpec((1, N // 2, 3, 8, LANES), lambda i: (i, 0, 0, 0, 0))]
         + [anywhere] * 4,
         out_specs=[anywhere] * (1 + len(parts)),
         out_shape=[jax.ShapeDtypeStruct((count_of, *cube), F32) for count_of in (half, *map(len, parts))],
         scratch_shapes=[
-            pltpu.VMEM((slabs * lines, LANES), F32),
-            pltpu.VMEM((slabs * lines, LANES), F32),
+            pltpu.VMEM((N, *cube[1:]), F32),
+            pltpu.VMEM((N, *cube[1:]), F32),
             *(pltpu.VMEM(t.shape, BF) for t in constants),
             pltpu.SemaphoreType.DMA((height // 8, 2, half)),
             pltpu.SemaphoreType.DMA((height // 8, 2, half)),

time: 100 us -> 99.7 us (level)
  no operation moved by 1% of the time
where the time goes in v6:
time: 99.7 us; the launch traced here: 99.5 us
  Pallas kernels  70.8 us (71%)
  starting transfers between devices  14.3 us (14%)
  blocking collectives  7.43 us (7%)
  waiting for transfers between devices  6.13 us (6%)
    pallas_call x1, Pallas kernels, local(): pl.pallas_call(functools.partial(potential_kernel, planes, calls, parts),...  23.3 us
    pallas_call x4, Pallas kernels, local(): mine, theirs = spread(points[call], points[call])  18.3 us
    pallas_call x4, Pallas kernels, local(): pl.pallas_call(functools.partial(collect_kernel, planes, height, unroll),...  16.3 us
    ppermute x12, starting transfers between devices, swap(): return lax.ppermute(x, 'grid', [(i, i ^ bits) for i in range(slabs)])  9.42 us
    pallas_call x1, Pallas kernels, local(): pl.pallas_call(functools.partial(sort_kernel, planes), in_specs=[pl.Block...  8.2 us
    all_to_all x1, blocking collectives, local(): sums = lax.all_to_all(part, 'grid', split_axis=0, concat_axis=0, tiled=True)  7.43 us
    ppermute x12, waiting for transfers between devices, swap(): return lax.ppermute(x, 'grid', [(i, i ^ bits) for i in range(slabs)])  6.12 us
    ppermute x3, starting transfers between devices, local(): lax.ppermute(mine, 'band', [(i, (i + shift) % bands) for i in range(bands)])  4.87 us
  transfers between devices with their start and end apart: 15, of which 4 were waited for; matrix products, arithmetic and copies ran while one was open for 0% of the time, Pallas kernels for 58%

profile of v6, /device:TPU:0, one launch (start us, length us, event | category | flops | bytes accessed | tf_op | source)
XLA Modules:
  0.0 99.5 jit_solution(16261668861333044167)
XLA Ops:
  0.6 8.2 %sort_points.1 = (f32[200,256]{1,0:T(8,128)}, f32[64,256]{1,0:T(8,128)}) custom-call(s32[128,128]{1,0:T(8,128)} %bitcast.61, f32[2,128,128]{2,1,0:T(8,128)} %bitcast.46), custom_call_target="tpu_custom_call" | custom-call | flops 10000000000 | tf_op jit(solution)/shard_map/sort_points/pallas_call | solution.py:560
  8.8 3.0 %collective-permute-start.1 = (f32[200,256]{1,0:T(8,128)}, f32[200,256]{1,0:T(8,128)S(1)}, u32[]{:S(2)}, u32[]{:S(2)}) collective-permute-start(f32[200,256]{1,0:T(8,128)} %get-tuple-element.39), channel_id=1, source_target_pairs={{0,16},{4,20},{8,24},{12,28},{16,0},{20,4},{24,8},{28,12},{1,17},{... | collective-permute-start | bytes 614408 | tf_op jit(solution)/shard_map/ppermute | solution.py:584
  11.9 1.5 %collective-permute-start = (f32[200,256]{1,0:T(8,128)}, f32[200,256]{1,0:T(8,128)S(1)}, u32[]{:S(2)}, u32[]{:S(2)}) collective-permute-start(f32[200,256]{1,0:T(8,128)} %get-tuple-element.39), channel_id=1, source_target_pairs={{0,8},{4,12},{8,0},{12,4},{16,24},{20,28},{24,16},{28,20},{1,9},{5... | collective-permute-start | bytes 614408 | tf_op jit(solution)/shard_map/ppermute | solution.py:584
  13.4 4.8 %spread_points.4 = (f32[1,1152,128]{2,1,0:T(8,128)S(1)}, f32[1,1152,128]{2,1,0:T(8,128)S(1)}) custom-call(f32[1,200,256]{2,1,0:T(8,128)} %bitcast.2.slab_ref.steps_ref, f32[1,200,256]{2,1,0:T(8,128)} %bitcast.2.slab_ref.steps_ref), custom_call_target="tpu_custom_call" | custom-call | flops 8000000000 | tf_op jit(solution)/shard_map/spread_points/pallas_call | solution.py:611
  18.6 4.5 %spread_points.5 = (f32[1,1152,128]{2,1,0:T(8,128)S(1)}, f32[1,1152,128]{2,1,0:T(8,128)S(1)}) custom-call(f32[1,200,256]{2,1,0:T(8,128)S(1)} %bitcast.42, f32[1,200,256]{2,1,0:T(8,128)S(1)} %bitcast.43), custom_call_target="tpu_custom_call" | custom-call | flops 8000000000 | tf_op jit(solution)/shard_map/spread_points/pallas_call | solution.py:611
  23.4 4.5 %spread_points.6 = (f32[1,1152,128]{2,1,0:T(8,128)S(1)}, f32[1,1152,128]{2,1,0:T(8,128)S(1)}) custom-call(f32[1,200,256]{2,1,0:T(8,128)S(1)} %bitcast.34, f32[1,200,256]{2,1,0:T(8,128)S(1)} %bitcast.35), custom_call_target="tpu_custom_call" | custom-call | flops 8000000000 | tf_op jit(solution)/shard_map/spread_points/pallas_call | solution.py:611
  27.9 0.4 collective-permute-start.5
  28.3 4.5 %spread_points.7 = (f32[1,1152,128]{2,1,0:T(8,128)S(1)}, f32[1,1152,128]{2,1,0:T(8,128)S(1)}) custom-call(f32[1,200,256]{2,1,0:T(8,128)S(1)} %bitcast.38, f32[1,200,256]{2,1,0:T(8,128)S(1)} %bitcast.39), custom_call_target="tpu_custom_call" | custom-call | flops 8000000000 | tf_op jit(solution)/shard_map/spread_points/pallas_call | solution.py:611
  33.1 1.8 %collective-permute-done.6 = f32[1,1152,128]{2,1,0:T(8,128)S(1)} collective-permute-done((f32[1,1152,128]{2,1,0:T(8,128)S(1)}, f32[1,1152,128]{2,1,0:T(8,128)S(1)}, u32[]{:S(2)}, u32[]{:S(2)}) %collective-permute-start.6) | collective-permute-done | bytes 589856 | tf_op jit(solution)/shard_map/ppermute | solution.py:584
  34.9 3.9 %collective-permute-start.9 = (f32[2,128,128]{2,1,0:T(8,128)S(1)}, f32[2,128,128]{2,1,0:T(8,128)S(1)}, u32[]{:S(2)}, u32[]{:S(2)}) collective-permute-start(f32[2,128,128]{2,1,0:T(8,128)S(1)} %bitcast.47), channel_id=1, source_target_pairs={{0,3},{1,0},{2,1},{3,2},{4,7},{5,4},{6,5},{7,6},{8,11},{9,8},{10,9... | collective-permute-start | bytes 393224 | tf_op jit(solution)/shard_map/ppermute | solution.py:623
  38.8 1.0 %collective-permute-start.7 = (f32[2,128,128]{2,1,0:T(8,128)S(1)}, f32[2,128,128]{2,1,0:T(8,128)S(1)}, u32[]{:S(2)}, u32[]{:S(2)}) collective-permute-start(f32[2,128,128]{2,1,0:T(8,128)S(1)} %bitcast.49), channel_id=1, source_target_pairs={{0,1},{1,2},{2,3},{3,0},{4,5},{5,6},{6,7},{7,4},{8,9},{9,10},{10,1... | collective-permute-start | bytes 393224 | tf_op jit(solution)/shard_map/ppermute | solution.py:623
  39.8 23.3 %apply_potential.1 = (f32[4,24,2,3,8,128]{5,4,3,2,1,0:T(8,128)S(1)}, f32[1,24,2,3,8,128]{5,4,3,2,1,0:T(8,128)S(1)}, f32[3,24,2,3,8,128]{5,4,3,2,1,0:T(8,128)S(1)}) custom-call(f32[1,24,2,3,8,128]{5,4,3,2,1,0:T(8,128)S(1)} %bitcast.56, f32[1,24,2,3,8,128]{5,4,3,2,1,0:T(8,128)S(1)} %bitcast.57, f32[1,24,2,3,8,128]{5,4,3,2,1,0:T(8,128)S(1)} %bitcast.58, ...), custom_call_target="tpu_custom_call" | custom-call | flops 40000000000 | tf_op jit(solution)/shard_map/apply_potential/pallas_call | solution.py:627
  63.2 2.0 %collective-permute-done.10 = f32[1,24,2,3,8,128]{5,4,3,2,1,0:T(8,128)S(1)} collective-permute-done((f32[1,24,2,3,8,128]{5,4,3,2,1,0:T(8,128)S(1)}, f32[1,24,2,3,8,128]{5,4,3,2,1,0:T(8,128)S(1)}, u32[]{:S(2)}, u32[]{:S(2)}) %collective-permute-start.10) | collective-permute-done | bytes 589856 | tf_op jit(solution)/shard_map/ppermute | solution.py:584
  65.3 4.0 %collect_points.5 = f32[1,128,256]{2,1,0:T(8,128)S(1)} custom-call(f32[1,200,256]{2,1,0:T(8,128)S(1)} %bitcast.44, f32[1,200,256]{2,1,0:T(8,128)S(1)} %bitcast.45, f32[4,1152,128]{2,1,0:T(8,128)S(1)} %bitcast.52, f32[1,1152,128]{2,1,0:T(8,128)S(1)} %bitcast.33), custom_call_target="tpu_custom_call" | custom-call | flops 8000000000 | tf_op jit(solution)/shard_map/collect_points/pallas_call | solution.py:665
  69.3 1.6 %collective-permute-start.12 = (f32[1,128,256]{2,1,0:T(8,128)S(1)}, f32[1,128,256]{2,1,0:T(8,128)S(1)}, u32[]{:S(2)}, u32[]{:S(2)}) collective-permute-start(f32[1,128,256]{2,1,0:T(8,128)S(1)} %collect_points.5), channel_id=1, source_target_pairs={{0,8},{4,12},{8,0},{12,4},{16,24},{20,28},{24,16},{28,20},{1,9},{5... | collective-permute-start | bytes 393224 | tf_op jit(solution)/shard_map/ppermute | solution.py:584
  70.8 4.0 %collect_points.7 = f32[1,128,256]{2,1,0:T(8,128)S(1)} custom-call(f32[1,200,256]{2,1,0:T(8,128)S(1)} %bitcast.40, f32[1,200,256]{2,1,0:T(8,128)S(1)} %bitcast.41, f32[4,1152,128]{2,1,0:T(8,128)S(1)} %bitcast.53, f32[3,1152,128]{2,1,0:T(8,128)S(1)} %bitcast.26), custom_call_target="tpu_custom_call" | custom-call | flops 8000000000 | tf_op jit(solution)/shard_map/collect_points/pallas_call | solution.py:665
  74.8 4.2 %collect_points.6 = f32[1,128,256]{2,1,0:T(8,128)S(1)} custom-call(f32[1,200,256]{2,1,0:T(8,128)S(1)} %bitcast.36, f32[1,200,256]{2,1,0:T(8,128)S(1)} %bitcast.37, f32[4,1152,128]{2,1,0:T(8,128)S(1)} %bitcast.54, f32[3,1152,128]{2,1,0:T(8,128)S(1)} %bitcast.27), custom_call_target="tpu_custom_call" | custom-call | flops 8000000000 | tf_op jit(solution)/shard_map/collect_points/pallas_call | solution.py:665
  79.0 1.6 %collective-permute-start.13 = (f32[1,128,256]{2,1,0:T(8,128)S(1)}, f32[1,128,256]{2,1,0:T(8,128)S(1)}, u32[]{:S(2)}, u32[]{:S(2)}) collective-permute-start(f32[1,128,256]{2,1,0:T(8,128)S(1)} %collect_points.6), channel_id=1, source_target_pairs={{0,16},{4,20},{8,24},{12,28},{16,0},{20,4},{24,8},{28,12},{1,17},{... | collective-permute-start | bytes 393224 | tf_op jit(solution)/shard_map/ppermute | solution.py:584
  80.6 0.5 collective-permute-start.14
  81.1 4.2 %collect_points.4.refs_0_ = f32[1,128,256]{2,1,0:T(8,128)S(1)} custom-call(f32[1,200,256]{2,1,0:T(8,128)} %bitcast.2.slab_ref.steps_ref, f32[1,200,256]{2,1,0:T(8,128)} %bitcast.2.slab_ref.steps_ref, f32[4,1152,128]{2,1,0:T(8,128)S(1)} %bitcast.55, f32[3,1152,128]{2,1,0:T(8,128)S(1)} %bitcast.28), custom_call_target="tpu_custom_call" | custom-call | flops 8000000000 | tf_op jit(solution)/shard_map/collect_points/pallas_call | solution.py:665
  85.3 2.0 %collective-permute-done.13.refs_2_ = f32[1,128,256]{2,1,0:T(8,128)S(1)} collective-permute-done((f32[1,128,256]{2,1,0:T(8,128)S(1)}, f32[1,128,256]{2,1,0:T(8,128)S(1)}, u32[]{:S(2)}, u32[]{:S(2)}) %collective-permute-start.13) | collective-permute-done | bytes 131104 | tf_op jit(solution)/shard_map/ppermute | solution.py:584
  87.4 3.8 %unsort_points.1 = (f32[2,128,128]{2,1,0:T(8,128)S(1)}, f32[8,8,128]{2,1,0:T(8,128)S(1)}) custom-call(f32[1,128,256]{2,1,0:T(8,128)S(1)} %collect_points.4.refs_0_, f32[1,128,256]{2,1,0:T(8,128)S(1)} %collective-permute-done.12.refs_1_, f32[1,128,256]{2,1,0:T(8,128)S(1)} %collective-permute-done.13.refs_2_, ...), custom_call_target="tpu_custom_call" | custom-call | flops 6000000000 | tf_op jit(solution)/shard_map/unsort_points/pallas_call | solution.py:684
  91.2 7.4 %all_to_all.5.sum_ref = f32[8,8,128]{2,1,0:T(8,128)S(1)} all-to-all(f32[8,8,128]{2,1,0:T(8,128)S(1)} %get-tuple-element.62), channel_id=1, replica_groups=mesh['grid'=8,'band'=4] {'grid'}, dimensions={0} | all-to-all | bytes 65536 | tf_op jit(solution)/shard_map/all_to_all | solution.py:695
  98.6 0.8 residual.1
  (31 shorter events, 1.3 us)
Async XLA Ops:
  8.8 14.6 %collective-permute-start.1 = (f32[200,256]{1,0:T(8,128)}, f32[200,256]{1,0:T(8,128)S(1)}, u32[]{:S(2)}, u32[]{:S(2)}) collective-permute-start(f32[200,256]{1,0:T(8,128)} %get-tuple-element.39), channel_id=1, source_target_pairs={{0,16},{4,20},{8,24},{12,28},{16,0},{20,4},{24,8},{28,12},{1,17},{... | collective-permute-start | bytes 614408 | tf_op jit(solution)/shard_map/ppermute | solution.py:584
  11.9 6.7 %collective-permute-start = (f32[200,256]{1,0:T(8,128)}, f32[200,256]{1,0:T(8,128)S(1)}, u32[]{:S(2)}, u32[]{:S(2)}) collective-permute-start(f32[200,256]{1,0:T(8,128)} %get-tuple-element.39), channel_id=1, source_target_pairs={{0,8},{4,12},{8,0},{12,4},{16,24},{20,28},{24,16},{28,20},{1,9},{5... | collective-permute-start | bytes 614408 | tf_op jit(solution)/shard_map/ppermute | solution.py:584
  18.2 10.1 %collective-permute-start.2 = (f32[200,256]{1,0:T(8,128)}, f32[200,256]{1,0:T(8,128)S(1)}, u32[]{:S(2)}, u32[]{:S(2)}) collective-permute-start(f32[200,256]{1,0:T(8,128)} %get-tuple-element.39), channel_id=1, source_target_pairs={{0,24},{4,28},{8,16},{12,20},{16,8},{20,12},{24,0},{28,4},{1,25},{... | collective-permute-start | bytes 614408 | tf_op jit(solution)/shard_map/ppermute | solution.py:584
  18.3 14.8 %collective-permute-start.3 = (f32[1,1152,128]{2,1,0:T(8,128)S(1)}, f32[1,1152,128]{2,1,0:T(8,128)S(1)}, u32[]{:S(2)}, u32[]{:S(2)}) collective-permute-start(f32[1,1152,128]{2,1,0:T(8,128)S(1)} %get-tuple-element.41), channel_id=1, source_target_pairs={{0,4},{4,0},{8,12},{12,8},{16,20},{20,16},{24,28},{28,24},{1,5},{5... | collective-permute-start | bytes 1769480 | tf_op jit(solution)/shard_map/ppermute | solution.py:584
  23.1 10.0 %collective-permute-start.4 = (f32[1,1152,128]{2,1,0:T(8,128)S(1)}, f32[1,1152,128]{2,1,0:T(8,128)S(1)}, u32[]{:S(2)}, u32[]{:S(2)}) collective-permute-start(f32[1,1152,128]{2,1,0:T(8,128)S(1)} %get-tuple-element.42), channel_id=1, source_target_pairs={{0,4},{4,0},{8,12},{12,8},{16,20},{20,16},{24,28},{28,24},{1,5},{5... | collective-permute-start | bytes 1769480 | tf_op jit(solution)/shard_map/ppermute | solution.py:584
  27.9 5.2 %collective-permute-start.5 = (f32[1,1152,128]{2,1,0:T(8,128)S(1)}, f32[1,1152,128]{2,1,0:T(8,128)S(1)}, u32[]{:S(2)}, u32[]{:S(2)}) collective-permute-start(f32[1,1152,128]{2,1,0:T(8,128)S(1)} %get-tuple-element.43), channel_id=1, source_target_pairs={{0,4},{4,0},{8,12},{12,8},{16,20},{20,16},{24,28},{28,24},{1,5},{5... | collective-permute-start | bytes 1769480 | tf_op jit(solution)/shard_map/ppermute | solution.py:584
  28.3 6.6 %copy-start = (f32[2,1,16384]{2,1,0:T(1,128)S(1)}, f32[2,1,16384]{2,1,0:T(1,128)}, u32[]{:S(2)}) copy-start(f32[2,1,16384]{2,1,0:T(1,128)} %param.7) | copy-start | bytes 393220
  28.3 11.5 %copy-start.1 = (bf16[384,1152]{1,0:T(8,128)(2,1)S(1)}, bf16[384,1152]{1,0:T(8,128)(2,1)}, u32[]{:S(2)}) copy-start(bf16[384,1152]{1,0:T(8,128)(2,1)} %constant.11.clone.refs_12_) | copy-start | bytes 2654212
  28.3 11.5 %copy-start.2 = (bf16[384,1152]{1,0:T(8,128)(2,1)S(1)}, bf16[384,1152]{1,0:T(8,128)(2,1)}, u32[]{:S(2)}) copy-start(bf16[384,1152]{1,0:T(8,128)(2,1)} %constant.8.clone.refs_9_) | copy-start | bytes 2654212
  28.3 11.5 %copy-start.3 = (bf16[1152,256]{1,0:T(8,128)(2,1)S(1)}, bf16[1152,256]{1,0:T(8,128)(2,1)}, u32[]{:S(2)}) copy-start(bf16[1152,256]{1,0:T(8,128)(2,1)} %constant.10.clone.refs_11_) | copy-start | bytes 1769476
  28.3 11.5 %copy-start.4 = (bf16[768,384]{1,0:T(8,128)(2,1)S(1)}, bf16[768,384]{1,0:T(8,128)(2,1)}, u32[]{:S(2)}) copy-start(bf16[768,384]{1,0:T(8,128)(2,1)} %constant.9.clone.refs_10_) | copy-start | bytes 1769476
  32.8 2.1 %collective-permute-start.6 = (f32[1,1152,128]{2,1,0:T(8,128)S(1)}, f32[1,1152,128]{2,1,0:T(8,128)S(1)}, u32[]{:S(2)}, u32[]{:S(2)}) collective-permute-start(f32[1,1152,128]{2,1,0:T(8,128)S(1)} %get-tuple-element.44), channel_id=1, source_target_pairs={{0,4},{4,0},{8,12},{12,8},{16,20},{20,16},{24,28},{28,24},{1,5},{5... | collective-permute-start | bytes 1769480 | tf_op jit(solution)/shard_map/ppermute | solution.py:584
  34.9 28.2 %collective-permute-start.9 = (f32[2,128,128]{2,1,0:T(8,128)S(1)}, f32[2,128,128]{2,1,0:T(8,128)S(1)}, u32[]{:S(2)}, u32[]{:S(2)}) collective-permute-start(f32[2,128,128]{2,1,0:T(8,128)S(1)} %bitcast.47), channel_id=1, source_target_pairs={{0,3},{1,0},{2,1},{3,2},{4,7},{5,4},{6,5},{7,6},{8,11},{9,8},{10,9... | collective-permute-start | bytes 393224 | tf_op jit(solution)/shard_map/ppermute | solution.py:623
  38.8 24.3 %collective-permute-start.8 = (f32[2,128,128]{2,1,0:T(8,128)S(1)}, f32[2,128,128]{2,1,0:T(8,128)S(1)}, u32[]{:S(2)}, u32[]{:S(2)}) collective-permute-start(f32[2,128,128]{2,1,0:T(8,128)S(1)} %bitcast.48), channel_id=1, source_target_pairs={{0,2},{1,3},{2,0},{3,1},{4,6},{5,7},{6,4},{7,5},{8,10},{9,11},{10,... | collective-permute-start | bytes 393224 | tf_op jit(solution)/shard_map/ppermute | solution.py:623
  38.8 24.3 %collective-permute-start.7 = (f32[2,128,128]{2,1,0:T(8,128)S(1)}, f32[2,128,128]{2,1,0:T(8,128)S(1)}, u32[]{:S(2)}, u32[]{:S(2)}) collective-permute-start(f32[2,128,128]{2,1,0:T(8,128)S(1)} %bitcast.49), channel_id=1, source_target_pairs={{0,1},{1,2},{2,3},{3,0},{4,5},{5,6},{6,7},{7,4},{8,9},{9,10},{10,1... | collective-permute-start | bytes 393224 | tf_op jit(solution)/shard_map/ppermute | solution.py:623
  63.1 2.1 %collective-permute-start.10 = (f32[1,24,2,3,8,128]{5,4,3,2,1,0:T(8,128)S(1)}, f32[1,24,2,3,8,128]{5,4,3,2,1,0:T(8,128)S(1)}, u32[]{:S(2)}, u32[]{:S(2)}) collective-permute-start(f32[1,24,2,3,8,128]{5,4,3,2,1,0:T(8,128)S(1)} %get-tuple-element.53), channel_id=1, source_target_pairs={{0,4},{4,0},{8,12},{12,8},{16,20},{20,16},{24,28},{28,24},{1,5},{5... | collective-permute-start | bytes 1769480 | tf_op jit(solution)/shard_map/ppermute | solution.py:584
  65.2 5.7 %collective-permute-start.11 = (f32[3,24,2,3,8,128]{5,4,3,2,1,0:T(8,128)S(1)}, f32[3,24,2,3,8,128]{5,4,3,2,1,0:T(8,128)S(1)}, u32[]{:S(2)}, u32[]{:S(2)}) collective-permute-start(f32[3,24,2,3,8,128]{5,4,3,2,1,0:T(8,128)S(1)} %get-tuple-element.55), channel_id=1, source_target_pairs={{0,4},{4,0},{8,12},{12,8},{16,20},{20,16},{24,28},{28,24},{1,5},{5... | collective-permute-start | bytes 5308424 | tf_op jit(solution)/shard_map/ppermute | solution.py:584
  69.3 16.0 %collective-permute-start.12 = (f32[1,128,256]{2,1,0:T(8,128)S(1)}, f32[1,128,256]{2,1,0:T(8,128)S(1)}, u32[]{:S(2)}, u32[]{:S(2)}) collective-permute-start(f32[1,128,256]{2,1,0:T(8,128)S(1)} %collect_points.5), channel_id=1, source_target_pairs={{0,8},{4,12},{8,0},{12,4},{16,24},{20,28},{24,16},{28,20},{1,9},{5... | collective-permute-start | bytes 393224 | tf_op jit(solution)/shard_map/ppermute | solution.py:584
  79.0 8.4 %copy-start.5 = (f32[64,256]{1,0:T(8,128)S(1)}, f32[64,256]{1,0:T(8,128)}, u32[]{:S(2)}) copy-start(f32[64,256]{1,0:T(8,128)} %get-tuple-element.57.refs_4_) | copy-start | bytes 196612
  79.0 8.3 %collective-permute-start.13 = (f32[1,128,256]{2,1,0:T(8,128)S(1)}, f32[1,128,256]{2,1,0:T(8,128)S(1)}, u32[]{:S(2)}, u32[]{:S(2)}) collective-permute-start(f32[1,128,256]{2,1,0:T(8,128)S(1)} %collect_points.6), channel_id=1, source_target_pairs={{0,16},{4,20},{8,24},{12,28},{16,0},{20,4},{24,8},{28,12},{1,17},{... | collective-permute-start | bytes 393224 | tf_op jit(solution)/shard_map/ppermute | solution.py:584
  80.6 6.8 %collective-permute-start.14 = (f32[1,128,256]{2,1,0:T(8,128)S(1)}, f32[1,128,256]{2,1,0:T(8,128)S(1)}, u32[]{:S(2)}, u32[]{:S(2)}) collective-permute-start(f32[1,128,256]{2,1,0:T(8,128)S(1)} %collect_points.7), channel_id=1, source_target_pairs={{0,24},{4,28},{8,16},{12,20},{16,8},{20,12},{24,0},{28,4},{1,25},{... | collective-permute-start | bytes 393224 | tf_op jit(solution)/shard_map/ppermute | solution.py:584

commit v7 on v6

--- a/solution.py
+++ b/solution.py
@@ -95,7 +95,7 @@
 
 
 def sort_kernel(
-    planes, m_hbm, c_hbm, out_ref, d_ref, acc_ref, val_ref, gb_ref, cum_ref, tot_ref, lane_ref, m_ref, c_ref, sems
+    planes, m_hbm, c_hbm, out_ref, d_ref, both_ref, acc_ref, val_ref, gb_ref, cum_ref, tot_ref, lane_ref, m_ref, c_ref, sems
 ):
     rows = gb_ref.shape[0]
     fetch_m = pltpu.make_async_copy(m_hbm, m_ref, sems.at[0])
@@ -185,8 +185,11 @@
 
     lax.fori_loop(0, rows // 8, body, 0)
     got = [acc_ref[q * rows : (q + 1) * rows] for q in range(7)]
-    out_ref[0:rows] = got[0] + got[1]
-    out_ref[rows : 2 * rows] = got[2] + got[3]
+    both_ref[0:2] = c_ref[...]
+    for q in range(2):
+        value = got[2 * q] + got[2 * q + 1]
+        out_ref[q * rows : (q + 1) * rows] = value
+        both_ref[2 + q] = unfold(value)
     out_ref[2 * rows : 3 * rows] = (got[4] * planes + got[5]) * LANES + got[6]
     out_ref[3 * rows : 3 * rows + 8] = plane_of
 
@@ -225,12 +228,8 @@
     return 1.0 - 2.0 * s * s, 2.0 * s * c
 
 
-def powers(freq, w_ref):
-    s, c = sin_cos(freq * (2.0 * math.pi / N))
-    for q in range(4):
-        w_ref[4 + 2 * q] = c
-        w_ref[5 + 2 * q] = s
-        s, c = 2.0 * s * c, c * c - s * s
+def times(a, b):
+    return a[0] * b[0] - a[1] * b[1], a[0] * b[1] + a[1] * b[0]
 
 
 def firsts(planes):
@@ -250,18 +249,20 @@
     return jnp.broadcast_to(ref[index, pl.ds(c, 1), :], (8, CHUNK))
 
 
-def rise(w_ref, c):
-    k = lax.broadcasted_iota(jnp.int32, (8, CHUNK), 0)
-    er = ei = None
-    for bit in range(3):
-        on = (k & (1 << bit)) != 0
-        fr = jnp.where(on, row_of(w_ref, 4 + 2 * bit, c), 1.0)
-        fi = jnp.where(on, row_of(w_ref, 5 + 2 * bit, c), 0.0)
-        if er is None:
-            er, ei = fr, fi
-        else:
-            er, ei = er * fr - ei * fi, er * fi + ei * fr
-    return er, ei
+def rise(e_ref, start, turn):
+    rows = turn[0].shape[0]
+    value = start
+    for k in range(8):
+        for p in range(2):
+            for q in range(2):
+                e_ref[p, q, pl.ds(k, rows, stride=8), :] = value[p][:, q * LANES : (q + 1) * LANES]
+        if k < 7:
+            value = times(value, turn)
+
+
+def risen(e_ref, c):
+    where = pl.ds(pl.multiple_of(c * 8, 8), 8)
+    return tuple(jnp.concatenate([e_ref[p, 0, where, :], e_ref[p, 1, where, :]], axis=1) for p in range(2))
 
 
 def prepare(planes, cell, w_ref, code_ref, id_ref):
@@ -269,19 +270,22 @@
     code_ref[0] = gb
     code_ref[1] = gc
     id_ref[...] = ident(LANES)
-    for q, first in enumerate(firsts(planes)):
-        w_ref[2 * q], w_ref[2 * q + 1] = phase(freq, first)
-    powers(freq, w_ref)
-
-
-def spread_kernel(planes, height, unroll, slab_ref, steps_ref, own_ref, sib_ref, w_ref, code_ref, id_ref):
+    s, c = sin_cos(freq * (2.0 * math.pi / N))
+    turn = eight = (c, s)
+    for _ in range(3):
+        eight = times(eight, eight)
+    w_ref[0], w_ref[1] = eight
+    return turn, [phase(freq, first) for first in firsts(planes)]
+
+
+def spread_kernel(
+    planes, height, unroll, slab_ref, steps_ref, own_ref, sib_ref, w_ref, code_ref, id_ref, e0_ref, e1_ref
+):
     rows = w_ref.shape[1]
-    prepare(planes, slab_ref[0, 2 * rows : 3 * rows], w_ref, code_ref, id_ref)
-    re, im = slab_ref[0, 0:rows], slab_ref[0, rows : 2 * rows]
-    for q in range(2):
-        sr, si = w_ref[2 * q], w_ref[2 * q + 1]
-        w_ref[2 * q] = re * sr - im * si
-        w_ref[2 * q + 1] = re * si + im * sr
+    turn, starts = prepare(planes, slab_ref[0, 2 * rows : 3 * rows], w_ref, code_ref, id_ref)
+    value = slab_ref[0, 0:rows], slab_ref[0, rows : 2 * rows]
+    for e_ref, start in zip((e0_ref, e1_ref), starts):
+        rise(e_ref, times(value, start), turn)
     own_ref[...] = jnp.zeros_like(own_ref)
     sib_ref[...] = jnp.zeros_like(sib_ref)
 
@@ -289,17 +293,15 @@
         ids = id_ref[...]
         for j in range(unroll):
             g, c, code = pair_code(planes, steps_ref, code_ref, rows, i * unroll + j)
-            er, ei = rise(w_ref, c)
-            jr, ji = row_of(w_ref, 10, c), row_of(w_ref, 11, c)
+            eight = row_of(w_ref, 0, c), row_of(w_ref, 1, c)
             lines = []
-            for q in range(2):
-                zr, zi = row_of(w_ref, 2 * q, c), row_of(w_ref, 2 * q + 1, c)
-                zr, zi = er * zr - ei * zi, er * zi + ei * zr
-                real, imag = [zr], [zi]
+            for e_ref in (e0_ref, e1_ref):
+                z = risen(e_ref, c)
+                real, imag = [z[0]], [z[1]]
                 for _ in range(height // 8 - 1):
-                    zr, zi = zr * jr - zi * ji, zr * ji + zi * jr
-                    real.append(zr)
-                    imag.append(zi)
+                    z = times(z, eight)
+                    real.append(z[0])
+                    imag.append(z[1])
                 lines += real + imag
             high, low = split(jnp.concatenate(lines, axis=0))
             got = lax.dot_general(
@@ -315,10 +317,13 @@
 
 
 def collect_kernel(
-    planes, height, unroll, slab_ref, steps_ref, own_ref, sib_ref, h_ref, w_ref, code_ref, id_ref, u2_ref
+    planes, height, unroll, slab_ref, steps_ref, own_ref, sib_ref, h_ref, w_ref, code_ref, id_ref, e_ref, u2_ref
 ):
     rows = w_ref.shape[1]
-    prepare(planes, slab_ref[0, 2 * rows : 3 * rows], w_ref, code_ref, id_ref)
+    turn, starts = prepare(planes, slab_ref[0, 2 * rows : 3 * rows], w_ref, code_ref, id_ref)
+    for q, start in enumerate(starts):
+        w_ref[2 + 2 * q], w_ref[3 + 2 * q] = start
+    rise(e_ref, (jnp.ones_like(turn[0]), jnp.zeros_like(turn[0])), turn)
     for g in range(planes):
         where = slice(g * 2 * height, (g + 1) * 2 * height)
         high, low = split(jnp.concatenate([own_ref[0, where, :], sib_ref[0, where, :]], axis=0))
@@ -331,7 +336,7 @@
             g, c, code = pair_code(planes, steps_ref, code_ref, rows, i * unroll + j)
             got = mm(u2_ref[g], one_hot(code, ids))
             got = got[: 4 * height] + got[4 * height :]
-            jr, ji = row_of(w_ref, 10, c), row_of(w_ref, 11, c)
+            jr, ji = row_of(w_ref, 0, c), row_of(w_ref, 1, c)
             hr = hi = 0.0
             for q in range(2):
                 value = got[q * 2 * height : (q + 1) * 2 * height]
@@ -342,9 +347,9 @@
                         ar * jr + ai * ji + value[8 * t : 8 * t + 8],
                         ai * jr - ar * ji + value[height + 8 * t : height + 8 * t + 8],
                     )
-                zr, zi = row_of(w_ref, 2 * q, c), row_of(w_ref, 2 * q + 1, c)
+                zr, zi = row_of(w_ref, 2 + 2 * q, c), row_of(w_ref, 3 + 2 * q, c)
                 hr, hi = hr + ar * zr + ai * zi, hi + ai * zr - ar * zi
-            er, ei = rise(w_ref, c)
+            er, ei = risen(e_ref, c)
             h_ref[0, pl.ds(c, 1), :] += jnp.sum(hr * er + hi * ei, axis=0, keepdims=True)
             h_ref[0, pl.ds(rows + c, 1), :] += jnp.sum(hi * er - hr * ei, axis=0, keepdims=True)
         return carry
@@ -463,16 +468,28 @@
                 copy.wait()
 
 
-def unsort_kernel(arrivals, bands, *refs):
-    recv_refs = refs[:arrivals]
-    d_ref, *coef_refs = refs[arrivals : arrivals + 1 + bands]
-    h_ref, part_ref, hl_ref, wide_ref = refs[arrivals + 1 + bands :]
-    rows = d_ref.shape[0]
+def sum_kernel(arrivals, *refs):
+    recv_refs, coef_refs, (total_ref, part_ref) = refs[:arrivals], refs[arrivals:-2], refs[-2:]
     total = None
     for recv in recv_refs:
         for s in range(recv.shape[0]):
             total = recv[s] if total is None else total + recv[s]
-    high, low = split(total)
+    total_ref[...] = total
+    rows = total.shape[0] // 2
+    hr, hi = unfold(total[:rows]), unfold(total[rows:])
+    real, imag = [], []
+    for coef in coef_refs:
+        cr, ci = coef[2], coef[3]
+        real.append(jnp.sum(cr * hr + ci * hi, axis=0, keepdims=True))
+        imag.append(jnp.sum(cr * hi - ci * hr, axis=0, keepdims=True))
+    sums = jnp.concatenate(real + imag, axis=0)
+    for s in range(part_ref.shape[0]):
+        part_ref[s] = sums
+
+
+def unsort_kernel(total_ref, d_ref, h_ref, hl_ref, wide_ref):
+    rows = d_ref.shape[0]
+    high, low = split(total_ref[...])
     hl_ref[0 : 2 * rows] = high
     hl_ref[2 * rows :] = low
     hi_id = lax.broadcasted_iota(jnp.int32, (rows, CHUNK), 0).astype(F32)
@@ -495,25 +512,22 @@
         return carry
 
     lax.fori_loop(0, rows // 8, body, 0)
-    hr, hi = unfold(wide_ref[0]), unfold(wide_ref[1])
-    h_ref[0] = hr
-    h_ref[1] = hi
-    real, imag = [], []
-    for coef in coef_refs:
-        cr, ci = coef[0], coef[1]
-        real.append(jnp.sum(cr * hr + ci * hi, axis=0, keepdims=True))
-        imag.append(jnp.sum(cr * hi - ci * hr, axis=0, keepdims=True))
-    sums = jnp.concatenate(real + imag, axis=0)
-    for s in range(part_ref.shape[0]):
-        part_ref[s] = sums
-
-
-def residual_kernel(scale, bands, sum_ref, h_ref, *refs):
-    coef_refs, (out_ref, sub_ref) = refs[:bands], refs[bands:]
+    h_ref[0] = unfold(wide_ref[0])
+    h_ref[1] = unfold(wide_ref[1])
+
+
+def residual_kernel(scale, bands, h_ref, *refs):
+    coef_refs, sum_refs, (out_ref, sub_ref, all_ref) = refs[:bands], refs[bands:-3], refs[-3:]
     band = lax.axis_index("band")
-    sub = sum_ref[0]
-    for s in range(1, sum_ref.shape[0]):
-        sub = sub + sum_ref[s]
+    me = lax.axis_index("grid")
+    if len(sum_refs) > 1:
+        for bits, part in enumerate(sum_refs):
+            all_ref[me ^ bits] = part[0]
+    else:
+        all_ref[...] = sum_refs[0][...]
+    sub = all_ref[0]
+    for s in range(1, all_ref.shape[0]):
+        sub = sub + all_ref[s]
     sub = jnp.sum(sub, axis=1, keepdims=True) * scale
     lane = lax.broadcasted_iota(jnp.int32, (1, LANES), 1)
     hr, hi = h_ref[0], h_ref[1]
@@ -557,12 +571,13 @@
     anywhere = pl.BlockSpec(memory_space=pl.ANY)
     coef = coefficients.reshape(2, 2 * rows, LANES)
     table_rows = 3 * rows + 8
-    sorted_pts, dest = pl.pallas_call(
+    sorted_pts, dest, both = pl.pallas_call(
         functools.partial(sort_kernel, planes),
         in_specs=[pl.BlockSpec(memory_space=pltpu.HBM)] * 2,
         out_shape=(
             jax.ShapeDtypeStruct((table_rows, CHUNK), F32),
             jax.ShapeDtypeStruct((rows, CHUNK), F32),
+            jax.ShapeDtypeStruct((4, 2 * rows, LANES), F32),
         ),
         scratch_shapes=[
             pltpu.VMEM((7 * rows, CHUNK), F32),
@@ -594,14 +609,15 @@
     slab_spec = pl.BlockSpec((1, table_rows, CHUNK), lambda s: (s, 0, 0))
     steps_spec = pl.BlockSpec((None, 8, CHUNK), lambda s: (s, table_rows // 8 - 1, 0), memory_space=pltpu.SMEM)
     block_spec = pl.BlockSpec((1, lines, LANES), lambda s: (s, 0, 0))
-    point_scratch = [pltpu.VMEM((12, rows, CHUNK), F32), pltpu.VMEM((2, rows, CHUNK), F32), pltpu.VMEM((LANES, LANES), BF)]
+    point_scratch = [pltpu.VMEM((6, rows, CHUNK), F32), pltpu.VMEM((2, rows, CHUNK), F32), pltpu.VMEM((LANES, LANES), BF)]
+    risen_scratch = pltpu.VMEM((2, 2, 8 * rows, LANES), F32)
     spread = pl.pallas_call(
         functools.partial(spread_kernel, planes, height, unroll),
         grid=(per_call,),
         in_specs=[slab_spec, steps_spec],
         out_specs=(block_spec, block_spec),
         out_shape=(jax.ShapeDtypeStruct((per_call, lines, LANES), F32),) * 2,
-        scratch_shapes=point_scratch,
+        scratch_shapes=point_scratch + [risen_scratch] * 2,
         compiler_params=params(20),
         cost_estimate=cost(8e9),
         name="spread_points",
@@ -617,8 +633,8 @@
     cells = potential if height == planes else jnp.pad(potential, ((0, height - planes), (0, 0)))
     cells = cells.reshape(height // 8, 8, N * N // LANES, LANES).transpose(0, 2, 1, 3)
     cells = cells.reshape(height // 8, N // 2, 3, 8, LANES)
-    *sib, mine = lax.optimization_barrier((*sib, coef))
-    coefs = [coef]
+    *sib, mine = lax.optimization_barrier((*sib, both))
+    coefs = [both]
     for shift in range(1, bands):
         coefs.append(lax.ppermute(mine, "band", [(i, (i + shift) % bands) for i in range(bands)]))
     constants = [jnp.asarray(t) for t in tables()]
@@ -668,7 +684,7 @@
                 in_specs=[slab_spec, steps_spec, block_at(first), block_at(part.index(first))],
                 out_specs=pl.BlockSpec((1, 2 * rows, CHUNK), lambda s: (s, 0, 0)),
                 out_shape=jax.ShapeDtypeStruct((per_call, 2 * rows, CHUNK), F32),
-                scratch_shapes=point_scratch + [pltpu.VMEM((planes, 8 * height, LANES), BF)],
+                scratch_shapes=point_scratch + [risen_scratch, pltpu.VMEM((planes, 8 * height, LANES), BF)],
                 compiler_params=params(24),
                 cost_estimate=cost(8e9),
                 name="collect_points",
@@ -681,28 +697,40 @@
         blocks = jnp.take(partial[0], (ids ^ me) // 2, axis=0)
         blocks = jnp.where(((ids ^ me) % 2 == 0)[:, None, None], blocks, 0.0)
         arrived = [lax.all_to_all(blocks, "grid", split_axis=0, concat_axis=0, tiled=True)]
-    applied, part = pl.pallas_call(
-        functools.partial(unsort_kernel, len(arrived), bands),
+    direct = slabs <= 8
+    total, part = pl.pallas_call(
+        functools.partial(sum_kernel, len(arrived)),
         out_shape=(
-            jax.ShapeDtypeStruct((2, 2 * rows, LANES), F32),
-            jax.ShapeDtypeStruct((slabs, 2 * bands, LANES), F32),
+            jax.ShapeDtypeStruct((2 * rows, CHUNK), F32),
+            jax.ShapeDtypeStruct((1 if direct else slabs, 2 * bands, LANES), F32),
         ),
+        compiler_params=params(16),
+        cost_estimate=cost(1e9),
+        name="sum_points",
+    )(*arrived, *coefs)
+    if direct:
+        sums = [part] + [swap(part, bits) for bits in range(1, slabs)]
+    else:
+        sums = [lax.all_to_all(part, "grid", split_axis=0, concat_axis=0, tiled=True)]
+    applied = pl.pallas_call(
+        unsort_kernel,
+        out_shape=jax.ShapeDtypeStruct((2, 2 * rows, LANES), F32),
         scratch_shapes=[pltpu.VMEM((4 * rows, CHUNK), BF), pltpu.VMEM((2, rows, CHUNK), F32)],
         compiler_params=params(12),
         cost_estimate=cost(6e9),
         name="unsort_points",
-    )(*arrived, dest, *coefs)
-    sums = lax.all_to_all(part, "grid", split_axis=0, concat_axis=0, tiled=True)
+    )(total, dest)
     resid, sub = pl.pallas_call(
         functools.partial(residual_kernel, 1.0 / (count * slabs), bands),
         out_shape=(
             jax.ShapeDtypeStruct((2, 2 * rows, LANES), F32),
             jax.ShapeDtypeStruct((2, 1, bands), F32),
         ),
+        scratch_shapes=[pltpu.VMEM((slabs, 2 * bands, LANES), F32)],
         compiler_params=params(8),
         cost_estimate=cost(2e9),
         name="residual",
-    )(sums, applied, *coefs)
+    )(applied, *coefs, *sums)
     return sub.transpose(0, 2, 1), resid.reshape(2, 1, count)
 
 

time: 99.7 us -> 99.6 us (level)
  blocking collectives: 7.43 us -> 0 us
  starting transfers between devices: 14.3 us -> 20.8 us
  Pallas kernels: 70.8 us -> 71.9 us
    all_to_all x1 -> x0, blocking collectives: 7.43 us -> none  [local(): sums = lax.all_to_all(part, 'grid', split_axis=0, concat_axis=0, tiled=True)]
    ppermute x12 -> x19, starting transfers between devices: 9.42 us -> 15.8 us  [swap(): return lax.ppermute(x, 'grid', [(i, i ^ bits) for i in range(slabs)])]
    ppermute x12 -> x19, waiting for transfers between devices: 6.12 us -> 5.82 us  [swap(): return lax.ppermute(x, 'grid', [(i, i ^ bits) for i in range(slabs)])]
    pallas_call x1 -> x2, Pallas kernels: 3.82 us -> 3.82 us  [the longest x1 3.7 us: local(): pl.pallas_call(unsort_kernel, out_shape=jax.ShapeDtypeStruct((2, 2 * rows...]
  transfers between devices with their start and end apart: 15 -> 22, of which waited for: 4 -> 4; matrix products, arithmetic and copies ran while one was open for 0% -> 0% of each run, Pallas kernels for 58% -> 63%
where the time goes in v7:
time: 99.6 us; the launch traced here: 99.4 us
  Pallas kernels  71.9 us (72%)
  starting transfers between devices  20.8 us (21%)
  waiting for transfers between devices  5.83 us (6%)
    pallas_call x1, Pallas kernels, local(): pl.pallas_call(functools.partial(potential_kernel, planes, calls, parts),...  23.2 us
    pallas_call x4, Pallas kernels, local(): mine, theirs = spread(points[call], points[call])  18.7 us
    pallas_call x4, Pallas kernels, local(): pl.pallas_call(functools.partial(collect_kernel, planes, height, unroll),...  17 us
    ppermute x19, starting transfers between devices, swap(): return lax.ppermute(x, 'grid', [(i, i ^ bits) for i in range(slabs)])  15.8 us
    pallas_call x1, Pallas kernels, local(): pl.pallas_call(functools.partial(sort_kernel, planes), in_specs=[pl.Block...  8.27 us
    ppermute x19, waiting for transfers between devices, swap(): return lax.ppermute(x, 'grid', [(i, i ^ bits) for i in range(slabs)])  5.82 us
    ppermute x3, starting transfers between devices, local(): lax.ppermute(mine, 'band', [(i, (i + shift) % bands) for i in range(bands)])  4.95 us
    pallas_call x1, Pallas kernels, local(): pl.pallas_call(unsort_kernel, out_shape=jax.ShapeDtypeStruct((2, 2 * rows...  3.7 us
  transfers between devices with their start and end apart: 22, of which 4 were waited for; matrix products, arithmetic and copies ran while one was open for 0% of the time, Pallas kernels for 63%

profile of v7, /device:TPU:0, one launch (start us, length us, event | category | flops | bytes accessed | tf_op | source)
XLA Modules:
  0.0 99.4 jit_solution(17948047018591126356)
XLA Ops:
  0.6 8.3 %sort_points.1 = (f32[200,256]{1,0:T(8,128)}, f32[64,256]{1,0:T(8,128)}, f32[4,128,128]{2,1,0:T(8,128)}) custom-call(s32[128,128]{1,0:T(8,128)} %bitcast.56, f32[2,128,128]{2,1,0:T(8,128)} %bitcast.55), custom_call_target="tpu_custom_call" | custom-call | flops 10000000000 | tf_op jit(solution)/shard_map/sort_points/pallas_call | solution.py:574
  8.9 3.0 %collective-permute-start.1 = (f32[200,256]{1,0:T(8,128)}, f32[200,256]{1,0:T(8,128)S(1)}, u32[]{:S(2)}, u32[]{:S(2)}) collective-permute-start(f32[200,256]{1,0:T(8,128)} %get-tuple-element.40), channel_id=1, source_target_pairs={{0,16},{4,20},{8,24},{12,28},{16,0},{20,4},{24,8},{28,12},{1,17},{... | collective-permute-start | bytes 614408 | tf_op jit(solution)/shard_map/ppermute | solution.py:599
  11.9 1.5 %collective-permute-start = (f32[200,256]{1,0:T(8,128)}, f32[200,256]{1,0:T(8,128)S(1)}, u32[]{:S(2)}, u32[]{:S(2)}) collective-permute-start(f32[200,256]{1,0:T(8,128)} %get-tuple-element.40), channel_id=1, source_target_pairs={{0,8},{4,12},{8,0},{12,4},{16,24},{20,28},{24,16},{28,20},{1,9},{5... | collective-permute-start | bytes 614408 | tf_op jit(solution)/shard_map/ppermute | solution.py:599
  13.4 4.9 %spread_points.4 = (f32[1,1152,128]{2,1,0:T(8,128)S(1)}, f32[1,1152,128]{2,1,0:T(8,128)S(1)}) custom-call(f32[1,200,256]{2,1,0:T(8,128)} %bitcast.2.slab_ref.steps_ref, f32[1,200,256]{2,1,0:T(8,128)} %bitcast.2.slab_ref.steps_ref), custom_call_target="tpu_custom_call" | custom-call | flops 8000000000 | tf_op jit(solution)/shard_map/spread_points/pallas_call | solution.py:627
  18.7 4.6 %spread_points.5 = (f32[1,1152,128]{2,1,0:T(8,128)S(1)}, f32[1,1152,128]{2,1,0:T(8,128)S(1)}) custom-call(f32[1,200,256]{2,1,0:T(8,128)S(1)} %bitcast.42, f32[1,200,256]{2,1,0:T(8,128)S(1)} %bitcast.43), custom_call_target="tpu_custom_call" | custom-call | flops 8000000000 | tf_op jit(solution)/shard_map/spread_points/pallas_call | solution.py:627
  23.6 4.6 %spread_points.6 = (f32[1,1152,128]{2,1,0:T(8,128)S(1)}, f32[1,1152,128]{2,1,0:T(8,128)S(1)}) custom-call(f32[1,200,256]{2,1,0:T(8,128)S(1)} %bitcast.34, f32[1,200,256]{2,1,0:T(8,128)S(1)} %bitcast.35), custom_call_target="tpu_custom_call" | custom-call | flops 8000000000 | tf_op jit(solution)/shard_map/spread_points/pallas_call | solution.py:627
  28.6 4.6 %spread_points.7 = (f32[1,1152,128]{2,1,0:T(8,128)S(1)}, f32[1,1152,128]{2,1,0:T(8,128)S(1)}) custom-call(f32[1,200,256]{2,1,0:T(8,128)S(1)} %bitcast.38, f32[1,200,256]{2,1,0:T(8,128)S(1)} %bitcast.39), custom_call_target="tpu_custom_call" | custom-call | flops 8000000000 | tf_op jit(solution)/shard_map/spread_points/pallas_call | solution.py:627
  33.6 1.7 %collective-permute-done.6 = f32[1,1152,128]{2,1,0:T(8,128)S(1)} collective-permute-done((f32[1,1152,128]{2,1,0:T(8,128)S(1)}, f32[1,1152,128]{2,1,0:T(8,128)S(1)}, u32[]{:S(2)}, u32[]{:S(2)}) %collective-permute-start.6) | collective-permute-done | bytes 589856 | tf_op jit(solution)/shard_map/ppermute | solution.py:599
  35.3 3.9 %collective-permute-start.9 = (f32[4,128,128]{2,1,0:T(8,128)S(1)}, f32[4,128,128]{2,1,0:T(8,128)S(1)}, u32[]{:S(2)}, u32[]{:S(2)}) collective-permute-start(f32[4,128,128]{2,1,0:T(8,128)S(1)} %copy-done), channel_id=1, source_target_pairs={{0,3},{1,0},{2,1},{3,2},{4,7},{5,4},{6,5},{7,6},{8,11},{9,8},{10,9... | collective-permute-start | bytes 786440 | tf_op jit(solution)/shard_map/ppermute | solution.py:639
  39.2 1.0 %collective-permute-start.7 = (f32[4,128,128]{2,1,0:T(8,128)S(1)}, f32[4,128,128]{2,1,0:T(8,128)S(1)}, u32[]{:S(2)}, u32[]{:S(2)}) collective-permute-start(f32[4,128,128]{2,1,0:T(8,128)S(1)} %copy-done), channel_id=1, source_target_pairs={{0,1},{1,2},{2,3},{3,0},{4,5},{5,6},{6,7},{7,4},{8,9},{9,10},{10,1... | collective-permute-start | bytes 786440 | tf_op jit(solution)/shard_map/ppermute | solution.py:639
  40.2 23.2 %apply_potential.1 = (f32[4,24,2,3,8,128]{5,4,3,2,1,0:T(8,128)S(1)}, f32[1,24,2,3,8,128]{5,4,3,2,1,0:T(8,128)S(1)}, f32[3,24,2,3,8,128]{5,4,3,2,1,0:T(8,128)S(1)}) custom-call(f32[1,24,2,3,8,128]{5,4,3,2,1,0:T(8,128)S(1)} %bitcast.50, f32[1,24,2,3,8,128]{5,4,3,2,1,0:T(8,128)S(1)} %bitcast.51, f32[1,24,2,3,8,128]{5,4,3,2,1,0:T(8,128)S(1)} %bitcast.52, ...), custom_call_target="tpu_custom_call" | custom-call | flops 40000000000 | tf_op jit(solution)/shard_map/apply_potential/pallas_call | solution.py:643
  63.6 2.0 %collective-permute-done.10 = f32[1,24,2,3,8,128]{5,4,3,2,1,0:T(8,128)S(1)} collective-permute-done((f32[1,24,2,3,8,128]{5,4,3,2,1,0:T(8,128)S(1)}, f32[1,24,2,3,8,128]{5,4,3,2,1,0:T(8,128)S(1)}, u32[]{:S(2)}, u32[]{:S(2)}) %collective-permute-start.10) | collective-permute-done | bytes 589856 | tf_op jit(solution)/shard_map/ppermute | solution.py:599
  65.7 4.1 %collect_points.5 = f32[1,128,256]{2,1,0:T(8,128)S(1)} custom-call(f32[1,200,256]{2,1,0:T(8,128)S(1)} %bitcast.44, f32[1,200,256]{2,1,0:T(8,128)S(1)} %bitcast.45, f32[4,1152,128]{2,1,0:T(8,128)S(1)} %bitcast.46, f32[1,1152,128]{2,1,0:T(8,128)S(1)} %bitcast.33), custom_call_target="tpu_custom_call" | custom-call | flops 8000000000 | tf_op jit(solution)/shard_map/collect_points/pallas_call | solution.py:681
  69.9 1.6 %collective-permute-start.12 = (f32[1,128,256]{2,1,0:T(8,128)S(1)}, f32[1,128,256]{2,1,0:T(8,128)S(1)}, u32[]{:S(2)}, u32[]{:S(2)}) collective-permute-start(f32[1,128,256]{2,1,0:T(8,128)S(1)} %collect_points.5), channel_id=1, source_target_pairs={{0,8},{4,12},{8,0},{12,4},{16,24},{20,28},{24,16},{28,20},{1,9},{5... | collective-permute-start | bytes 393224 | tf_op jit(solution)/shard_map/ppermute | solution.py:599
  71.4 4.1 %collect_points.7 = f32[1,128,256]{2,1,0:T(8,128)S(1)} custom-call(f32[1,200,256]{2,1,0:T(8,128)S(1)} %bitcast.40, f32[1,200,256]{2,1,0:T(8,128)S(1)} %bitcast.41, f32[4,1152,128]{2,1,0:T(8,128)S(1)} %bitcast.47, f32[3,1152,128]{2,1,0:T(8,128)S(1)} %bitcast.26), custom_call_target="tpu_custom_call" | custom-call | flops 8000000000 | tf_op jit(solution)/shard_map/collect_points/pallas_call | solution.py:681
  75.6 4.3 %collect_points.6 = f32[1,128,256]{2,1,0:T(8,128)S(1)} custom-call(f32[1,200,256]{2,1,0:T(8,128)S(1)} %bitcast.36, f32[1,200,256]{2,1,0:T(8,128)S(1)} %bitcast.37, f32[4,1152,128]{2,1,0:T(8,128)S(1)} %bitcast.48, f32[3,1152,128]{2,1,0:T(8,128)S(1)} %bitcast.27), custom_call_target="tpu_custom_call" | custom-call | flops 8000000000 | tf_op jit(solution)/shard_map/collect_points/pallas_call | solution.py:681
  79.9 1.6 %collective-permute-start.13 = (f32[1,128,256]{2,1,0:T(8,128)S(1)}, f32[1,128,256]{2,1,0:T(8,128)S(1)}, u32[]{:S(2)}, u32[]{:S(2)}) collective-permute-start(f32[1,128,256]{2,1,0:T(8,128)S(1)} %collect_points.6), channel_id=1, source_target_pairs={{0,16},{4,20},{8,24},{12,28},{16,0},{20,4},{24,8},{28,12},{1,17},{... | collective-permute-start | bytes 393224 | tf_op jit(solution)/shard_map/ppermute | solution.py:599
  82.0 4.4 %collect_points.4.refs_0_ = f32[1,128,256]{2,1,0:T(8,128)S(1)} custom-call(f32[1,200,256]{2,1,0:T(8,128)} %bitcast.2.slab_ref.steps_ref, f32[1,200,256]{2,1,0:T(8,128)} %bitcast.2.slab_ref.steps_ref, f32[4,1152,128]{2,1,0:T(8,128)S(1)} %bitcast.49, f32[3,1152,128]{2,1,0:T(8,128)S(1)} %bitcast.28), custom_call_target="tpu_custom_call" | custom-call | flops 8000000000 | tf_op jit(solution)/shard_map/collect_points/pallas_call | solution.py:681
  86.4 1.9 %collective-permute-done.13.refs_2_ = f32[1,128,256]{2,1,0:T(8,128)S(1)} collective-permute-done((f32[1,128,256]{2,1,0:T(8,128)S(1)}, f32[1,128,256]{2,1,0:T(8,128)S(1)}, u32[]{:S(2)}, u32[]{:S(2)}) %collective-permute-start.13) | collective-permute-done | bytes 131104 | tf_op jit(solution)/shard_map/ppermute | solution.py:599
  88.8 1.2 %collective-permute-start.20 = (f32[1,8,128]{2,1,0:T(8,128)S(1)}, f32[1,8,128]{2,1,0:T(8,128)S(1)}, u32[]{:S(2)}, u32[]{:S(2)}) collective-permute-start(f32[1,8,128]{2,1,0:T(8,128)S(1)} %get-tuple-element.65.refs_4_), channel_id=1, source_target_pairs={{0,24},{4,28},{8,16},{12,20},{16,8},{20,12},{24,0},{28,4},{1,25},{... | collective-permute-start | bytes 12296 | tf_op jit(solution)/shard_map/ppermute | solution.py:599
  90.0 2.3 %collective-permute-start.19 = (f32[1,8,128]{2,1,0:T(8,128)S(1)}, f32[1,8,128]{2,1,0:T(8,128)S(1)}, u32[]{:S(2)}, u32[]{:S(2)}) collective-permute-start(f32[1,8,128]{2,1,0:T(8,128)S(1)} %get-tuple-element.65.refs_4_), channel_id=1, source_target_pairs={{0,20},{4,16},{8,28},{12,24},{16,4},{20,0},{24,12},{28,8},{1,21},{... | collective-permute-start | bytes 12296 | tf_op jit(solution)/shard_map/ppermute | solution.py:599
  93.0 1.1 %collective-permute-start.16 = (f32[1,8,128]{2,1,0:T(8,128)S(1)}, f32[1,8,128]{2,1,0:T(8,128)S(1)}, u32[]{:S(2)}, u32[]{:S(2)}) collective-permute-start(f32[1,8,128]{2,1,0:T(8,128)S(1)} %get-tuple-element.65.refs_4_), channel_id=1, source_target_pairs={{0,8},{4,12},{8,0},{12,4},{16,24},{20,28},{24,16},{28,20},{1,9},{5... | collective-permute-start | bytes 12296 | tf_op jit(solution)/shard_map/ppermute | solution.py:599
  94.7 3.7 %unsort_points.1.h_ref = f32[2,128,128]{2,1,0:T(8,128)S(1)} custom-call(f32[128,256]{1,0:T(8,128)S(1)} %get-tuple-element.63.total_ref, f32[64,256]{1,0:T(8,128)S(1)} %copy-done.5), custom_call_target="tpu_custom_call" | custom-call | flops 6000000000 | tf_op jit(solution)/shard_map/unsort_points/pallas_call | solution.py:715
  98.5 0.9 residual.1
  (45 shorter events, 3.9 us)
Async XLA Ops:
  8.9 14.7 %collective-permute-start.1 = (f32[200,256]{1,0:T(8,128)}, f32[200,256]{1,0:T(8,128)S(1)}, u32[]{:S(2)}, u32[]{:S(2)}) collective-permute-start(f32[200,256]{1,0:T(8,128)} %get-tuple-element.40), channel_id=1, source_target_pairs={{0,16},{4,20},{8,24},{12,28},{16,0},{20,4},{24,8},{28,12},{1,17},{... | collective-permute-start | bytes 614408 | tf_op jit(solution)/shard_map/ppermute | solution.py:599
  11.9 6.7 %collective-permute-start = (f32[200,256]{1,0:T(8,128)}, f32[200,256]{1,0:T(8,128)S(1)}, u32[]{:S(2)}, u32[]{:S(2)}) collective-permute-start(f32[200,256]{1,0:T(8,128)} %get-tuple-element.40), channel_id=1, source_target_pairs={{0,8},{4,12},{8,0},{12,4},{16,24},{20,28},{24,16},{28,20},{1,9},{5... | collective-permute-start | bytes 614408 | tf_op jit(solution)/shard_map/ppermute | solution.py:599
  18.3 10.2 %collective-permute-start.2 = (f32[200,256]{1,0:T(8,128)}, f32[200,256]{1,0:T(8,128)S(1)}, u32[]{:S(2)}, u32[]{:S(2)}) collective-permute-start(f32[200,256]{1,0:T(8,128)} %get-tuple-element.40), channel_id=1, source_target_pairs={{0,24},{4,28},{8,16},{12,20},{16,8},{20,12},{24,0},{28,4},{1,25},{... | collective-permute-start | bytes 614408 | tf_op jit(solution)/shard_map/ppermute | solution.py:599
  18.4 15.1 %collective-permute-start.3 = (f32[1,1152,128]{2,1,0:T(8,128)S(1)}, f32[1,1152,128]{2,1,0:T(8,128)S(1)}, u32[]{:S(2)}, u32[]{:S(2)}) collective-permute-start(f32[1,1152,128]{2,1,0:T(8,128)S(1)} %get-tuple-element.42), channel_id=1, source_target_pairs={{0,4},{4,0},{8,12},{12,8},{16,20},{20,16},{24,28},{28,24},{1,5},{5... | collective-permute-start | bytes 1769480 | tf_op jit(solution)/shard_map/ppermute | solution.py:599
  23.3 10.2 %collective-permute-start.4 = (f32[1,1152,128]{2,1,0:T(8,128)S(1)}, f32[1,1152,128]{2,1,0:T(8,128)S(1)}, u32[]{:S(2)}, u32[]{:S(2)}) collective-permute-start(f32[1,1152,128]{2,1,0:T(8,128)S(1)} %get-tuple-element.43), channel_id=1, source_target_pairs={{0,4},{4,0},{8,12},{12,8},{16,20},{20,16},{24,28},{28,24},{1,5},{5... | collective-permute-start | bytes 1769480 | tf_op jit(solution)/shard_map/ppermute | solution.py:599
  28.2 5.3 %collective-permute-start.5 = (f32[1,1152,128]{2,1,0:T(8,128)S(1)}, f32[1,1152,128]{2,1,0:T(8,128)S(1)}, u32[]{:S(2)}, u32[]{:S(2)}) collective-permute-start(f32[1,1152,128]{2,1,0:T(8,128)S(1)} %get-tuple-element.44), channel_id=1, source_target_pairs={{0,4},{4,0},{8,12},{12,8},{16,20},{20,16},{24,28},{28,24},{1,5},{5... | collective-permute-start | bytes 1769480 | tf_op jit(solution)/shard_map/ppermute | solution.py:599
  28.6 11.7 %copy-start.1 = (bf16[384,1152]{1,0:T(8,128)(2,1)S(1)}, bf16[384,1152]{1,0:T(8,128)(2,1)}, u32[]{:S(2)}) copy-start(bf16[384,1152]{1,0:T(8,128)(2,1)} %constant.11.clone.refs_12_) | copy-start | bytes 2654212
  28.6 11.7 %copy-start.2 = (bf16[384,1152]{1,0:T(8,128)(2,1)S(1)}, bf16[384,1152]{1,0:T(8,128)(2,1)}, u32[]{:S(2)}) copy-start(bf16[384,1152]{1,0:T(8,128)(2,1)} %constant.8.clone.refs_9_) | copy-start | bytes 2654212
  33.2 2.1 %collective-permute-start.6 = (f32[1,1152,128]{2,1,0:T(8,128)S(1)}, f32[1,1152,128]{2,1,0:T(8,128)S(1)}, u32[]{:S(2)}, u32[]{:S(2)}) collective-permute-start(f32[1,1152,128]{2,1,0:T(8,128)S(1)} %get-tuple-element.45), channel_id=1, source_target_pairs={{0,4},{4,0},{8,12},{12,8},{16,20},{20,16},{24,28},{28,24},{1,5},{5... | collective-permute-start | bytes 1769480 | tf_op jit(solution)/shard_map/ppermute | solution.py:599
  35.3 28.2 %collective-permute-start.9 = (f32[4,128,128]{2,1,0:T(8,128)S(1)}, f32[4,128,128]{2,1,0:T(8,128)S(1)}, u32[]{:S(2)}, u32[]{:S(2)}) collective-permute-start(f32[4,128,128]{2,1,0:T(8,128)S(1)} %copy-done), channel_id=1, source_target_pairs={{0,3},{1,0},{2,1},{3,2},{4,7},{5,4},{6,5},{7,6},{8,11},{9,8},{10,9... | collective-permute-start | bytes 786440 | tf_op jit(solution)/shard_map/ppermute | solution.py:639
  39.2 24.3 %collective-permute-start.8 = (f32[4,128,128]{2,1,0:T(8,128)S(1)}, f32[4,128,128]{2,1,0:T(8,128)S(1)}, u32[]{:S(2)}, u32[]{:S(2)}) collective-permute-start(f32[4,128,128]{2,1,0:T(8,128)S(1)} %copy-done), channel_id=1, source_target_pairs={{0,2},{1,3},{2,0},{3,1},{4,6},{5,7},{6,4},{7,5},{8,10},{9,11},{10,... | collective-permute-start | bytes 786440 | tf_op jit(solution)/shard_map/ppermute | solution.py:639
  39.2 24.3 %collective-permute-start.7 = (f32[4,128,128]{2,1,0:T(8,128)S(1)}, f32[4,128,128]{2,1,0:T(8,128)S(1)}, u32[]{:S(2)}, u32[]{:S(2)}) collective-permute-start(f32[4,128,128]{2,1,0:T(8,128)S(1)} %copy-done), channel_id=1, source_target_pairs={{0,1},{1,2},{2,3},{3,0},{4,5},{5,6},{6,7},{7,4},{8,9},{9,10},{10,1... | collective-permute-start | bytes 786440 | tf_op jit(solution)/shard_map/ppermute | solution.py:639
  63.5 2.1 %collective-permute-start.10 = (f32[1,24,2,3,8,128]{5,4,3,2,1,0:T(8,128)S(1)}, f32[1,24,2,3,8,128]{5,4,3,2,1,0:T(8,128)S(1)}, u32[]{:S(2)}, u32[]{:S(2)}) collective-permute-start(f32[1,24,2,3,8,128]{5,4,3,2,1,0:T(8,128)S(1)} %get-tuple-element.55), channel_id=1, source_target_pairs={{0,4},{4,0},{8,12},{12,8},{16,20},{20,16},{24,28},{28,24},{1,5},{5... | collective-permute-start | bytes 1769480 | tf_op jit(solution)/shard_map/ppermute | solution.py:599
  65.6 5.8 %collective-permute-start.11 = (f32[3,24,2,3,8,128]{5,4,3,2,1,0:T(8,128)S(1)}, f32[3,24,2,3,8,128]{5,4,3,2,1,0:T(8,128)S(1)}, u32[]{:S(2)}, u32[]{:S(2)}) collective-permute-start(f32[3,24,2,3,8,128]{5,4,3,2,1,0:T(8,128)S(1)} %get-tuple-element.57), channel_id=1, source_target_pairs={{0,4},{4,0},{8,12},{12,8},{16,20},{20,16},{24,28},{28,24},{1,5},{5... | collective-permute-start | bytes 5308424 | tf_op jit(solution)/shard_map/ppermute | solution.py:599
  69.9 16.5 %collective-permute-start.12 = (f32[1,128,256]{2,1,0:T(8,128)S(1)}, f32[1,128,256]{2,1,0:T(8,128)S(1)}, u32[]{:S(2)}, u32[]{:S(2)}) collective-permute-start(f32[1,128,256]{2,1,0:T(8,128)S(1)} %collect_points.5), channel_id=1, source_target_pairs={{0,8},{4,12},{8,0},{12,4},{16,24},{20,28},{24,16},{28,20},{1,9},{5... | collective-permute-start | bytes 393224 | tf_op jit(solution)/shard_map/ppermute | solution.py:599
  79.9 8.4 %collective-permute-start.13 = (f32[1,128,256]{2,1,0:T(8,128)S(1)}, f32[1,128,256]{2,1,0:T(8,128)S(1)}, u32[]{:S(2)}, u32[]{:S(2)}) collective-permute-start(f32[1,128,256]{2,1,0:T(8,128)S(1)} %collect_points.6), channel_id=1, source_target_pairs={{0,16},{4,20},{8,24},{12,28},{16,0},{20,4},{24,8},{28,12},{1,17},{... | collective-permute-start | bytes 393224 | tf_op jit(solution)/shard_map/ppermute | solution.py:599
  81.5 6.8 %collective-permute-start.14 = (f32[1,128,256]{2,1,0:T(8,128)S(1)}, f32[1,128,256]{2,1,0:T(8,128)S(1)}, u32[]{:S(2)}, u32[]{:S(2)}) collective-permute-start(f32[1,128,256]{2,1,0:T(8,128)S(1)} %collect_points.7), channel_id=1, source_target_pairs={{0,24},{4,28},{8,16},{12,20},{16,8},{20,12},{24,0},{28,4},{1,25},{... | collective-permute-start | bytes 393224 | tf_op jit(solution)/shard_map/ppermute | solution.py:599
  88.4 4.6 %collective-permute-start.21 = (f32[1,8,128]{2,1,0:T(8,128)S(1)}, f32[1,8,128]{2,1,0:T(8,128)S(1)}, u32[]{:S(2)}, u32[]{:S(2)}) collective-permute-start(f32[1,8,128]{2,1,0:T(8,128)S(1)} %get-tuple-element.65.refs_4_), channel_id=1, source_target_pairs={{0,28},{4,24},{8,20},{12,16},{16,12},{20,8},{24,4},{28,0},{1,29},{... | collective-permute-start | bytes 12296 | tf_op jit(solution)/shard_map/ppermute | solution.py:599
  88.8 5.3 %collective-permute-start.20 = (f32[1,8,128]{2,1,0:T(8,128)S(1)}, f32[1,8,128]{2,1,0:T(8,128)S(1)}, u32[]{:S(2)}, u32[]{:S(2)}) collective-permute-start(f32[1,8,128]{2,1,0:T(8,128)S(1)} %get-tuple-element.65.refs_4_), channel_id=1, source_target_pairs={{0,24},{4,28},{8,16},{12,20},{16,8},{20,12},{24,0},{28,4},{1,25},{... | collective-permute-start | bytes 12296 | tf_op jit(solution)/shard_map/ppermute | solution.py:599
  90.0 8.4 %collective-permute-start.19 = (f32[1,8,128]{2,1,0:T(8,128)S(1)}, f32[1,8,128]{2,1,0:T(8,128)S(1)}, u32[]{:S(2)}, u32[]{:S(2)}) collective-permute-start(f32[1,8,128]{2,1,0:T(8,128)S(1)} %get-tuple-element.65.refs_4_), channel_id=1, source_target_pairs={{0,20},{4,16},{8,28},{12,24},{16,4},{20,0},{24,12},{28,8},{1,21},{... | collective-permute-start | bytes 12296 | tf_op jit(solution)/shard_map/ppermute | solution.py:599
  92.3 6.1 %collective-permute-start.18 = (f32[1,8,128]{2,1,0:T(8,128)S(1)}, f32[1,8,128]{2,1,0:T(8,128)S(1)}, u32[]{:S(2)}, u32[]{:S(2)}) collective-permute-start(f32[1,8,128]{2,1,0:T(8,128)S(1)} %get-tuple-element.65.refs_4_), channel_id=1, source_target_pairs={{0,16},{4,20},{8,24},{12,28},{16,0},{20,4},{24,8},{28,12},{1,17},{... | collective-permute-start | bytes 12296 | tf_op jit(solution)/shard_map/ppermute | solution.py:599
  92.9 5.6 %collective-permute-start.17 = (f32[1,8,128]{2,1,0:T(8,128)S(1)}, f32[1,8,128]{2,1,0:T(8,128)S(1)}, u32[]{:S(2)}, u32[]{:S(2)}) collective-permute-start(f32[1,8,128]{2,1,0:T(8,128)S(1)} %get-tuple-element.65.refs_4_), channel_id=1, source_target_pairs={{0,12},{4,8},{8,4},{12,0},{16,28},{20,24},{24,20},{28,16},{1,13},{... | collective-permute-start | bytes 12296 | tf_op jit(solution)/shard_map/ppermute | solution.py:599
  93.0 5.5 %collective-permute-start.16 = (f32[1,8,128]{2,1,0:T(8,128)S(1)}, f32[1,8,128]{2,1,0:T(8,128)S(1)}, u32[]{:S(2)}, u32[]{:S(2)}) collective-permute-start(f32[1,8,128]{2,1,0:T(8,128)S(1)} %get-tuple-element.65.refs_4_), channel_id=1, source_target_pairs={{0,8},{4,12},{8,0},{12,4},{16,24},{20,28},{24,16},{28,20},{1,9},{5... | collective-permute-start | bytes 12296 | tf_op jit(solution)/shard_map/ppermute | solution.py:599
  94.1 4.3 %collective-permute-start.15 = (f32[1,8,128]{2,1,0:T(8,128)S(1)}, f32[1,8,128]{2,1,0:T(8,128)S(1)}, u32[]{:S(2)}, u32[]{:S(2)}) collective-permute-start(f32[1,8,128]{2,1,0:T(8,128)S(1)} %get-tuple-element.65.refs_4_), channel_id=1, source_target_pairs={{0,4},{4,0},{8,12},{12,8},{16,20},{20,16},{24,28},{28,24},{1,5},{5... | collective-permute-start | bytes 12296 | tf_op jit(solution)/shard_map/ppermute | solution.py:599
  (4 other events, 38.4 us)

commit v8 on v6

--- a/solution.py
+++ b/solution.py
@@ -95,7 +95,7 @@
 
 
 def sort_kernel(
-    planes, m_hbm, c_hbm, out_ref, d_ref, acc_ref, val_ref, gb_ref, cum_ref, tot_ref, lane_ref, m_ref, c_ref, sems
+    planes, m_hbm, c_hbm, out_ref, d_ref, both_ref, acc_ref, val_ref, gb_ref, cum_ref, tot_ref, lane_ref, m_ref, c_ref, sems
 ):
     rows = gb_ref.shape[0]
     fetch_m = pltpu.make_async_copy(m_hbm, m_ref, sems.at[0])
@@ -185,8 +185,11 @@
 
     lax.fori_loop(0, rows // 8, body, 0)
     got = [acc_ref[q * rows : (q + 1) * rows] for q in range(7)]
-    out_ref[0:rows] = got[0] + got[1]
-    out_ref[rows : 2 * rows] = got[2] + got[3]
+    both_ref[0:2] = c_ref[...]
+    for q in range(2):
+        value = got[2 * q] + got[2 * q + 1]
+        out_ref[q * rows : (q + 1) * rows] = value
+        both_ref[2 + q] = unfold(value)
     out_ref[2 * rows : 3 * rows] = (got[4] * planes + got[5]) * LANES + got[6]
     out_ref[3 * rows : 3 * rows + 8] = plane_of
 
@@ -463,16 +466,28 @@
                 copy.wait()
 
 
-def unsort_kernel(arrivals, bands, *refs):
-    recv_refs = refs[:arrivals]
-    d_ref, *coef_refs = refs[arrivals : arrivals + 1 + bands]
-    h_ref, part_ref, hl_ref, wide_ref = refs[arrivals + 1 + bands :]
-    rows = d_ref.shape[0]
+def sum_kernel(arrivals, *refs):
+    recv_refs, coef_refs, (total_ref, part_ref) = refs[:arrivals], refs[arrivals:-2], refs[-2:]
     total = None
     for recv in recv_refs:
         for s in range(recv.shape[0]):
             total = recv[s] if total is None else total + recv[s]
-    high, low = split(total)
+    total_ref[...] = total
+    rows = total.shape[0] // 2
+    hr, hi = unfold(total[:rows]), unfold(total[rows:])
+    real, imag = [], []
+    for coef in coef_refs:
+        cr, ci = coef[2], coef[3]
+        real.append(jnp.sum(cr * hr + ci * hi, axis=0, keepdims=True))
+        imag.append(jnp.sum(cr * hi - ci * hr, axis=0, keepdims=True))
+    sums = jnp.concatenate(real + imag, axis=0)
+    for s in range(part_ref.shape[0]):
+        part_ref[s] = sums
+
+
+def unsort_kernel(total_ref, d_ref, h_ref, hl_ref, wide_ref):
+    rows = d_ref.shape[0]
+    high, low = split(total_ref[...])
     hl_ref[0 : 2 * rows] = high
     hl_ref[2 * rows :] = low
     hi_id = lax.broadcasted_iota(jnp.int32, (rows, CHUNK), 0).astype(F32)
@@ -495,25 +510,22 @@
         return carry
 
     lax.fori_loop(0, rows // 8, body, 0)
-    hr, hi = unfold(wide_ref[0]), unfold(wide_ref[1])
-    h_ref[0] = hr
-    h_ref[1] = hi
-    real, imag = [], []
-    for coef in coef_refs:
-        cr, ci = coef[0], coef[1]
-        real.append(jnp.sum(cr * hr + ci * hi, axis=0, keepdims=True))
-        imag.append(jnp.sum(cr * hi - ci * hr, axis=0, keepdims=True))
-    sums = jnp.concatenate(real + imag, axis=0)
-    for s in range(part_ref.shape[0]):
-        part_ref[s] = sums
-
-
-def residual_kernel(scale, bands, sum_ref, h_ref, *refs):
-    coef_refs, (out_ref, sub_ref) = refs[:bands], refs[bands:]
+    h_ref[0] = unfold(wide_ref[0])
+    h_ref[1] = unfold(wide_ref[1])
+
+
+def residual_kernel(scale, bands, h_ref, *refs):
+    coef_refs, sum_refs, (out_ref, sub_ref, all_ref) = refs[:bands], refs[bands:-3], refs[-3:]
     band = lax.axis_index("band")
-    sub = sum_ref[0]
-    for s in range(1, sum_ref.shape[0]):
-        sub = sub + sum_ref[s]
+    me = lax.axis_index("grid")
+    if len(sum_refs) > 1:
+        for j, part in enumerate(sum_refs):
+            all_ref[lax.div(me, 2) ^ j] = part[0]
+    else:
+        all_ref[...] = sum_refs[0][...]
+    sub = all_ref[0]
+    for s in range(1, all_ref.shape[0]):
+        sub = sub + all_ref[s]
     sub = jnp.sum(sub, axis=1, keepdims=True) * scale
     lane = lax.broadcasted_iota(jnp.int32, (1, LANES), 1)
     hr, hi = h_ref[0], h_ref[1]
@@ -557,12 +569,13 @@
     anywhere = pl.BlockSpec(memory_space=pl.ANY)
     coef = coefficients.reshape(2, 2 * rows, LANES)
     table_rows = 3 * rows + 8
-    sorted_pts, dest = pl.pallas_call(
+    sorted_pts, dest, both = pl.pallas_call(
         functools.partial(sort_kernel, planes),
         in_specs=[pl.BlockSpec(memory_space=pltpu.HBM)] * 2,
         out_shape=(
             jax.ShapeDtypeStruct((table_rows, CHUNK), F32),
             jax.ShapeDtypeStruct((rows, CHUNK), F32),
+            jax.ShapeDtypeStruct((4, 2 * rows, LANES), F32),
         ),
         scratch_shapes=[
             pltpu.VMEM((7 * rows, CHUNK), F32),
@@ -613,12 +626,15 @@
             sorted_pts, theirs = lax.optimization_barrier((sorted_pts, theirs))
             points.append(swap(sorted_pts, 6)[None])
         own.append(mine)
-        sib.append(swap(theirs, 1))
+        if call < calls - 1:
+            sib.append(swap(theirs, 1))
+    sent = theirs
     cells = potential if height == planes else jnp.pad(potential, ((0, height - planes), (0, 0)))
     cells = cells.reshape(height // 8, 8, N * N // LANES, LANES).transpose(0, 2, 1, 3)
     cells = cells.reshape(height // 8, N // 2, 3, 8, LANES)
-    *sib, mine = lax.optimization_barrier((*sib, coef))
-    coefs = [coef]
+    *sib, sent, mine = lax.optimization_barrier((*sib, sent, both))
+    sib.append(swap(sent, 1))
+    coefs = [both]
     for shift in range(1, bands):
         coefs.append(lax.ppermute(mine, "band", [(i, (i + shift) % bands) for i in range(bands)]))
     constants = [jnp.asarray(t) for t in tables()]
@@ -657,52 +673,68 @@
     def block_at(first):
         return pl.BlockSpec((1, lines, LANES), lambda s: (first + s, 0, 0))
 
-    partial = []
-    for call, table in enumerate(points):
+    partial = [None] * calls
+    for call in [*range(1, calls), 0]:
+        table = points[call]
+        if call == 0 and half == 4:
+            diagonal, table = lax.optimization_barrier((swap(partial[3], 6), table))
         first = call * per_call
         number, part = next((i, part) for i, part in enumerate(parts) if first in part)
-        partial.append(
-            pl.pallas_call(
-                functools.partial(collect_kernel, planes, height, unroll),
-                grid=(per_call,),
-                in_specs=[slab_spec, steps_spec, block_at(first), block_at(part.index(first))],
-                out_specs=pl.BlockSpec((1, 2 * rows, CHUNK), lambda s: (s, 0, 0)),
-                out_shape=jax.ShapeDtypeStruct((per_call, 2 * rows, CHUNK), F32),
-                scratch_shapes=point_scratch + [pltpu.VMEM((planes, 8 * height, LANES), BF)],
-                compiler_params=params(24),
-                cost_estimate=cost(8e9),
-                name="collect_points",
-            )(table, table, keep, other[number])
-        )
+        partial[call] = pl.pallas_call(
+            functools.partial(collect_kernel, planes, height, unroll),
+            grid=(per_call,),
+            in_specs=[slab_spec, steps_spec, block_at(first), block_at(part.index(first))],
+            out_specs=pl.BlockSpec((1, 2 * rows, CHUNK), lambda s: (s, 0, 0)),
+            out_shape=jax.ShapeDtypeStruct((per_call, 2 * rows, CHUNK), F32),
+            scratch_shapes=point_scratch + [pltpu.VMEM((planes, 8 * height, LANES), BF)],
+            compiler_params=params(24),
+            cost_estimate=cost(8e9),
+            name="collect_points",
+        )(table, table, keep, other[number])
     if half <= 4:
-        arrived = [partial[0]] + [swap(partial[j], 2 * j) for j in range(1, half)]
+        arrived = [partial[0]] + [swap(partial[j], 2 * j) for j in range(1, min(half, 3))]
+        if half == 4:
+            arrived.append(diagonal)
     else:
         ids = jnp.arange(slabs)
         blocks = jnp.take(partial[0], (ids ^ me) // 2, axis=0)
         blocks = jnp.where(((ids ^ me) % 2 == 0)[:, None, None], blocks, 0.0)
         arrived = [lax.all_to_all(blocks, "grid", split_axis=0, concat_axis=0, tiled=True)]
-    applied, part = pl.pallas_call(
-        functools.partial(unsort_kernel, len(arrived), bands),
+    direct = slabs <= 8
+    total, part = pl.pallas_call(
+        functools.partial(sum_kernel, len(arrived)),
         out_shape=(
-            jax.ShapeDtypeStruct((2, 2 * rows, LANES), F32),
-            jax.ShapeDtypeStruct((slabs, 2 * bands, LANES), F32),
+            jax.ShapeDtypeStruct((2 * rows, CHUNK), F32),
+            jax.ShapeDtypeStruct((1 if direct else slabs, 2 * bands, LANES), F32),
         ),
+        compiler_params=params(16),
+        cost_estimate=cost(1e9),
+        name="sum_points",
+    )(*arrived, *coefs)
+    if direct:
+        pair = part + swap(part, 1)
+        sums = [pair] + [swap(pair, 2 * j) for j in range(1, half)]
+    else:
+        sums = [lax.all_to_all(part, "grid", split_axis=0, concat_axis=0, tiled=True)]
+    applied = pl.pallas_call(
+        unsort_kernel,
+        out_shape=jax.ShapeDtypeStruct((2, 2 * rows, LANES), F32),
         scratch_shapes=[pltpu.VMEM((4 * rows, CHUNK), BF), pltpu.VMEM((2, rows, CHUNK), F32)],
         compiler_params=params(12),
         cost_estimate=cost(6e9),
         name="unsort_points",
-    )(*arrived, dest, *coefs)
-    sums = lax.all_to_all(part, "grid", split_axis=0, concat_axis=0, tiled=True)
+    )(total, dest)
     resid, sub = pl.pallas_call(
         functools.partial(residual_kernel, 1.0 / (count * slabs), bands),
         out_shape=(
             jax.ShapeDtypeStruct((2, 2 * rows, LANES), F32),
             jax.ShapeDtypeStruct((2, 1, bands), F32),
         ),
+        scratch_shapes=[pltpu.VMEM((half if direct else slabs, 2 * bands, LANES), F32)],
         compiler_params=params(8),
         cost_estimate=cost(2e9),
         name="residual",
-    )(sums, applied, *coefs)
+    )(applied, *coefs, *sums)
     return sub.transpose(0, 2, 1), resid.reshape(2, 1, count)
 
 

time: 99.7 us -> 94.9 us (0.952)
  blocking collectives: 7.43 us -> 0 us
  starting transfers between devices: 14.3 us -> 19.2 us
  waiting for transfers between devices: 6.13 us -> 3.62 us
    all_to_all x1 -> x0, blocking collectives: 7.43 us -> none  [local(): sums = lax.all_to_all(part, 'grid', split_axis=0, concat_axis=0, tiled=True)]
    ppermute x12 -> x16, starting transfers between devices: 9.42 us -> 13.3 us  [swap(): return lax.ppermute(x, 'grid', [(i, i ^ bits) for i in range(slabs)])]
    ppermute x12 -> x16, waiting for transfers between devices: 6.12 us -> 3.61 us  [swap(): return lax.ppermute(x, 'grid', [(i, i ^ bits) for i in range(slabs)])]
    ppermute x3, starting transfers between devices: 4.87 us -> 5.93 us  [local(): lax.ppermute(mine, 'band', [(i, (i + shift) % bands) for i in range(bands)])]
    pallas_call x1 -> x2, Pallas kernels: 3.82 us -> 3.81 us  [the longest x1 3.69 us: local(): pl.pallas_call(unsort_kernel, out_shape=jax.ShapeDtypeStruct((2, 2 * rows...]
  transfers between devices with their start and end apart: 15 -> 19, of which waited for: 4 -> 4; matrix products, arithmetic and copies ran while one was open for 0% -> 0% of each run, Pallas kernels for 58% -> 65%
where the time goes in v8:
time: 94.9 us; the launch traced here: 94.6 us
  Pallas kernels  70.9 us (75%)
  starting transfers between devices  19.2 us (20%)
  waiting for transfers between devices  3.62 us (4%)
    pallas_call x1, Pallas kernels, local(): pl.pallas_call(functools.partial(potential_kernel, planes, calls, parts),...  23.3 us
    pallas_call x4, Pallas kernels, local(): mine, theirs = spread(points[call], points[call])  18.3 us
    pallas_call x4, Pallas kernels, local(): pl.pallas_call(functools.partial(collect_kernel, planes, height, unroll),...  16.3 us
    ppermute x16, starting transfers between devices, swap(): return lax.ppermute(x, 'grid', [(i, i ^ bits) for i in range(slabs)])  13.3 us
    pallas_call x1, Pallas kernels, local(): pl.pallas_call(functools.partial(sort_kernel, planes), in_specs=[pl.Block...  8.27 us
    ppermute x3, starting transfers between devices, local(): lax.ppermute(mine, 'band', [(i, (i + shift) % bands) for i in range(bands)])  5.93 us
    pallas_call x1, Pallas kernels, local(): pl.pallas_call(unsort_kernel, out_shape=jax.ShapeDtypeStruct((2, 2 * rows...  3.69 us
    ppermute x16, waiting for transfers between devices, swap(): return lax.ppermute(x, 'grid', [(i, i ^ bits) for i in range(slabs)])  3.61 us
  transfers between devices with their start and end apart: 19, of which 4 were waited for; matrix products, arithmetic and copies ran while one was open for 0% of the time, Pallas kernels for 65%

profile of v8, /device:TPU:0, one launch (start us, length us, event | category | flops | bytes accessed | tf_op | source)
XLA Modules:
  0.0 94.6 jit_solution(2282898807227832315)
XLA Ops:
  0.6 8.3 %sort_points.1 = (f32[200,256]{1,0:T(8,128)}, f32[64,256]{1,0:T(8,128)}, f32[4,128,128]{2,1,0:T(8,128)}) custom-call(s32[128,128]{1,0:T(8,128)} %bitcast.56, f32[2,128,128]{2,1,0:T(8,128)} %bitcast.55), custom_call_target="tpu_custom_call" | custom-call | flops 10000000000 | tf_op jit(solution)/shard_map/sort_points/pallas_call | solution.py:572
  8.9 3.0 %collective-permute-start.1 = (f32[200,256]{1,0:T(8,128)}, f32[200,256]{1,0:T(8,128)S(1)}, u32[]{:S(2)}, u32[]{:S(2)}) collective-permute-start(f32[200,256]{1,0:T(8,128)} %get-tuple-element.39), channel_id=1, source_target_pairs={{0,8},{4,12},{8,0},{12,4},{16,24},{20,28},{24,16},{28,20},{1,9},{5... | collective-permute-start | bytes 614408 | tf_op jit(solution)/shard_map/ppermute | solution.py:597
  11.9 1.5 %collective-permute-start.2 = (f32[200,256]{1,0:T(8,128)}, f32[200,256]{1,0:T(8,128)S(1)}, u32[]{:S(2)}, u32[]{:S(2)}) collective-permute-start(f32[200,256]{1,0:T(8,128)} %get-tuple-element.39), channel_id=1, source_target_pairs={{0,16},{4,20},{8,24},{12,28},{16,0},{20,4},{24,8},{28,12},{1,17},{... | collective-permute-start | bytes 614408 | tf_op jit(solution)/shard_map/ppermute | solution.py:597
  13.4 4.8 %spread_points.4 = (f32[1,1152,128]{2,1,0:T(8,128)S(1)}, f32[1,1152,128]{2,1,0:T(8,128)S(1)}) custom-call(f32[1,200,256]{2,1,0:T(8,128)} %bitcast.2.slab_ref.steps_ref, f32[1,200,256]{2,1,0:T(8,128)} %bitcast.2.slab_ref.steps_ref), custom_call_target="tpu_custom_call" | custom-call | flops 8000000000 | tf_op jit(solution)/shard_map/spread_points/pallas_call | solution.py:624
  18.4 4.5 %spread_points.5 = (f32[1,1152,128]{2,1,0:T(8,128)S(1)}, f32[1,1152,128]{2,1,0:T(8,128)S(1)}) custom-call(f32[1,200,256]{2,1,0:T(8,128)S(1)} %bitcast.38, f32[1,200,256]{2,1,0:T(8,128)S(1)} %bitcast.39), custom_call_target="tpu_custom_call" | custom-call | flops 8000000000 | tf_op jit(solution)/shard_map/spread_points/pallas_call | solution.py:624
  23.5 4.5 %spread_points.6 = (f32[1,1152,128]{2,1,0:T(8,128)S(1)}, f32[1,1152,128]{2,1,0:T(8,128)S(1)}) custom-call(f32[1,200,256]{2,1,0:T(8,128)S(1)} %bitcast.34, f32[1,200,256]{2,1,0:T(8,128)S(1)} %bitcast.35), custom_call_target="tpu_custom_call" | custom-call | flops 8000000000 | tf_op jit(solution)/shard_map/spread_points/pallas_call | solution.py:624
  28.1 4.5 %spread_points.7 = (f32[1,1152,128]{2,1,0:T(8,128)S(1)}, f32[1,1152,128]{2,1,0:T(8,128)S(1)}) custom-call(f32[1,200,256]{2,1,0:T(8,128)S(1)} %bitcast.42, f32[1,200,256]{2,1,0:T(8,128)S(1)} %bitcast.43), custom_call_target="tpu_custom_call" | custom-call | flops 8000000000 | tf_op jit(solution)/shard_map/spread_points/pallas_call | solution.py:624
  33.2 2.0 %collective-permute-start.7 = (f32[4,128,128]{2,1,0:T(8,128)S(1)}, f32[4,128,128]{2,1,0:T(8,128)S(1)}, u32[]{:S(2)}, u32[]{:S(2)}) collective-permute-start(f32[4,128,128]{2,1,0:T(8,128)S(1)} %copy-done), channel_id=1, source_target_pairs={{0,1},{1,2},{2,3},{3,0},{4,5},{5,6},{6,7},{7,4},{8,9},{9,10},{10,1... | collective-permute-start | bytes 786440 | tf_op jit(solution)/shard_map/ppermute | solution.py:639
  35.2 2.6 %collective-permute-start.8 = (f32[4,128,128]{2,1,0:T(8,128)S(1)}, f32[4,128,128]{2,1,0:T(8,128)S(1)}, u32[]{:S(2)}, u32[]{:S(2)}) collective-permute-start(f32[4,128,128]{2,1,0:T(8,128)S(1)} %copy-done), channel_id=1, source_target_pairs={{0,2},{1,3},{2,0},{3,1},{4,6},{5,7},{6,4},{7,5},{8,10},{9,11},{10,... | collective-permute-start | bytes 786440 | tf_op jit(solution)/shard_map/ppermute | solution.py:639
  37.8 1.3 %collective-permute-start.9 = (f32[4,128,128]{2,1,0:T(8,128)S(1)}, f32[4,128,128]{2,1,0:T(8,128)S(1)}, u32[]{:S(2)}, u32[]{:S(2)}) collective-permute-start(f32[4,128,128]{2,1,0:T(8,128)S(1)} %copy-done), channel_id=1, source_target_pairs={{0,3},{1,0},{2,1},{3,2},{4,7},{5,4},{6,5},{7,6},{8,11},{9,8},{10,9... | collective-permute-start | bytes 786440 | tf_op jit(solution)/shard_map/ppermute | solution.py:639
  39.2 23.3 %apply_potential.1 = (f32[4,24,2,3,8,128]{5,4,3,2,1,0:T(8,128)S(1)}, f32[1,24,2,3,8,128]{5,4,3,2,1,0:T(8,128)S(1)}, f32[3,24,2,3,8,128]{5,4,3,2,1,0:T(8,128)S(1)}) custom-call(f32[1,24,2,3,8,128]{5,4,3,2,1,0:T(8,128)S(1)} %bitcast.50, f32[1,24,2,3,8,128]{5,4,3,2,1,0:T(8,128)S(1)} %bitcast.51, f32[1,24,2,3,8,128]{5,4,3,2,1,0:T(8,128)S(1)} %bitcast.52, ...), custom_call_target="tpu_custom_call" | custom-call | flops 40000000000 | tf_op jit(solution)/shard_map/apply_potential/pallas_call | solution.py:643
  62.6 2.0 %collective-permute-done.10 = f32[1,24,2,3,8,128]{5,4,3,2,1,0:T(8,128)S(1)} collective-permute-done((f32[1,24,2,3,8,128]{5,4,3,2,1,0:T(8,128)S(1)}, f32[1,24,2,3,8,128]{5,4,3,2,1,0:T(8,128)S(1)}, u32[]{:S(2)}, u32[]{:S(2)}) %collective-permute-start.10) | collective-permute-done | bytes 589856 | tf_op jit(solution)/shard_map/ppermute | solution.py:597
  64.7 4.0 %collect_points.6 = f32[1,128,256]{2,1,0:T(8,128)S(1)} custom-call(f32[1,200,256]{2,1,0:T(8,128)S(1)} %bitcast.40, f32[1,200,256]{2,1,0:T(8,128)S(1)} %bitcast.41, f32[4,1152,128]{2,1,0:T(8,128)S(1)} %bitcast.46, f32[1,1152,128]{2,1,0:T(8,128)S(1)} %bitcast.33), custom_call_target="tpu_custom_call" | custom-call | flops 8000000000 | tf_op jit(solution)/shard_map/collect_points/pallas_call | solution.py:683
  68.7 1.6 %collective-permute-start.13 = (f32[1,128,256]{2,1,0:T(8,128)S(1)}, f32[1,128,256]{2,1,0:T(8,128)S(1)}, u32[]{:S(2)}, u32[]{:S(2)}) collective-permute-start(f32[1,128,256]{2,1,0:T(8,128)S(1)} %collect_points.6), channel_id=1, source_target_pairs={{0,8},{4,12},{8,0},{12,4},{16,24},{20,28},{24,16},{28,20},{1,9},{5... | collective-permute-start | bytes 393224 | tf_op jit(solution)/shard_map/ppermute | solution.py:597
  70.2 4.0 %collect_points.4 = f32[1,128,256]{2,1,0:T(8,128)S(1)} custom-call(f32[1,200,256]{2,1,0:T(8,128)S(1)} %bitcast.44, f32[1,200,256]{2,1,0:T(8,128)S(1)} %bitcast.45, f32[4,1152,128]{2,1,0:T(8,128)S(1)} %bitcast.47, f32[3,1152,128]{2,1,0:T(8,128)S(1)} %bitcast.26), custom_call_target="tpu_custom_call" | custom-call | flops 8000000000 | tf_op jit(solution)/shard_map/collect_points/pallas_call | solution.py:683
  74.2 1.6 %collective-permute-start.12 = (f32[1,128,256]{2,1,0:T(8,128)S(1)}, f32[1,128,256]{2,1,0:T(8,128)S(1)}, u32[]{:S(2)}, u32[]{:S(2)}) collective-permute-start(f32[1,128,256]{2,1,0:T(8,128)S(1)} %collect_points.4), channel_id=1, source_target_pairs={{0,24},{4,28},{8,16},{12,20},{16,8},{20,12},{24,0},{28,4},{1,25},{... | collective-permute-start | bytes 393224 | tf_op jit(solution)/shard_map/ppermute | solution.py:597
  75.8 4.2 %collect_points.7 = f32[1,128,256]{2,1,0:T(8,128)S(1)} custom-call(f32[1,200,256]{2,1,0:T(8,128)S(1)} %bitcast.36, f32[1,200,256]{2,1,0:T(8,128)S(1)} %bitcast.37, f32[4,1152,128]{2,1,0:T(8,128)S(1)} %bitcast.48, f32[3,1152,128]{2,1,0:T(8,128)S(1)} %bitcast.27), custom_call_target="tpu_custom_call" | custom-call | flops 8000000000 | tf_op jit(solution)/shard_map/collect_points/pallas_call | solution.py:683
  80.6 4.2 %collect_points.5.refs_0_ = f32[1,128,256]{2,1,0:T(8,128)S(1)} custom-call(f32[1,200,256]{2,1,0:T(8,128)} %bitcast.2.slab_ref.steps_ref, f32[1,200,256]{2,1,0:T(8,128)} %bitcast.2.slab_ref.steps_ref, f32[4,1152,128]{2,1,0:T(8,128)S(1)} %bitcast.49, f32[3,1152,128]{2,1,0:T(8,128)S(1)} %bitcast.28), custom_call_target="tpu_custom_call" | custom-call | flops 8000000000 | tf_op jit(solution)/shard_map/collect_points/pallas_call | solution.py:683
  85.4 1.2 %collective-permute-done.15 = f32[1,8,128]{2,1,0:T(8,128)S(1)} collective-permute-done((f32[1,8,128]{2,1,0:T(8,128)S(1)}, f32[1,8,128]{2,1,0:T(8,128)S(1)}, u32[]{:S(2)}, u32[]{:S(2)}) %collective-permute-start.15) | collective-permute-done | bytes 4128 | tf_op jit(solution)/shard_map/ppermute | solution.py:597
  86.6 1.5 %collective-permute-start.16 = (f32[1,8,128]{2,1,0:T(8,128)S(1)}, f32[1,8,128]{2,1,0:T(8,128)S(1)}, u32[]{:S(2)}, u32[]{:S(2)}) collective-permute-start(f32[1,8,128]{2,1,0:T(8,128)S(1)} %add.3.refs_4_), channel_id=1, source_target_pairs={{0,8},{4,12},{8,0},{12,4},{16,24},{20,28},{24,16},{28,20},{1,9},{5... | collective-permute-start | bytes 12296 | tf_op jit(solution)/shard_map/ppermute | solution.py:597
  88.0 1.1 %collective-permute-start.17 = (f32[1,8,128]{2,1,0:T(8,128)S(1)}, f32[1,8,128]{2,1,0:T(8,128)S(1)}, u32[]{:S(2)}, u32[]{:S(2)}) collective-permute-start(f32[1,8,128]{2,1,0:T(8,128)S(1)} %add.3.refs_4_), channel_id=1, source_target_pairs={{0,16},{4,20},{8,24},{12,28},{16,0},{20,4},{24,8},{28,12},{1,17},{... | collective-permute-start | bytes 12296 | tf_op jit(solution)/shard_map/ppermute | solution.py:597
  89.1 0.9 collective-permute-start.18
  90.1 3.7 %unsort_points.1.h_ref = f32[2,128,128]{2,1,0:T(8,128)S(1)} custom-call(f32[128,256]{1,0:T(8,128)S(1)} %get-tuple-element.67.total_ref, f32[64,256]{1,0:T(8,128)S(1)} %copy-done.5), custom_call_target="tpu_custom_call" | custom-call | flops 6000000000 | tf_op jit(solution)/shard_map/unsort_points/pallas_call | solution.py:719
  93.8 0.9 residual.1
  (40 shorter events, 2.8 us)
Async XLA Ops:
  8.9 9.5 %collective-permute-start.1 = (f32[200,256]{1,0:T(8,128)}, f32[200,256]{1,0:T(8,128)S(1)}, u32[]{:S(2)}, u32[]{:S(2)}) collective-permute-start(f32[200,256]{1,0:T(8,128)} %get-tuple-element.39), channel_id=1, source_target_pairs={{0,8},{4,12},{8,0},{12,4},{16,24},{20,28},{24,16},{28,20},{1,9},{5... | collective-permute-start | bytes 614408 | tf_op jit(solution)/shard_map/ppermute | solution.py:597
  11.9 11.6 %collective-permute-start.2 = (f32[200,256]{1,0:T(8,128)}, f32[200,256]{1,0:T(8,128)S(1)}, u32[]{:S(2)}, u32[]{:S(2)}) collective-permute-start(f32[200,256]{1,0:T(8,128)} %get-tuple-element.39), channel_id=1, source_target_pairs={{0,16},{4,20},{8,24},{12,28},{16,0},{20,4},{24,8},{28,12},{1,17},{... | collective-permute-start | bytes 614408 | tf_op jit(solution)/shard_map/ppermute | solution.py:597
  18.2 9.8 %collective-permute-start = (f32[200,256]{1,0:T(8,128)}, f32[200,256]{1,0:T(8,128)S(1)}, u32[]{:S(2)}, u32[]{:S(2)}) collective-permute-start(f32[200,256]{1,0:T(8,128)} %get-tuple-element.39), channel_id=1, source_target_pairs={{0,24},{4,28},{8,16},{12,20},{16,8},{20,12},{24,0},{28,4},{1,25},{... | collective-permute-start | bytes 614408 | tf_op jit(solution)/shard_map/ppermute | solution.py:597
  18.4 14.3 %collective-permute-start.3 = (f32[1,1152,128]{2,1,0:T(8,128)S(1)}, f32[1,1152,128]{2,1,0:T(8,128)S(1)}, u32[]{:S(2)}, u32[]{:S(2)}) collective-permute-start(f32[1,1152,128]{2,1,0:T(8,128)S(1)} %get-tuple-element.44), channel_id=1, source_target_pairs={{0,4},{4,0},{8,12},{12,8},{16,20},{20,16},{24,28},{28,24},{1,5},{5... | collective-permute-start | bytes 1769480 | tf_op jit(solution)/shard_map/ppermute | solution.py:597
  22.9 9.8 %collective-permute-start.4 = (f32[1,1152,128]{2,1,0:T(8,128)S(1)}, f32[1,1152,128]{2,1,0:T(8,128)S(1)}, u32[]{:S(2)}, u32[]{:S(2)}) collective-permute-start(f32[1,1152,128]{2,1,0:T(8,128)S(1)} %get-tuple-element.45), channel_id=1, source_target_pairs={{0,4},{4,0},{8,12},{12,8},{16,20},{20,16},{24,28},{28,24},{1,5},{5... | collective-permute-start | bytes 1769480 | tf_op jit(solution)/shard_map/ppermute | solution.py:597
  28.0 4.7 %collective-permute-start.5 = (f32[1,1152,128]{2,1,0:T(8,128)S(1)}, f32[1,1152,128]{2,1,0:T(8,128)S(1)}, u32[]{:S(2)}, u32[]{:S(2)}) collective-permute-start(f32[1,1152,128]{2,1,0:T(8,128)S(1)} %get-tuple-element.46), channel_id=1, source_target_pairs={{0,4},{4,0},{8,12},{12,8},{16,20},{20,16},{24,28},{28,24},{1,5},{5... | collective-permute-start | bytes 1769480 | tf_op jit(solution)/shard_map/ppermute | solution.py:597
  28.1 11.1 %copy-start.1 = (bf16[384,1152]{1,0:T(8,128)(2,1)S(1)}, bf16[384,1152]{1,0:T(8,128)(2,1)}, u32[]{:S(2)}) copy-start(bf16[384,1152]{1,0:T(8,128)(2,1)} %constant.11.clone.refs_12_) | copy-start | bytes 2654212
  28.1 11.1 %copy-start.2 = (bf16[384,1152]{1,0:T(8,128)(2,1)S(1)}, bf16[384,1152]{1,0:T(8,128)(2,1)}, u32[]{:S(2)}) copy-start(bf16[384,1152]{1,0:T(8,128)(2,1)} %constant.8.clone.refs_9_) | copy-start | bytes 2654212
  28.1 11.1 %copy-start.3 = (bf16[1152,256]{1,0:T(8,128)(2,1)S(1)}, bf16[1152,256]{1,0:T(8,128)(2,1)}, u32[]{:S(2)}) copy-start(bf16[1152,256]{1,0:T(8,128)(2,1)} %constant.10.clone.refs_11_) | copy-start | bytes 1769476
  28.1 11.1 %copy-start.4 = (bf16[768,384]{1,0:T(8,128)(2,1)S(1)}, bf16[768,384]{1,0:T(8,128)(2,1)}, u32[]{:S(2)}) copy-start(bf16[768,384]{1,0:T(8,128)(2,1)} %constant.9.clone.refs_10_) | copy-start | bytes 1769476
  32.7 6.5 %collective-permute-start.6 = (f32[1,1152,128]{2,1,0:T(8,128)S(1)}, f32[1,1152,128]{2,1,0:T(8,128)S(1)}, u32[]{:S(2)}, u32[]{:S(2)}) collective-permute-start(f32[1,1152,128]{2,1,0:T(8,128)S(1)} %get-tuple-element.52), channel_id=1, source_target_pairs={{0,4},{4,0},{8,12},{12,8},{16,20},{20,16},{24,28},{28,24},{1,5},{5... | collective-permute-start | bytes 1769480 | tf_op jit(solution)/shard_map/ppermute | solution.py:597
  33.2 29.2 %collective-permute-start.7 = (f32[4,128,128]{2,1,0:T(8,128)S(1)}, f32[4,128,128]{2,1,0:T(8,128)S(1)}, u32[]{:S(2)}, u32[]{:S(2)}) collective-permute-start(f32[4,128,128]{2,1,0:T(8,128)S(1)} %copy-done), channel_id=1, source_target_pairs={{0,1},{1,2},{2,3},{3,0},{4,5},{5,6},{6,7},{7,4},{8,9},{9,10},{10,1... | collective-permute-start | bytes 786440 | tf_op jit(solution)/shard_map/ppermute | solution.py:639
  35.2 27.2 %collective-permute-start.8 = (f32[4,128,128]{2,1,0:T(8,128)S(1)}, f32[4,128,128]{2,1,0:T(8,128)S(1)}, u32[]{:S(2)}, u32[]{:S(2)}) collective-permute-start(f32[4,128,128]{2,1,0:T(8,128)S(1)} %copy-done), channel_id=1, source_target_pairs={{0,2},{1,3},{2,0},{3,1},{4,6},{5,7},{6,4},{7,5},{8,10},{9,11},{10,... | collective-permute-start | bytes 786440 | tf_op jit(solution)/shard_map/ppermute | solution.py:639
  37.8 24.7 %collective-permute-start.9 = (f32[4,128,128]{2,1,0:T(8,128)S(1)}, f32[4,128,128]{2,1,0:T(8,128)S(1)}, u32[]{:S(2)}, u32[]{:S(2)}) collective-permute-start(f32[4,128,128]{2,1,0:T(8,128)S(1)} %copy-done), channel_id=1, source_target_pairs={{0,3},{1,0},{2,1},{3,2},{4,7},{5,4},{6,5},{7,6},{8,11},{9,8},{10,9... | collective-permute-start | bytes 786440 | tf_op jit(solution)/shard_map/ppermute | solution.py:639
  62.5 2.1 %collective-permute-start.10 = (f32[1,24,2,3,8,128]{5,4,3,2,1,0:T(8,128)S(1)}, f32[1,24,2,3,8,128]{5,4,3,2,1,0:T(8,128)S(1)}, u32[]{:S(2)}, u32[]{:S(2)}) collective-permute-start(f32[1,24,2,3,8,128]{5,4,3,2,1,0:T(8,128)S(1)} %get-tuple-element.57), channel_id=1, source_target_pairs={{0,4},{4,0},{8,12},{12,8},{16,20},{20,16},{24,28},{28,24},{1,5},{5... | collective-permute-start | bytes 1769480 | tf_op jit(solution)/shard_map/ppermute | solution.py:597
  64.6 5.7 %collective-permute-start.11 = (f32[3,24,2,3,8,128]{5,4,3,2,1,0:T(8,128)S(1)}, f32[3,24,2,3,8,128]{5,4,3,2,1,0:T(8,128)S(1)}, u32[]{:S(2)}, u32[]{:S(2)}) collective-permute-start(f32[3,24,2,3,8,128]{5,4,3,2,1,0:T(8,128)S(1)} %get-tuple-element.59), channel_id=1, source_target_pairs={{0,4},{4,0},{8,12},{12,8},{16,20},{20,16},{24,28},{28,24},{1,5},{5... | collective-permute-start | bytes 5308424 | tf_op jit(solution)/shard_map/ppermute | solution.py:597
  68.7 16.2 %collective-permute-start.13 = (f32[1,128,256]{2,1,0:T(8,128)S(1)}, f32[1,128,256]{2,1,0:T(8,128)S(1)}, u32[]{:S(2)}, u32[]{:S(2)}) collective-permute-start(f32[1,128,256]{2,1,0:T(8,128)S(1)} %collect_points.6), channel_id=1, source_target_pairs={{0,8},{4,12},{8,0},{12,4},{16,24},{20,28},{24,16},{28,20},{1,9},{5... | collective-permute-start | bytes 393224 | tf_op jit(solution)/shard_map/ppermute | solution.py:597
  74.2 6.4 %collective-permute-start.12 = (f32[1,128,256]{2,1,0:T(8,128)S(1)}, f32[1,128,256]{2,1,0:T(8,128)S(1)}, u32[]{:S(2)}, u32[]{:S(2)}) collective-permute-start(f32[1,128,256]{2,1,0:T(8,128)S(1)} %collect_points.4), channel_id=1, source_target_pairs={{0,24},{4,28},{8,16},{12,20},{16,8},{20,12},{24,0},{28,4},{1,25},{... | collective-permute-start | bytes 393224 | tf_op jit(solution)/shard_map/ppermute | solution.py:597
  79.9 5.3 %collective-permute-start.14 = (f32[1,128,256]{2,1,0:T(8,128)S(1)}, f32[1,128,256]{2,1,0:T(8,128)S(1)}, u32[]{:S(2)}, u32[]{:S(2)}) collective-permute-start(f32[1,128,256]{2,1,0:T(8,128)S(1)} %collect_points.7), channel_id=1, source_target_pairs={{0,16},{4,20},{8,24},{12,28},{16,0},{20,4},{24,8},{28,12},{1,17},{... | collective-permute-start | bytes 393224 | tf_op jit(solution)/shard_map/ppermute | solution.py:597
  84.9 5.2 %copy-start.5 = (f32[64,256]{1,0:T(8,128)S(1)}, f32[64,256]{1,0:T(8,128)}, u32[]{:S(2)}) copy-start(f32[64,256]{1,0:T(8,128)} %get-tuple-element.68.d_ref) | copy-start | bytes 196612
  85.3 1.2 %collective-permute-start.15 = (f32[1,8,128]{2,1,0:T(8,128)S(1)}, f32[1,8,128]{2,1,0:T(8,128)S(1)}, u32[]{:S(2)}, u32[]{:S(2)}) collective-permute-start(f32[1,8,128]{2,1,0:T(8,128)S(1)} %get-tuple-element.69), channel_id=1, source_target_pairs={{0,4},{4,0},{8,12},{12,8},{16,20},{20,16},{24,28},{28,24},{1,5},{5... | collective-permute-start | bytes 12296 | tf_op jit(solution)/shard_map/ppermute | solution.py:597
  86.6 7.2 %collective-permute-start.16 = (f32[1,8,128]{2,1,0:T(8,128)S(1)}, f32[1,8,128]{2,1,0:T(8,128)S(1)}, u32[]{:S(2)}, u32[]{:S(2)}) collective-permute-start(f32[1,8,128]{2,1,0:T(8,128)S(1)} %add.3.refs_4_), channel_id=1, source_target_pairs={{0,8},{4,12},{8,0},{12,4},{16,24},{20,28},{24,16},{28,20},{1,9},{5... | collective-permute-start | bytes 12296 | tf_op jit(solution)/shard_map/ppermute | solution.py:597
  88.0 5.7 %collective-permute-start.17 = (f32[1,8,128]{2,1,0:T(8,128)S(1)}, f32[1,8,128]{2,1,0:T(8,128)S(1)}, u32[]{:S(2)}, u32[]{:S(2)}) collective-permute-start(f32[1,8,128]{2,1,0:T(8,128)S(1)} %add.3.refs_4_), channel_id=1, source_target_pairs={{0,16},{4,20},{8,24},{12,28},{16,0},{20,4},{24,8},{28,12},{1,17},{... | collective-permute-start | bytes 12296 | tf_op jit(solution)/shard_map/ppermute | solution.py:597
  89.1 4.6 %collective-permute-start.18 = (f32[1,8,128]{2,1,0:T(8,128)S(1)}, f32[1,8,128]{2,1,0:T(8,128)S(1)}, u32[]{:S(2)}, u32[]{:S(2)}) collective-permute-start(f32[1,8,128]{2,1,0:T(8,128)S(1)} %add.3.refs_4_), channel_id=1, source_target_pairs={{0,24},{4,28},{8,16},{12,20},{16,8},{20,12},{24,0},{28,4},{1,25},{... | collective-permute-start | bytes 12296 | tf_op jit(solution)/shard_map/ppermute | solution.py:597
  (1 other events, 5.1 us)

commit v9 on v8

--- a/solution.py
+++ b/solution.py
@@ -409,48 +409,67 @@
             for copy in arrivals(t):
                 copy.wait()
 
-    group = 8
+    group = 4
 
     def turn(x):
         return jnp.transpose(x, (1, 0, 2))
 
-    def abreast(x):
-        return jnp.concatenate([x[j] for j in range(group)], axis=1)
-
-    x = jnp.concatenate([abreast(turn(t_ref[:, q, step])) for q in range(2)], axis=0)
-    high, low = split(x)
-    x = mm(bf_ref[...], jnp.concatenate([high, high, low], axis=0))
-    x = jnp.concatenate(
-        [
-            jnp.concatenate([x[:N, j * LANES : (j + 1) * LANES], x[N:, j * LANES : (j + 1) * LANES]], axis=1)
-            for j in range(group)
-        ],
-        axis=0,
-    )
-    high, low = split(x)
-    x = mm(jnp.concatenate([high, high, low], axis=1), cf_ref[...])
+    planes_re, planes_im = (turn(t_ref[:, q, step]) for q in range(2))
     cells = [turn(v_ref[0, :, q]) for q in range(3)]
-    v = []
-    for j in range(group):
-        t = [cell[j] for cell in cells]
-        v.append(jnp.concatenate([t[0], t[1][:, :64]], axis=1))
-        v.append(jnp.concatenate([t[1][:, 64:], t[2]], axis=1))
-    v = jnp.concatenate(v, axis=0)
-    x = x * jnp.concatenate([v, v], axis=1)
-    high, low = split(x)
-    x = mm(jnp.concatenate([high, high, low], axis=1), ci_ref[...])
-    x = jnp.concatenate(
-        [
-            jnp.concatenate([x[j * N : (j + 1) * N, q * LANES : (q + 1) * LANES] for j in range(group)], axis=1)
-            for q in range(2)
-        ],
-        axis=0,
-    )
-    high, low = split(x)
-    x = mm(bi_ref[...], jnp.concatenate([high, high, low], axis=0))
+
+    def rows_of(first):
+        x = jnp.concatenate(
+            [
+                jnp.concatenate([source[first + j] for j in range(group)], axis=1)
+                for source in (planes_re, planes_im)
+            ],
+            axis=0,
+        )
+        high, low = split(x)
+        return jnp.concatenate([high, high, low], axis=0)
+
+    def columns_of(x):
+        x = jnp.concatenate(
+            [
+                jnp.concatenate([x[q * N : (q + 1) * N, j * LANES : (j + 1) * LANES] for q in range(2)], axis=1)
+                for j in range(group)
+            ],
+            axis=0,
+        )
+        high, low = split(x)
+        return jnp.concatenate([high, high, low], axis=1)
+
+    def weigh(first, x):
+        v = []
+        for j in range(group):
+            t = [cell[first + j] for cell in cells]
+            v.append(jnp.concatenate([t[0], t[1][:, :64]], axis=1))
+            v.append(jnp.concatenate([t[1][:, 64:], t[2]], axis=1))
+        v = jnp.concatenate(v, axis=0)
+        high, low = split(x * jnp.concatenate([v, v], axis=1))
+        return jnp.concatenate([high, high, low], axis=1)
+
+    def rows_again(x):
+        x = jnp.concatenate(
+            [
+                jnp.concatenate(
+                    [x[j * N : (j + 1) * N, q * LANES : (q + 1) * LANES] for j in range(group)], axis=1
+                )
+                for q in range(2)
+            ],
+            axis=0,
+        )
+        high, low = split(x)
+        return jnp.concatenate([high, high, low], axis=0)
+
+    chains = (0, group)
+    data = [mm(bf_ref[...], rows_of(first)) for first in chains]
+    data = [mm(columns_of(x), cf_ref[...]) for x in data]
+    data = [mm(weigh(first, x), ci_ref[...]) for first, x in zip(chains, data)]
+    data = [mm(bi_ref[...], rows_again(x)) for x in data]
     for q in range(2):
-        part = x[q * N : (q + 1) * N]
-        u_ref[:, q, step] = turn(jnp.stack([part[:, j * LANES : (j + 1) * LANES] for j in range(group)]))
+        lines = [x[q * N : (q + 1) * N, j * LANES : (j + 1) * LANES] for x in data for j in range(group)]
+        u_ref[:, q, step] = turn(jnp.stack(lines))
 
     for t in range(tiles):
 
@@ -563,7 +582,7 @@
     count = coefficients.shape[2]
     rows = count // CHUNK
     height = -(-planes // 8) * 8
-    unroll = 44
+    unroll = 88
     me = lax.axis_index("grid")
     half = slabs // 2
     anywhere = pl.BlockSpec(memory_space=pl.ANY)

time: 94.9 us -> 89.5 us (0.943)
  Pallas kernels: 70.9 us -> 64.6 us
    pallas_call x1, Pallas kernels: 23.3 us -> 18.3 us  [local(): pl.pallas_call(functools.partial(potential_kernel, planes, calls, parts),...]
    pallas_call x4, Pallas kernels: 16.3 us -> 15.4 us  [local(): pl.pallas_call(functools.partial(collect_kernel, planes, height, unroll),...]
  transfers between devices with their start and end apart: 19 -> 19, of which waited for: 4 -> 4; matrix products, arithmetic and copies ran while one was open for 0% -> 0% of each run, Pallas kernels for 65% -> 63%
where the time goes in v9:
time: 89.5 us; the launch traced here: 88.6 us
  Pallas kernels  64.6 us (72%)
  starting transfers between devices  19.2 us (21%)
  waiting for transfers between devices  3.81 us (4%)
    pallas_call x1, Pallas kernels, local(): pl.pallas_call(functools.partial(potential_kernel, planes, calls, parts),...  18.3 us
    pallas_call x4, Pallas kernels, local(): mine, theirs = spread(points[call], points[call])  18.1 us
    pallas_call x4, Pallas kernels, local(): pl.pallas_call(functools.partial(collect_kernel, planes, height, unroll),...  15.4 us
    ppermute x16, starting transfers between devices, swap(): return lax.ppermute(x, 'grid', [(i, i ^ bits) for i in range(slabs)])  13.3 us
    pallas_call x1, Pallas kernels, local(): pl.pallas_call(functools.partial(sort_kernel, planes), in_specs=[pl.Block...  8.27 us
    ppermute x3, starting transfers between devices, local(): lax.ppermute(mine, 'band', [(i, (i + shift) % bands) for i in range(bands)])  5.92 us
    ppermute x16, waiting for transfers between devices, swap(): return lax.ppermute(x, 'grid', [(i, i ^ bits) for i in range(slabs)])  3.8 us
    pallas_call x1, Pallas kernels, local(): pl.pallas_call(unsort_kernel, out_shape=jax.ShapeDtypeStruct((2, 2 * rows...  3.7 us
  transfers between devices with their start and end apart: 19, of which 4 were waited for; matrix products, arithmetic and copies ran while one was open for 0% of the time, Pallas kernels for 63%

profile of v9, /device:TPU:0, one launch (start us, length us, event | category | flops | bytes accessed | tf_op | source)
XLA Modules:
  0.0 88.6 jit_solution(17659792949498686677)
XLA Ops:
  0.6 8.3 %sort_points.1 = (f32[200,256]{1,0:T(8,128)}, f32[64,256]{1,0:T(8,128)}, f32[4,128,128]{2,1,0:T(8,128)}) custom-call(s32[128,128]{1,0:T(8,128)} %bitcast.56, f32[2,128,128]{2,1,0:T(8,128)} %bitcast.55), custom_call_target="tpu_custom_call" | custom-call | flops 10000000000 | tf_op jit(solution)/shard_map/sort_points/pallas_call | solution.py:591
  8.9 3.0 %collective-permute-start.1 = (f32[200,256]{1,0:T(8,128)}, f32[200,256]{1,0:T(8,128)S(1)}, u32[]{:S(2)}, u32[]{:S(2)}) collective-permute-start(f32[200,256]{1,0:T(8,128)} %get-tuple-element.39), channel_id=1, source_target_pairs={{0,8},{4,12},{8,0},{12,4},{16,24},{20,28},{24,16},{28,20},{1,9},{5... | collective-permute-start | bytes 614408 | tf_op jit(solution)/shard_map/ppermute | solution.py:616
  11.9 1.5 %collective-permute-start.2 = (f32[200,256]{1,0:T(8,128)}, f32[200,256]{1,0:T(8,128)S(1)}, u32[]{:S(2)}, u32[]{:S(2)}) collective-permute-start(f32[200,256]{1,0:T(8,128)} %get-tuple-element.39), channel_id=1, source_target_pairs={{0,16},{4,20},{8,24},{12,28},{16,0},{20,4},{24,8},{28,12},{1,17},{... | collective-permute-start | bytes 614408 | tf_op jit(solution)/shard_map/ppermute | solution.py:616
  13.4 4.7 %spread_points.4 = (f32[1,1152,128]{2,1,0:T(8,128)S(1)}, f32[1,1152,128]{2,1,0:T(8,128)S(1)}) custom-call(f32[1,200,256]{2,1,0:T(8,128)} %bitcast.2.slab_ref.steps_ref, f32[1,200,256]{2,1,0:T(8,128)} %bitcast.2.slab_ref.steps_ref), custom_call_target="tpu_custom_call" | custom-call | flops 8000000000 | tf_op jit(solution)/shard_map/spread_points/pallas_call | solution.py:643
  18.3 4.4 %spread_points.5 = (f32[1,1152,128]{2,1,0:T(8,128)S(1)}, f32[1,1152,128]{2,1,0:T(8,128)S(1)}) custom-call(f32[1,200,256]{2,1,0:T(8,128)S(1)} %bitcast.38, f32[1,200,256]{2,1,0:T(8,128)S(1)} %bitcast.39), custom_call_target="tpu_custom_call" | custom-call | flops 8000000000 | tf_op jit(solution)/shard_map/spread_points/pallas_call | solution.py:643
  23.2 4.4 %spread_points.6 = (f32[1,1152,128]{2,1,0:T(8,128)S(1)}, f32[1,1152,128]{2,1,0:T(8,128)S(1)}) custom-call(f32[1,200,256]{2,1,0:T(8,128)S(1)} %bitcast.34, f32[1,200,256]{2,1,0:T(8,128)S(1)} %bitcast.35), custom_call_target="tpu_custom_call" | custom-call | flops 8000000000 | tf_op jit(solution)/shard_map/spread_points/pallas_call | solution.py:643
  27.8 4.6 %spread_points.7 = (f32[1,1152,128]{2,1,0:T(8,128)S(1)}, f32[1,1152,128]{2,1,0:T(8,128)S(1)}) custom-call(f32[1,200,256]{2,1,0:T(8,128)S(1)} %bitcast.42, f32[1,200,256]{2,1,0:T(8,128)S(1)} %bitcast.43), custom_call_target="tpu_custom_call" | custom-call | flops 8000000000 | tf_op jit(solution)/shard_map/spread_points/pallas_call | solution.py:643
  33.0 2.0 %collective-permute-start.7 = (f32[4,128,128]{2,1,0:T(8,128)S(1)}, f32[4,128,128]{2,1,0:T(8,128)S(1)}, u32[]{:S(2)}, u32[]{:S(2)}) collective-permute-start(f32[4,128,128]{2,1,0:T(8,128)S(1)} %copy-done), channel_id=1, source_target_pairs={{0,1},{1,2},{2,3},{3,0},{4,5},{5,6},{6,7},{7,4},{8,9},{9,10},{10,1... | collective-permute-start | bytes 786440 | tf_op jit(solution)/shard_map/ppermute | solution.py:658
  34.9 2.6 %collective-permute-start.8 = (f32[4,128,128]{2,1,0:T(8,128)S(1)}, f32[4,128,128]{2,1,0:T(8,128)S(1)}, u32[]{:S(2)}, u32[]{:S(2)}) collective-permute-start(f32[4,128,128]{2,1,0:T(8,128)S(1)} %copy-done), channel_id=1, source_target_pairs={{0,2},{1,3},{2,0},{3,1},{4,6},{5,7},{6,4},{7,5},{8,10},{9,11},{10,... | collective-permute-start | bytes 786440 | tf_op jit(solution)/shard_map/ppermute | solution.py:658
  37.5 1.3 %collective-permute-start.9 = (f32[4,128,128]{2,1,0:T(8,128)S(1)}, f32[4,128,128]{2,1,0:T(8,128)S(1)}, u32[]{:S(2)}, u32[]{:S(2)}) collective-permute-start(f32[4,128,128]{2,1,0:T(8,128)S(1)} %copy-done), channel_id=1, source_target_pairs={{0,3},{1,0},{2,1},{3,2},{4,7},{5,4},{6,5},{7,6},{8,11},{9,8},{10,9... | collective-permute-start | bytes 786440 | tf_op jit(solution)/shard_map/ppermute | solution.py:658
  38.9 18.3 %apply_potential.1 = (f32[4,24,2,3,8,128]{5,4,3,2,1,0:T(8,128)S(1)}, f32[1,24,2,3,8,128]{5,4,3,2,1,0:T(8,128)S(1)}, f32[3,24,2,3,8,128]{5,4,3,2,1,0:T(8,128)S(1)}) custom-call(f32[1,24,2,3,8,128]{5,4,3,2,1,0:T(8,128)S(1)} %bitcast.50, f32[1,24,2,3,8,128]{5,4,3,2,1,0:T(8,128)S(1)} %bitcast.51, f32[1,24,2,3,8,128]{5,4,3,2,1,0:T(8,128)S(1)} %bitcast.52, ...), custom_call_target="tpu_custom_call" | custom-call | flops 40000000000 | tf_op jit(solution)/shard_map/apply_potential/pallas_call | solution.py:662
  57.3 2.0 %collective-permute-done.10 = f32[1,24,2,3,8,128]{5,4,3,2,1,0:T(8,128)S(1)} collective-permute-done((f32[1,24,2,3,8,128]{5,4,3,2,1,0:T(8,128)S(1)}, f32[1,24,2,3,8,128]{5,4,3,2,1,0:T(8,128)S(1)}, u32[]{:S(2)}, u32[]{:S(2)}) %collective-permute-start.10) | collective-permute-done | bytes 589856 | tf_op jit(solution)/shard_map/ppermute | solution.py:616
  59.4 3.8 %collect_points.6 = f32[1,128,256]{2,1,0:T(8,128)S(1)} custom-call(f32[1,200,256]{2,1,0:T(8,128)S(1)} %bitcast.40, f32[1,200,256]{2,1,0:T(8,128)S(1)} %bitcast.41, f32[4,1152,128]{2,1,0:T(8,128)S(1)} %bitcast.46, f32[1,1152,128]{2,1,0:T(8,128)S(1)} %bitcast.33), custom_call_target="tpu_custom_call" | custom-call | flops 8000000000 | tf_op jit(solution)/shard_map/collect_points/pallas_call | solution.py:702
  63.2 1.6 %collective-permute-start.13 = (f32[1,128,256]{2,1,0:T(8,128)S(1)}, f32[1,128,256]{2,1,0:T(8,128)S(1)}, u32[]{:S(2)}, u32[]{:S(2)}) collective-permute-start(f32[1,128,256]{2,1,0:T(8,128)S(1)} %collect_points.6), channel_id=1, source_target_pairs={{0,8},{4,12},{8,0},{12,4},{16,24},{20,28},{24,16},{28,20},{1,9},{5... | collective-permute-start | bytes 393224 | tf_op jit(solution)/shard_map/ppermute | solution.py:616
  64.8 3.8 %collect_points.4 = f32[1,128,256]{2,1,0:T(8,128)S(1)} custom-call(f32[1,200,256]{2,1,0:T(8,128)S(1)} %bitcast.44, f32[1,200,256]{2,1,0:T(8,128)S(1)} %bitcast.45, f32[4,1152,128]{2,1,0:T(8,128)S(1)} %bitcast.47, f32[3,1152,128]{2,1,0:T(8,128)S(1)} %bitcast.26), custom_call_target="tpu_custom_call" | custom-call | flops 8000000000 | tf_op jit(solution)/shard_map/collect_points/pallas_call | solution.py:702
  68.6 1.5 %collective-permute-start.12 = (f32[1,128,256]{2,1,0:T(8,128)S(1)}, f32[1,128,256]{2,1,0:T(8,128)S(1)}, u32[]{:S(2)}, u32[]{:S(2)}) collective-permute-start(f32[1,128,256]{2,1,0:T(8,128)S(1)} %collect_points.4), channel_id=1, source_target_pairs={{0,24},{4,28},{8,16},{12,20},{16,8},{20,12},{24,0},{28,4},{1,25},{... | collective-permute-start | bytes 393224 | tf_op jit(solution)/shard_map/ppermute | solution.py:616
  70.1 3.8 %collect_points.7 = f32[1,128,256]{2,1,0:T(8,128)S(1)} custom-call(f32[1,200,256]{2,1,0:T(8,128)S(1)} %bitcast.36, f32[1,200,256]{2,1,0:T(8,128)S(1)} %bitcast.37, f32[4,1152,128]{2,1,0:T(8,128)S(1)} %bitcast.48, f32[3,1152,128]{2,1,0:T(8,128)S(1)} %bitcast.27), custom_call_target="tpu_custom_call" | custom-call | flops 8000000000 | tf_op jit(solution)/shard_map/collect_points/pallas_call | solution.py:702
  75.0 4.0 %collect_points.5.refs_0_ = f32[1,128,256]{2,1,0:T(8,128)S(1)} custom-call(f32[1,200,256]{2,1,0:T(8,128)} %bitcast.2.slab_ref.steps_ref, f32[1,200,256]{2,1,0:T(8,128)} %bitcast.2.slab_ref.steps_ref, f32[4,1152,128]{2,1,0:T(8,128)S(1)} %bitcast.49, f32[3,1152,128]{2,1,0:T(8,128)S(1)} %bitcast.28), custom_call_target="tpu_custom_call" | custom-call | flops 8000000000 | tf_op jit(solution)/shard_map/collect_points/pallas_call | solution.py:702
  79.4 1.2 %collective-permute-done.15 = f32[1,8,128]{2,1,0:T(8,128)S(1)} collective-permute-done((f32[1,8,128]{2,1,0:T(8,128)S(1)}, f32[1,8,128]{2,1,0:T(8,128)S(1)}, u32[]{:S(2)}, u32[]{:S(2)}) %collective-permute-start.15) | collective-permute-done | bytes 4128 | tf_op jit(solution)/shard_map/ppermute | solution.py:616
  80.5 1.5 %collective-permute-start.16 = (f32[1,8,128]{2,1,0:T(8,128)S(1)}, f32[1,8,128]{2,1,0:T(8,128)S(1)}, u32[]{:S(2)}, u32[]{:S(2)}) collective-permute-start(f32[1,8,128]{2,1,0:T(8,128)S(1)} %add.3.refs_4_), channel_id=1, source_target_pairs={{0,8},{4,12},{8,0},{12,4},{16,24},{20,28},{24,16},{28,20},{1,9},{5... | collective-permute-start | bytes 12296 | tf_op jit(solution)/shard_map/ppermute | solution.py:616
  82.0 0.9 %collective-permute-start.17 = (f32[1,8,128]{2,1,0:T(8,128)S(1)}, f32[1,8,128]{2,1,0:T(8,128)S(1)}, u32[]{:S(2)}, u32[]{:S(2)}) collective-permute-start(f32[1,8,128]{2,1,0:T(8,128)S(1)} %add.3.refs_4_), channel_id=1, source_target_pairs={{0,16},{4,20},{8,24},{12,28},{16,0},{20,4},{24,8},{28,12},{1,17},{... | collective-permute-start | bytes 12296 | tf_op jit(solution)/shard_map/ppermute | solution.py:616
  82.9 1.1 %collective-permute-start.18 = (f32[1,8,128]{2,1,0:T(8,128)S(1)}, f32[1,8,128]{2,1,0:T(8,128)S(1)}, u32[]{:S(2)}, u32[]{:S(2)}) collective-permute-start(f32[1,8,128]{2,1,0:T(8,128)S(1)} %add.3.refs_4_), channel_id=1, source_target_pairs={{0,24},{4,28},{8,16},{12,20},{16,8},{20,12},{24,0},{28,4},{1,25},{... | collective-permute-start | bytes 12296 | tf_op jit(solution)/shard_map/ppermute | solution.py:616
  84.0 3.7 %unsort_points.1.h_ref = f32[2,128,128]{2,1,0:T(8,128)S(1)} custom-call(f32[128,256]{1,0:T(8,128)S(1)} %get-tuple-element.67.total_ref, f32[64,256]{1,0:T(8,128)S(1)} %copy-done.5), custom_call_target="tpu_custom_call" | custom-call | flops 6000000000 | tf_op jit(solution)/shard_map/unsort_points/pallas_call | solution.py:738
  87.7 0.9 residual.1
  (40 shorter events, 3.0 us)
Async XLA Ops:
  8.9 9.4 %collective-permute-start.1 = (f32[200,256]{1,0:T(8,128)}, f32[200,256]{1,0:T(8,128)S(1)}, u32[]{:S(2)}, u32[]{:S(2)}) collective-permute-start(f32[200,256]{1,0:T(8,128)} %get-tuple-element.39), channel_id=1, source_target_pairs={{0,8},{4,12},{8,0},{12,4},{16,24},{20,28},{24,16},{28,20},{1,9},{5... | collective-permute-start | bytes 614408 | tf_op jit(solution)/shard_map/ppermute | solution.py:616
  11.9 11.3 %collective-permute-start.2 = (f32[200,256]{1,0:T(8,128)}, f32[200,256]{1,0:T(8,128)S(1)}, u32[]{:S(2)}, u32[]{:S(2)}) collective-permute-start(f32[200,256]{1,0:T(8,128)} %get-tuple-element.39), channel_id=1, source_target_pairs={{0,16},{4,20},{8,24},{12,28},{16,0},{20,4},{24,8},{28,12},{1,17},{... | collective-permute-start | bytes 614408 | tf_op jit(solution)/shard_map/ppermute | solution.py:616
  18.1 9.6 %collective-permute-start = (f32[200,256]{1,0:T(8,128)}, f32[200,256]{1,0:T(8,128)S(1)}, u32[]{:S(2)}, u32[]{:S(2)}) collective-permute-start(f32[200,256]{1,0:T(8,128)} %get-tuple-element.39), channel_id=1, source_target_pairs={{0,24},{4,28},{8,16},{12,20},{16,8},{20,12},{24,0},{28,4},{1,25},{... | collective-permute-start | bytes 614408 | tf_op jit(solution)/shard_map/ppermute | solution.py:616
  18.2 14.1 %collective-permute-start.3 = (f32[1,1152,128]{2,1,0:T(8,128)S(1)}, f32[1,1152,128]{2,1,0:T(8,128)S(1)}, u32[]{:S(2)}, u32[]{:S(2)}) collective-permute-start(f32[1,1152,128]{2,1,0:T(8,128)S(1)} %get-tuple-element.44), channel_id=1, source_target_pairs={{0,4},{4,0},{8,12},{12,8},{16,20},{20,16},{24,28},{28,24},{1,5},{5... | collective-permute-start | bytes 1769480 | tf_op jit(solution)/shard_map/ppermute | solution.py:616
  22.7 9.7 %collective-permute-start.4 = (f32[1,1152,128]{2,1,0:T(8,128)S(1)}, f32[1,1152,128]{2,1,0:T(8,128)S(1)}, u32[]{:S(2)}, u32[]{:S(2)}) collective-permute-start(f32[1,1152,128]{2,1,0:T(8,128)S(1)} %get-tuple-element.45), channel_id=1, source_target_pairs={{0,4},{4,0},{8,12},{12,8},{16,20},{20,16},{24,28},{28,24},{1,5},{5... | collective-permute-start | bytes 1769480 | tf_op jit(solution)/shard_map/ppermute | solution.py:616
  27.6 4.8 %collective-permute-start.5 = (f32[1,1152,128]{2,1,0:T(8,128)S(1)}, f32[1,1152,128]{2,1,0:T(8,128)S(1)}, u32[]{:S(2)}, u32[]{:S(2)}) collective-permute-start(f32[1,1152,128]{2,1,0:T(8,128)S(1)} %get-tuple-element.46), channel_id=1, source_target_pairs={{0,4},{4,0},{8,12},{12,8},{16,20},{20,16},{24,28},{28,24},{1,5},{5... | collective-permute-start | bytes 1769480 | tf_op jit(solution)/shard_map/ppermute | solution.py:616
  27.7 5.2 %copy-start = (f32[4,128,128]{2,1,0:T(8,128)S(1)}, f32[4,128,128]{2,1,0:T(8,128)}, u32[]{:S(2)}) copy-start(f32[4,128,128]{2,1,0:T(8,128)} %get-tuple-element.63.refs_4_.refs_0_) | copy-start | bytes 786436
  27.7 11.1 %copy-start.1 = (bf16[384,1152]{1,0:T(8,128)(2,1)S(1)}, bf16[384,1152]{1,0:T(8,128)(2,1)}, u32[]{:S(2)}) copy-start(bf16[384,1152]{1,0:T(8,128)(2,1)} %constant.11.clone.refs_12_) | copy-start | bytes 2654212
  27.8 11.1 %copy-start.2 = (bf16[384,1152]{1,0:T(8,128)(2,1)S(1)}, bf16[384,1152]{1,0:T(8,128)(2,1)}, u32[]{:S(2)}) copy-start(bf16[384,1152]{1,0:T(8,128)(2,1)} %constant.8.clone.refs_9_) | copy-start | bytes 2654212
  27.8 11.1 %copy-start.3 = (bf16[1152,256]{1,0:T(8,128)(2,1)S(1)}, bf16[1152,256]{1,0:T(8,128)(2,1)}, u32[]{:S(2)}) copy-start(bf16[1152,256]{1,0:T(8,128)(2,1)} %constant.10.clone.refs_11_) | copy-start | bytes 1769476
  27.8 11.1 %copy-start.4 = (bf16[768,384]{1,0:T(8,128)(2,1)S(1)}, bf16[768,384]{1,0:T(8,128)(2,1)}, u32[]{:S(2)}) copy-start(bf16[768,384]{1,0:T(8,128)(2,1)} %constant.9.clone.refs_10_) | copy-start | bytes 1769476
  32.4 6.5 %collective-permute-start.6 = (f32[1,1152,128]{2,1,0:T(8,128)S(1)}, f32[1,1152,128]{2,1,0:T(8,128)S(1)}, u32[]{:S(2)}, u32[]{:S(2)}) collective-permute-start(f32[1,1152,128]{2,1,0:T(8,128)S(1)} %get-tuple-element.52), channel_id=1, source_target_pairs={{0,4},{4,0},{8,12},{12,8},{16,20},{20,16},{24,28},{28,24},{1,5},{5... | collective-permute-start | bytes 1769480 | tf_op jit(solution)/shard_map/ppermute | solution.py:616
  33.0 24.2 %collective-permute-start.7 = (f32[4,128,128]{2,1,0:T(8,128)S(1)}, f32[4,128,128]{2,1,0:T(8,128)S(1)}, u32[]{:S(2)}, u32[]{:S(2)}) collective-permute-start(f32[4,128,128]{2,1,0:T(8,128)S(1)} %copy-done), channel_id=1, source_target_pairs={{0,1},{1,2},{2,3},{3,0},{4,5},{5,6},{6,7},{7,4},{8,9},{9,10},{10,1... | collective-permute-start | bytes 786440 | tf_op jit(solution)/shard_map/ppermute | solution.py:658
  34.9 22.3 %collective-permute-start.8 = (f32[4,128,128]{2,1,0:T(8,128)S(1)}, f32[4,128,128]{2,1,0:T(8,128)S(1)}, u32[]{:S(2)}, u32[]{:S(2)}) collective-permute-start(f32[4,128,128]{2,1,0:T(8,128)S(1)} %copy-done), channel_id=1, source_target_pairs={{0,2},{1,3},{2,0},{3,1},{4,6},{5,7},{6,4},{7,5},{8,10},{9,11},{10,... | collective-permute-start | bytes 786440 | tf_op jit(solution)/shard_map/ppermute | solution.py:658
  37.5 19.7 %collective-permute-start.9 = (f32[4,128,128]{2,1,0:T(8,128)S(1)}, f32[4,128,128]{2,1,0:T(8,128)S(1)}, u32[]{:S(2)}, u32[]{:S(2)}) collective-permute-start(f32[4,128,128]{2,1,0:T(8,128)S(1)} %copy-done), channel_id=1, source_target_pairs={{0,3},{1,0},{2,1},{3,2},{4,7},{5,4},{6,5},{7,6},{8,11},{9,8},{10,9... | collective-permute-start | bytes 786440 | tf_op jit(solution)/shard_map/ppermute | solution.py:658
  57.2 2.1 %collective-permute-start.10 = (f32[1,24,2,3,8,128]{5,4,3,2,1,0:T(8,128)S(1)}, f32[1,24,2,3,8,128]{5,4,3,2,1,0:T(8,128)S(1)}, u32[]{:S(2)}, u32[]{:S(2)}) collective-permute-start(f32[1,24,2,3,8,128]{5,4,3,2,1,0:T(8,128)S(1)} %get-tuple-element.57), channel_id=1, source_target_pairs={{0,4},{4,0},{8,12},{12,8},{16,20},{20,16},{24,28},{28,24},{1,5},{5... | collective-permute-start | bytes 1769480 | tf_op jit(solution)/shard_map/ppermute | solution.py:616
  59.3 5.5 %collective-permute-start.11 = (f32[3,24,2,3,8,128]{5,4,3,2,1,0:T(8,128)S(1)}, f32[3,24,2,3,8,128]{5,4,3,2,1,0:T(8,128)S(1)}, u32[]{:S(2)}, u32[]{:S(2)}) collective-permute-start(f32[3,24,2,3,8,128]{5,4,3,2,1,0:T(8,128)S(1)} %get-tuple-element.59), channel_id=1, source_target_pairs={{0,4},{4,0},{8,12},{12,8},{16,20},{20,16},{24,28},{28,24},{1,5},{5... | collective-permute-start | bytes 5308424 | tf_op jit(solution)/shard_map/ppermute | solution.py:616
  63.2 15.9 %collective-permute-start.13 = (f32[1,128,256]{2,1,0:T(8,128)S(1)}, f32[1,128,256]{2,1,0:T(8,128)S(1)}, u32[]{:S(2)}, u32[]{:S(2)}) collective-permute-start(f32[1,128,256]{2,1,0:T(8,128)S(1)} %collect_points.6), channel_id=1, source_target_pairs={{0,8},{4,12},{8,0},{12,4},{16,24},{20,28},{24,16},{28,20},{1,9},{5... | collective-permute-start | bytes 393224 | tf_op jit(solution)/shard_map/ppermute | solution.py:616
  68.6 6.5 %collective-permute-start.12 = (f32[1,128,256]{2,1,0:T(8,128)S(1)}, f32[1,128,256]{2,1,0:T(8,128)S(1)}, u32[]{:S(2)}, u32[]{:S(2)}) collective-permute-start(f32[1,128,256]{2,1,0:T(8,128)S(1)} %collect_points.4), channel_id=1, source_target_pairs={{0,24},{4,28},{8,16},{12,20},{16,8},{20,12},{24,0},{28,4},{1,25},{... | collective-permute-start | bytes 393224 | tf_op jit(solution)/shard_map/ppermute | solution.py:616
  73.9 5.3 %collective-permute-start.14 = (f32[1,128,256]{2,1,0:T(8,128)S(1)}, f32[1,128,256]{2,1,0:T(8,128)S(1)}, u32[]{:S(2)}, u32[]{:S(2)}) collective-permute-start(f32[1,128,256]{2,1,0:T(8,128)S(1)} %collect_points.7), channel_id=1, source_target_pairs={{0,16},{4,20},{8,24},{12,28},{16,0},{20,4},{24,8},{28,12},{1,17},{... | collective-permute-start | bytes 393224 | tf_op jit(solution)/shard_map/ppermute | solution.py:616
  79.3 1.2 %collective-permute-start.15 = (f32[1,8,128]{2,1,0:T(8,128)S(1)}, f32[1,8,128]{2,1,0:T(8,128)S(1)}, u32[]{:S(2)}, u32[]{:S(2)}) collective-permute-start(f32[1,8,128]{2,1,0:T(8,128)S(1)} %get-tuple-element.69), channel_id=1, source_target_pairs={{0,4},{4,0},{8,12},{12,8},{16,20},{20,16},{24,28},{28,24},{1,5},{5... | collective-permute-start | bytes 12296 | tf_op jit(solution)/shard_map/ppermute | solution.py:616
  80.5 7.2 %collective-permute-start.16 = (f32[1,8,128]{2,1,0:T(8,128)S(1)}, f32[1,8,128]{2,1,0:T(8,128)S(1)}, u32[]{:S(2)}, u32[]{:S(2)}) collective-permute-start(f32[1,8,128]{2,1,0:T(8,128)S(1)} %add.3.refs_4_), channel_id=1, source_target_pairs={{0,8},{4,12},{8,0},{12,4},{16,24},{20,28},{24,16},{28,20},{1,9},{5... | collective-permute-start | bytes 12296 | tf_op jit(solution)/shard_map/ppermute | solution.py:616
  82.0 5.7 %collective-permute-start.17 = (f32[1,8,128]{2,1,0:T(8,128)S(1)}, f32[1,8,128]{2,1,0:T(8,128)S(1)}, u32[]{:S(2)}, u32[]{:S(2)}) collective-permute-start(f32[1,8,128]{2,1,0:T(8,128)S(1)} %add.3.refs_4_), channel_id=1, source_target_pairs={{0,16},{4,20},{8,24},{12,28},{16,0},{20,4},{24,8},{28,12},{1,17},{... | collective-permute-start | bytes 12296 | tf_op jit(solution)/shard_map/ppermute | solution.py:616
  82.9 4.8 %collective-permute-start.18 = (f32[1,8,128]{2,1,0:T(8,128)S(1)}, f32[1,8,128]{2,1,0:T(8,128)S(1)}, u32[]{:S(2)}, u32[]{:S(2)}) collective-permute-start(f32[1,8,128]{2,1,0:T(8,128)S(1)} %add.3.refs_4_), channel_id=1, source_target_pairs={{0,24},{4,28},{8,16},{12,20},{16,8},{20,12},{24,0},{28,4},{1,25},{... | collective-permute-start | bytes 12296 | tf_op jit(solution)/shard_map/ppermute | solution.py:616
  (1 other events, 4.9 us)
